TPU v7x, 32 devices: a whole 2x2x4 slice. The times are simulated.
32 devices in a mesh: dp: 16 (over z, y, core), tensor: 2 (over x).
Axes of the slice: x: 2, y: 2, z: 4, core: 2. Of those that a mesh axis runs over, the one named last changes fastest.
Arguments:
- tokens: bfloat16 [8192, 2048], P(('dp', 'tensor')), may hold values from -6 to 6
- lengths: int32 [16], P('dp'), may hold values from 1 to 512, 6144 in all
- cotangent: bfloat16 [8192, 2048], P(('dp', 'tensor')), may hold values from -6 to 6
- gain_in: float32 [2048], P(('dp', 'tensor')), may hold values from 0.5 to 1.5
- gain_ffn: float32 [2048], P(('dp', 'tensor')), may hold values from 0.5 to 1.5
- gain_out: float32 [512], P(('dp', 'tensor')), may hold values from 0.5 to 1.5
- w_query: float32 [2048, 1536], P('dp', 'tensor'), may hold values from -0.125 to 0.125
- w_key: float32 [2048, 1536], P('dp', 'tensor'), may hold values from -0.125 to 0.125
- w_value: float32 [2048, 3072], P('dp', 'tensor'), may hold values from -0.125 to 0.125
- w_gate: float32 [2048, 3072], P('dp', 'tensor'), may hold values from -0.125 to 0.125
- w_beta: float32 [2048, 6], P('dp', 'tensor'), may hold values from -0.125 to 0.125
- w_decay: float32 [2048, 6], P('dp', 'tensor'), may hold values from -0.125 to 0.125
- conv_query: float32 [4, 6, 256], P(None, 'tensor', 'dp'), may hold values from -3 to 3
- conv_key: float32 [4, 6, 256], P(None, 'tensor', 'dp'), may hold values from -3 to 3
- conv_value: float32 [4, 6, 512], P(None, 'tensor', 'dp'), may hold values from -3 to 3
- decay_log: float32 [6], replicated, may hold values from 0 to 2.7726
- decay_bias: float32 [6], replicated, may hold values from -6.91 to -2.25
- w_output: float32 [3072, 2048], P('tensor', 'dp'), may hold values from -0.109375 to 0.109375
- w_ffn_gate: float32 [2048, 5632], P('dp', 'tensor'), may hold values from -0.125 to 0.125
- w_ffn_up: float32 [2048, 5632], P('dp', 'tensor'), may hold values from -0.125 to 0.125
- w_ffn_down: float32 [5632, 2048], P('tensor', 'dp'), may hold values from -0.078125 to 0.078125
Outputs:
- out_tokens: bfloat16 [8192, 2048], P(('dp', 'tensor'))
- grad_tokens: float32 [8192, 2048], P(('dp', 'tensor'))
- grad_gain_in: float32 [2048], P(('dp', 'tensor'))
- grad_gain_ffn: float32 [2048], P(('dp', 'tensor'))
- grad_gain_out: float32 [512], P(('dp', 'tensor'))
- grad_w_query: float32 [2048, 1536], P('dp', 'tensor')
- grad_w_key: float32 [2048, 1536], P('dp', 'tensor')
- grad_w_value: float32 [2048, 3072], P('dp', 'tensor')
- grad_w_gate: float32 [2048, 3072], P('dp', 'tensor')
- grad_w_beta: float32 [2048, 6], P('dp', 'tensor')
- grad_w_decay: float32 [2048, 6], P('dp', 'tensor')
- grad_conv_query: float32 [4, 6, 256], P(None, 'tensor', 'dp')
- grad_conv_key: float32 [4, 6, 256], P(None, 'tensor', 'dp')
- grad_conv_value: float32 [4, 6, 512], P(None, 'tensor', 'dp')
- grad_decay_log: float32 [6], replicated
- grad_decay_bias: float32 [6], replicated
- grad_w_output: float32 [3072, 2048], P('tensor', 'dp')
- grad_w_ffn_gate: float32 [2048, 5632], P('dp', 'tensor')
- grad_w_ffn_up: float32 [2048, 5632], P('dp', 'tensor')
- grad_w_ffn_down: float32 [5632, 2048], P('tensor', 'dp')
Inputs may be any that keep to these rules, and one draw needn't show every extreme that they name: The lengths of all slots sum to three quarters of 8192; the longest fills its slot of 512.
All inputs are finite; a program needn't handle non-finite values. No bound on the sum of `lengths` on one device may be relied on, other than what follows from the above.
Results may differ from a plain program's by a relative error of at most 0.023.
Values may be sent and summed in bfloat16 or wider, within the bound.
A program may use at most 320 MiB of HBM per device.

v0:
```python
import jax
import jax.numpy as jnp
from jax import lax
from jax.sharding import PartitionSpec as P

SPAN = 64


highest = lax.Precision.HIGHEST


def rms_scale(values):
    return lax.rsqrt(jnp.mean(values * values, axis=-1, keepdims=True) + 1e-05)


def unit_norm(values):
    return values * lax.rsqrt(jnp.sum(values * values, axis=-1, keepdims=True) + 1e-06)


def causal_conv(values, weights):
    length = values.shape[-2]
    tap_count = weights.shape[0]
    summed = jnp.zeros_like(values)
    for tap_index in range(tap_count):
        offset = tap_count - 1 - tap_index
        padding = [(0, 0)] * (values.ndim - 2) + [(offset, 0), (0, 0)]
        summed = summed + weights[tap_index] * jnp.pad(values, padding)[..., :length, :]
    return summed


def span_core(query_vecs, key_vecs, value_vecs, beta_vals, log_decays):
    length, head_count, key_size = query_vecs.shape
    value_size = value_vecs.shape[-1]
    blocks = length // SPAN

    def split_rows(tensor_in):
        shaped = tensor_in.reshape((blocks, SPAN) + tensor_in.shape[1:])
        return jnp.moveaxis(shaped, 2, 1)

    query_blocks = split_rows(query_vecs)
    key_blocks = split_rows(key_vecs)
    value_blocks = split_rows(value_vecs)
    beta_blocks = split_rows(beta_vals)
    decay_blocks = split_rows(log_decays)
    cumulative = jnp.cumsum(decay_blocks, axis=-1)
    row_index = jnp.arange(SPAN)
    strict = row_index[:, None] > row_index[None, :]
    inclusive = row_index[:, None] >= row_index[None, :]
    gaps = cumulative[..., :, None] - cumulative[..., None, :]
    strict_decay = jnp.where(strict, jnp.exp(jnp.where(strict, gaps, 0.0)), 0.0)
    inclusive_decay = jnp.where(inclusive, jnp.exp(jnp.where(inclusive, gaps, 0.0)), 0.0)
    key_gram = jnp.einsum("nhca,nhsa->nhcs", key_blocks, key_blocks, precision=highest)
    lower_matrix = (
        jnp.eye(SPAN, dtype=jnp.float32) + beta_blocks[..., None] * strict_decay * key_gram
    )
    value_part = lax.linalg.triangular_solve(
        lower_matrix,
        beta_blocks[..., None] * value_blocks,
        left_side=True,
        lower=True,
        unit_diagonal=True,
    )
    key_part = lax.linalg.triangular_solve(
        lower_matrix,
        (beta_blocks * jnp.exp(cumulative))[..., None] * key_blocks,
        left_side=True,
        lower=True,
        unit_diagonal=True,
    )
    score_blocks = (
        jnp.einsum("nhca,nhsa->nhcs", query_blocks, key_blocks, precision=highest) * inclusive_decay
    )
    last_decay = cumulative[..., -1]
    key_end = key_blocks * jnp.exp(last_decay[..., None] - cumulative)[..., None]
    start_decay = jnp.exp(cumulative)

    def block_step(carried, block_inputs):
        value_block, key_block, query_block, score_block, end_block, start_block, last_block = (
            block_inputs
        )
        update = value_block - jnp.einsum("hca,hav->hcv", key_block, carried, precision=highest)
        output = start_block[..., None] * jnp.einsum(
            "hca,hav->hcv", query_block, carried, precision=highest
        )
        output = output + jnp.einsum("hcs,hsv->hcv", score_block, update, precision=highest)
        carried = jnp.exp(last_block)[:, None, None] * carried + jnp.einsum(
            "hca,hcv->hav", end_block, update, precision=highest
        )
        return (carried, output)

    initial = jnp.zeros((head_count, key_size, value_size), jnp.float32)
    _, outputs = lax.scan(
        block_step,
        initial,
        (value_part, key_part, query_blocks, score_blocks, key_end, start_decay, last_decay),
    )
    return jnp.moveaxis(outputs, 1, 2).reshape(length, head_count, value_size)


def mixer_local(
    query_pre,
    key_pre,
    value_pre,
    gate_pre,
    beta_pre,
    decay_pre,
    conv_q,
    conv_k,
    conv_v,
    decay_log,
    decay_bias,
    gain_out,
    live_mask,
):
    length = query_pre.shape[0]
    head_count = decay_log.shape[0]
    key_size = conv_q.shape[2]
    value_size = conv_v.shape[2]
    query_vecs = unit_norm(
        jax.nn.silu(causal_conv(query_pre, conv_q.reshape(conv_q.shape[0], -1))).reshape(
            length, head_count, key_size
        )
    ) * key_size ** (-0.5)
    key_vecs = unit_norm(
        jax.nn.silu(causal_conv(key_pre, conv_k.reshape(conv_k.shape[0], -1))).reshape(
            length, head_count, key_size
        )
    )
    value_vecs = jax.nn.silu(causal_conv(value_pre, conv_v.reshape(conv_v.shape[0], -1))).reshape(
        length, head_count, value_size
    )
    beta_vals = jax.nn.sigmoid(beta_pre) * live_mask[:, None]
    log_decays = -jnp.exp(decay_log) * jax.nn.softplus(decay_pre + decay_bias)
    mixed = span_core(query_vecs, key_vecs, value_vecs, beta_vals, log_decays)
    gated = (
        mixed
        * rms_scale(mixed)
        * gain_out
        * jax.nn.silu(gate_pre.reshape(length, head_count, value_size))
        * live_mask[:, None, None]
    )
    return gated.reshape(length, head_count * value_size)


def norm_back(values, gain, grad_normed):
    scale = rms_scale(values)
    unit_vals = values * scale
    grad_unit = grad_normed * gain
    grad_values = scale * (
        grad_unit - unit_vals * jnp.mean(grad_unit * unit_vals, axis=-1, keepdims=True)
    )
    return (grad_values, jnp.sum(grad_normed * unit_vals, axis=0))


def fetch_mixer(masters):
    return (
        lax.all_gather(masters[0].astype(jnp.bfloat16), "dp", axis=0, tiled=True),
        lax.all_gather(masters[1].astype(jnp.bfloat16), "dp", axis=0, tiled=True),
        lax.all_gather(masters[2].astype(jnp.bfloat16), "dp", axis=0, tiled=True),
        lax.all_gather(masters[3].astype(jnp.bfloat16), "dp", axis=0, tiled=True),
        lax.all_gather(masters[4].astype(jnp.bfloat16), "dp", axis=0, tiled=True),
        lax.all_gather(masters[5].astype(jnp.bfloat16), "dp", axis=0, tiled=True),
        lax.all_gather(masters[6].astype(jnp.bfloat16), "dp", axis=2, tiled=True),
        lax.all_gather(masters[7].astype(jnp.bfloat16), "dp", axis=2, tiled=True),
        lax.all_gather(masters[8].astype(jnp.bfloat16), "dp", axis=2, tiled=True),
        lax.all_gather(masters[9].astype(jnp.bfloat16), "dp", axis=1, tiled=True),
    )


def fetch_ffn(gate_master, up_master, down_master):
    return (
        lax.all_gather(gate_master.astype(jnp.bfloat16), "dp", axis=0, tiled=True),
        lax.all_gather(up_master.astype(jnp.bfloat16), "dp", axis=0, tiled=True),
        lax.all_gather(down_master.astype(jnp.bfloat16), "dp", axis=1, tiled=True),
    )


def local(
    tokens,
    lengths,
    cotangent,
    gain_in,
    gain_ffn,
    gain_out,
    w_query,
    w_key,
    w_value,
    w_gate,
    w_beta,
    w_decay,
    conv_query,
    conv_key,
    conv_value,
    decay_log,
    decay_bias,
    w_output,
    w_ffn_gate,
    w_ffn_up,
    w_ffn_down,
):
    full_in, full_ffn, full_out = (
        lax.all_gather(gain_in, ("dp", "tensor"), axis=0, tiled=True),
        lax.all_gather(gain_ffn, ("dp", "tensor"), axis=0, tiled=True),
        lax.all_gather(gain_out, ("dp", "tensor"), axis=0, tiled=True),
    )
    mixer_masters = (
        w_query,
        w_key,
        w_value,
        w_gate,
        w_beta,
        w_decay,
        conv_query,
        conv_key,
        conv_value,
        w_output,
    )
    mixer_weights = fetch_mixer(mixer_masters)
    local_heads = w_beta.shape[1]
    head_start = lax.axis_index("tensor") * local_heads
    local_log = lax.dynamic_slice_in_dim(decay_log, head_start, local_heads)
    local_bias = lax.dynamic_slice_in_dim(decay_bias, head_start, local_heads)
    inputs = tokens.astype(jnp.float32)
    normed_in = (inputs * rms_scale(inputs) * full_in).astype(jnp.bfloat16)
    seq_in = lax.all_gather(normed_in, "tensor", axis=0, tiled=True)
    pre_acts = [
        jnp.dot(seq_in, mixer_weights[index], preferred_element_type=jnp.float32)
        for index in range(6)
    ]
    conv_floats = [mixer_weights[index].astype(jnp.float32) for index in range(6, 9)]
    positions = jnp.arange(seq_in.shape[0], dtype=jnp.int32)
    live_mask = (positions < lengths[0]).astype(jnp.float32)

    def mixer_fn(
        query_pre,
        key_pre,
        value_pre,
        gate_pre,
        beta_pre,
        decay_pre,
        conv_q,
        conv_k,
        conv_v,
        log_rate,
        rate_bias,
        norm_gain,
    ):
        return mixer_local(
            query_pre,
            key_pre,
            value_pre,
            gate_pre,
            beta_pre,
            decay_pre,
            conv_q,
            conv_k,
            conv_v,
            log_rate,
            rate_bias,
            norm_gain,
            live_mask,
        )

    mixed, pull_mixer = jax.vjp(
        mixer_fn,
        pre_acts[0],
        pre_acts[1],
        pre_acts[2],
        pre_acts[3],
        pre_acts[4],
        pre_acts[5],
        conv_floats[0],
        conv_floats[1],
        conv_floats[2],
        local_log,
        local_bias,
        full_out,
    )
    mixed_low = mixed.astype(jnp.bfloat16)
    attn_part = jnp.dot(mixed_low, mixer_weights[9], preferred_element_type=jnp.float32)
    hidden = inputs + lax.psum_scatter(attn_part, "tensor", scatter_dimension=0, tiled=True)
    normed_ffn = (hidden * rms_scale(hidden) * full_ffn).astype(jnp.bfloat16)
    seq_ffn = lax.all_gather(normed_ffn, "tensor", axis=0, tiled=True)
    gate_weight, up_weight, down_weight = fetch_ffn(w_ffn_gate, w_ffn_up, w_ffn_down)
    gate_act = jnp.dot(seq_ffn, gate_weight, preferred_element_type=jnp.float32)
    up_act = jnp.dot(seq_ffn, up_weight, preferred_element_type=jnp.float32)
    sigmoid_gate = jax.nn.sigmoid(gate_act)
    silu_gate = gate_act * sigmoid_gate
    inner = (silu_gate * up_act).astype(jnp.bfloat16)
    ffn_part = jnp.dot(inner, down_weight, preferred_element_type=jnp.float32)
    result = (
        hidden
        + lax.psum_scatter(
            ffn_part.astype(jnp.bfloat16), "tensor", scatter_dimension=0, tiled=True
        ).astype(jnp.float32)
    ).astype(jnp.bfloat16)
    gate_weight, up_weight, down_weight = fetch_ffn(w_ffn_gate, w_ffn_up, w_ffn_down)
    seq_cot = lax.all_gather(cotangent, "tensor", axis=0, tiled=True)
    grad_inner = jnp.dot(seq_cot, down_weight.T, preferred_element_type=jnp.float32)
    grad_down = jnp.dot(inner.T, seq_cot, preferred_element_type=jnp.float32)
    grad_gate_act = (
        grad_inner * up_act * sigmoid_gate * (1.0 + gate_act * (1.0 - sigmoid_gate))
    ).astype(jnp.bfloat16)
    grad_up_act = (grad_inner * silu_gate).astype(jnp.bfloat16)
    grad_gate_w = jnp.dot(seq_ffn.T, grad_gate_act, preferred_element_type=jnp.float32)
    grad_up_w = jnp.dot(seq_ffn.T, grad_up_act, preferred_element_type=jnp.float32)
    grad_seq_ffn = jnp.dot(grad_gate_act, gate_weight.T, preferred_element_type=jnp.float32)
    grad_seq_ffn = grad_seq_ffn + jnp.dot(
        grad_up_act, up_weight.T, preferred_element_type=jnp.float32
    )
    grad_normed_ffn = lax.psum_scatter(
        grad_seq_ffn.astype(jnp.bfloat16), "tensor", scatter_dimension=0, tiled=True
    ).astype(jnp.float32)
    ffn_grads = (
        lax.psum_scatter(grad_gate_w, "dp", scatter_dimension=0, tiled=True),
        lax.psum_scatter(grad_up_w, "dp", scatter_dimension=0, tiled=True),
        lax.psum_scatter(grad_down, "dp", scatter_dimension=1, tiled=True),
    )
    grad_hidden_norm, grad_gain_ffn = norm_back(hidden, full_ffn, grad_normed_ffn)
    grad_hidden = cotangent.astype(jnp.float32) + grad_hidden_norm
    mixer_weights = fetch_mixer(mixer_masters)
    grad_branch = grad_hidden.astype(jnp.bfloat16)
    seq_grad_branch = lax.all_gather(grad_branch, "tensor", axis=0, tiled=True)
    grad_mixed = jnp.dot(seq_grad_branch, mixer_weights[9].T, preferred_element_type=jnp.float32)
    grad_out_w = jnp.dot(mixed_low.T, seq_grad_branch, preferred_element_type=jnp.float32)
    pulled = pull_mixer(grad_mixed)
    grad_pre = [pulled[index].astype(jnp.bfloat16) for index in range(6)]
    grad_proj = [
        jnp.dot(seq_in.T, grad_pre[index], preferred_element_type=jnp.float32) for index in range(6)
    ]
    grad_seq_in = jnp.dot(grad_pre[0], mixer_weights[0].T, preferred_element_type=jnp.float32)
    for index in range(1, 6):
        grad_seq_in = grad_seq_in + jnp.dot(
            grad_pre[index], mixer_weights[index].T, preferred_element_type=jnp.float32
        )
    grad_normed_in = lax.psum_scatter(
        grad_seq_in.astype(jnp.bfloat16), "tensor", scatter_dimension=0, tiled=True
    ).astype(jnp.float32)
    mixer_grads = (
        lax.psum_scatter(grad_proj[0], "dp", scatter_dimension=0, tiled=True),
        lax.psum_scatter(grad_proj[1], "dp", scatter_dimension=0, tiled=True),
        lax.psum_scatter(grad_proj[2], "dp", scatter_dimension=0, tiled=True),
        lax.psum_scatter(grad_proj[3], "dp", scatter_dimension=0, tiled=True),
        lax.psum_scatter(grad_proj[4], "dp", scatter_dimension=0, tiled=True),
        lax.psum_scatter(grad_proj[5], "dp", scatter_dimension=0, tiled=True),
        lax.psum_scatter(pulled[6], "dp", scatter_dimension=2, tiled=True),
        lax.psum_scatter(pulled[7], "dp", scatter_dimension=2, tiled=True),
        lax.psum_scatter(pulled[8], "dp", scatter_dimension=2, tiled=True),
        lax.psum_scatter(grad_out_w, "dp", scatter_dimension=1, tiled=True),
    )
    grad_inputs_norm, grad_gain_in = norm_back(inputs, full_in, grad_normed_in)
    grad_tokens = grad_hidden + grad_inputs_norm
    padded_log = lax.dynamic_update_slice(jnp.zeros_like(decay_log), pulled[9], (head_start,))
    padded_bias = lax.dynamic_update_slice(jnp.zeros_like(decay_bias), pulled[10], (head_start,))
    summed_in, summed_ffn, summed_out, summed_log, summed_bias = lax.psum(
        (grad_gain_in, grad_gain_ffn, pulled[11], padded_log, padded_bias), ("dp", "tensor")
    )
    shard_index = lax.axis_index("dp") * lax.axis_size("tensor") + lax.axis_index("tensor")
    gain_piece = gain_in.shape[0]
    out_piece = gain_out.shape[0]
    return (
        result,
        grad_tokens,
        lax.dynamic_slice_in_dim(summed_in, shard_index * gain_piece, gain_piece),
        lax.dynamic_slice_in_dim(summed_ffn, shard_index * gain_piece, gain_piece),
        lax.dynamic_slice_in_dim(summed_out, shard_index * out_piece, out_piece),
        mixer_grads[0],
        mixer_grads[1],
        mixer_grads[2],
        mixer_grads[3],
        mixer_grads[4],
        mixer_grads[5],
        mixer_grads[6],
        mixer_grads[7],
        mixer_grads[8],
        summed_log,
        summed_bias,
        mixer_grads[9],
        ffn_grads[0],
        ffn_grads[1],
        ffn_grads[2],
    )


def solution(mesh):
    placed = (
        P(("dp", "tensor"), None),
        P("dp"),
        P(("dp", "tensor"), None),
        P(("dp", "tensor")),
        P(("dp", "tensor")),
        P(("dp", "tensor")),
        P("dp", "tensor"),
        P("dp", "tensor"),
        P("dp", "tensor"),
        P("dp", "tensor"),
        P("dp", "tensor"),
        P("dp", "tensor"),
        P(None, "tensor", "dp"),
        P(None, "tensor", "dp"),
        P(None, "tensor", "dp"),
        P(),
        P(),
        P("tensor", "dp"),
        P("dp", "tensor"),
        P("dp", "tensor"),
        P("tensor", "dp"),
    )
    return jax.shard_map(
        local,
        mesh=mesh,
        in_specs=placed,
        out_specs=(
            P(("dp", "tensor"), None),
            P(("dp", "tensor"), None),
            P(("dp", "tensor")),
            P(("dp", "tensor")),
            P(("dp", "tensor")),
            P("dp", "tensor"),
            P("dp", "tensor"),
            P("dp", "tensor"),
            P("dp", "tensor"),
            P("dp", "tensor"),
            P("dp", "tensor"),
            P(None, "tensor", "dp"),
            P(None, "tensor", "dp"),
            P(None, "tensor", "dp"),
            P(),
            P(),
            P("tensor", "dp"),
            P("dp", "tensor"),
            P("dp", "tensor"),
            P("tensor", "dp"),
        ),
        check_vma=False,
    )
```

profile of v0, /device:TPU:0, one launch (start us, length us, event | category | flops | bytes accessed | tf_op | source)
XLA Modules:
  0.0 2993.7 jit_solution(8830457867076277600)
XLA Ops:
  11.5 42.2 %all-reduce.35 = (f32[2048]{0:T(1024)S(1)}, f32[512]{0:T(512)S(1)}, f32[2048]{0:T(1024)S(1)}) all-reduce(f32[2048]{0:T(1024)S(1)} %dynamic-update-slice, f32[512]{0:T(512)S(1)} %dynamic-update-slice.1, f32[2048]{0:T(1024)S(1)} %dynamic-update-slice.2), channel_id=1, replica_groups=mesh['dp'=16,'tensor'=2] {'dp','tensor'}, use_global_device_ids=true, to_apply=%add.31 | all-reduce | flops 4608 | bytes 36864
  60.9 21.0 all_gather.72
  212.1 119.3 %custom-call.12 = f32[8,3,1,64,64]{3,4,2,1,0:T(8,128)} custom-call(f32[8,3,1,64,64]{4,3,2,1,0:T(8,128)} %get-tuple-element.933), custom_call_target="InvertDiagBlocksLowerTriangular" | custom-call | tf_op jit(solution)/shard_map/jvp()/triangular_solve | solution.py:56
  365.7 104.5 %while.54 = (s32[]{:T(128)}, f32[3,256,512]{2,1,0:T(8,128)S(1)}, f32[8,3,64,512]{3,2,1,0:T(8,128)}, f32[8,3,256,512]{3,2,1,0:T(8,128)}, f32[8,3,64,512]{3,2,1,0:...) while((s32[]{:T(128)}, f32[3,256,512]{2,1,0:T(8,128)S(1)}, ...), condition=%wide.region_5.6_spmd.clone, body=%wide.region_4.5_spmd.clone.sunk | while | flops 984121344 | bytes 13676790 | solution.py:92
  505.8 51.1 %reduce-scatter.28.cloned.1.call-done = f32[256,2048]{1,0:T(8,128)} async-done(((f32[512,2048]{1,0:T(8,128)}), f32[256,2048]{1,0:T(8,128)}) %reduce-scatter.28.cloned.1.call-update) | async-done | bytes 2097168 | tf_op jit(solution)/shard_map/reduce_scatter | solution.py:281
  564.6 89.8 %all-gather.27.cloned.1.call-done = bf16[2048,2816]{1,0:T(8,128)(2,1)} async-done(((bf16[128,2816]{1,0:T(8,128)(2,1)}), bf16[2048,2816]{1,0:T(8,128)(2,1)}) %all-gather.27.cloned.1.call-update) | async-done | bytes 11534352 | tf_op jit(solution)/shard_map/all_gather | solution.py:172
  654.3 33.5 %all-gather.25.cloned.1.call-done = bf16[512,2048]{1,0:T(8,128)(2,1)} async-done(((bf16[256,2048]{1,0:T(8,128)(2,1)}), bf16[512,2048]{1,0:T(8,128)(2,1)}) %all-gather.25.cloned.1.call-update) | async-done | bytes 2097168 | tf_op jit(solution)/shard_map/all_gather | solution.py:283
  700.7 84.4 %all-gather.29.cloned.1.call-done = bf16[2048,2816]{1,0:T(8,128)(2,1)} async-done(((bf16[128,2816]{1,0:T(8,128)(2,1)}), bf16[2048,2816]{1,0:T(8,128)(2,1)}) %all-gather.29.cloned.1.call-update) | async-done | bytes 11534352 | tf_op jit(solution)/shard_map/all_gather | solution.py:173
  818.1 100.2 %all-gather.31.cloned.1.call-done = bf16[2816,2048]{1,0:T(8,128)(2,1)} async-done(((bf16[2816,128]{1,0:T(8,128)(2,1)}), bf16[2816,2048]{1,0:T(8,128)(2,1)}) %all-gather.31.cloned.1.call-update) | async-done | bytes 11534352 | tf_op jit(solution)/shard_map/all_gather | solution.py:174
  955.6 30.1 %reduce-scatter.32.cloned.1.call-done = bf16[256,2048]{1,0:T(8,128)(2,1)} async-done(((bf16[512,2048]{1,0:T(8,128)(2,1)}), bf16[256,2048]{1,0:T(8,128)(2,1)}) %reduce-scatter.32.cloned.1.call-update) | async-done | bytes 1048592 | tf_op jit(solution)/shard_map/reduce_scatter | solution.py:311
  999.0 24.4 all-gather.35.cloned.1.call-done
  1068.3 222.3 %while.55 = (s32[]{:T(128)}, f32[3,256,512]{2,1,0:T(8,128)S(1)}, f32[8,3,64,512]{3,2,1,0:T(8,128)}, f32[8,3,64,256]{3,2,1,0:T(8,128)}, f32[8,3,64,256]{3,2,1,0:T...) while((s32[]{:T(128)}, f32[3,256,512]{2,1,0:T(8,128)S(1)}, ...), condition=%wide.region_16.17_spmd.clone, body=%wide.region_13.16_spmd.clone.sunk | while | flops 1967161088 | bytes 22627696 | solution.py:92
  1513.5 57.5 %reduce-scatter.54.cloned.1.call-done = f32[128,3]{1,0:T(8,128)} async-done(((f32[2048,3]{1,0:T(8,128)}), f32[128,3]{1,0:T(8,128)}) %reduce-scatter.54.cloned.1.call-update) | async-done | bytes 1552
  1572.5 59.6 %reduce-scatter.52.cloned.1.call-done = f32[128,3]{1,0:T(8,128)} async-done(((f32[2048,3]{1,0:T(8,128)}), f32[128,3]{1,0:T(8,128)}) %reduce-scatter.52.cloned.1.call-update) | async-done | bytes 1552
  1633.6 32.0 %reduce-scatter.34.cloned.1.call-done = bf16[256,2048]{1,0:T(8,128)(2,1)} async-done(((bf16[512,2048]{1,0:T(8,128)(2,1)}), bf16[256,2048]{1,0:T(8,128)(2,1)}) %reduce-scatter.34.cloned.1.call-update) | async-done | bytes 1048592 | tf_op jit(solution)/shard_map/reduce_scatter | solution.py:336
  1667.7 40.3 %all-reduce.34 = (f32[2048]{0:T(1024)S(1)}, f32[2048]{0:T(1024)S(1)}, f32[512]{0:T(512)S(1)}, f32[6]{0:T(128)}, f32[6]{0:T(128)}) all-reduce(f32[2048]{0:T(1024)S(1)} %get-tuple-element.791, f32[2048]{0:T(1024)S(1)} %copy-done.130, f32[512]{0:T(512)S(1)} %copy-done.144, ...), channel_id=1, replica_groups=mesh['dp'=16,'tensor'=2] {'dp','tensor'}, use_global_device_ids=true, to_apply=%region_30.32 | all-reduce | flops 4620 | bytes 36960 | tf_op jit(solution)/shard_map/psum | solution.py:355
  1714.9 75.0 %reduce-scatter.38.cloned.1.call-done = f32[128,768]{1,0:T(8,128)} async-done(((f32[2048,768]{1,0:T(8,128)}), f32[128,768]{1,0:T(8,128)}) %reduce-scatter.38.cloned.1.call-update) | async-done | bytes 393232 | tf_op jit(solution)/shard_map/reduce_scatter | solution.py:341
  1790.0 89.5 %reduce-scatter.36.cloned.1.call-done = f32[128,768]{1,0:T(8,128)} async-done(((f32[2048,768]{1,0:T(8,128)}), f32[128,768]{1,0:T(8,128)}) %reduce-scatter.36.cloned.1.call-update) | async-done | bytes 393232 | tf_op jit(solution)/shard_map/reduce_scatter | solution.py:340
  1879.5 138.4 %reduce-scatter.44.cloned.1.call-done = f32[1536,128]{1,0:T(8,128)} async-done(((f32[1536,2048]{1,0:T(8,128)}), f32[1536,128]{1,0:T(8,128)}) %reduce-scatter.44.cloned.1.call-update) | async-done | bytes 786448 | tf_op jit(solution)/shard_map/reduce_scatter | solution.py:349
  2017.9 138.6 %reduce-scatter.40.cloned.1.call-done = f32[128,1536]{1,0:T(8,128)} async-done(((f32[2048,1536]{1,0:T(8,128)}), f32[128,1536]{1,0:T(8,128)}) %reduce-scatter.40.cloned.1.call-update) | async-done | bytes 786448 | tf_op jit(solution)/shard_map/reduce_scatter | solution.py:342
  2156.5 138.4 %reduce-scatter.42.cloned.1.call-done = f32[128,1536]{1,0:T(8,128)} async-done(((f32[2048,1536]{1,0:T(8,128)}), f32[128,1536]{1,0:T(8,128)}) %reduce-scatter.42.cloned.1.call-update) | async-done | bytes 786448 | tf_op jit(solution)/shard_map/reduce_scatter | solution.py:343
  2295.0 230.6 %reduce-scatter.46.cloned.1.call-done = f32[128,2816]{1,0:T(8,128)} async-done(((f32[2048,2816]{1,0:T(8,128)}), f32[128,2816]{1,0:T(8,128)}) %reduce-scatter.46.cloned.1.call-update) | async-done | bytes 1441808 | tf_op jit(solution)/shard_map/reduce_scatter | solution.py:315
  2525.5 230.7 %reduce-scatter.48.cloned.1.call-done = f32[128,2816]{1,0:T(8,128)} async-done(((f32[2048,2816]{1,0:T(8,128)}), f32[128,2816]{1,0:T(8,128)}) %reduce-scatter.48.cloned.1.call-update) | async-done | bytes 1441808 | tf_op jit(solution)/shard_map/reduce_scatter | solution.py:316
  2756.2 230.7 %reduce-scatter.50.cloned.1.call-done = f32[2816,128]{1,0:T(8,128)} async-done(((f32[2816,2048]{1,0:T(8,128)}), f32[2816,128]{1,0:T(8,128)}) %reduce-scatter.50.cloned.1.call-update) | async-done | bytes 1441808 | tf_op jit(solution)/shard_map/reduce_scatter | solution.py:317
  (863 shorter events, 917.8 us)
Async XLA Ops:
  7.2 156.7 %all-gather.13.cloned.1.call-start = ((), (), s32[]{:S(2)}) async-start(), calls=%async_computation.17 | async-start | bytes 3145728 | tf_op jit(solution)/shard_map/all_gather | solution.py:225
  57.9 277.6 %all-gather.17.cloned.1.call-start = ((), (), s32[]{:S(2)}) async-start(), calls=%async_computation.19 | async-start | bytes 6684672 | tf_op jit(solution)/shard_map/all_gather | solution.py:159
  58.8 427.0 %all-gather.21.cloned.1.call-start = ((), (), s32[]{:S(2)}) async-start(), calls=%async_computation.21 | async-start | bytes 6684672 | tf_op jit(solution)/shard_map/all_gather | solution.py:160
  59.6 435.1 %all-gather.23.cloned.1.call-start = ((), (), s32[]{:S(2)}) async-start(), calls=%async_computation.22 | async-start | bytes 6684672 | tf_op jit(solution)/shard_map/all_gather | solution.py:166
  60.5 496.3 %reduce-scatter.28.cloned.1.call-start = ((), (), s32[]{:S(2)}) async-start(), calls=%async_computation.23 | async-start | bytes 6291456 | tf_op jit(solution)/shard_map/reduce_scatter | solution.py:281
  505.7 182.1 %all-gather.25.cloned.1.call-start = ((), (), s32[]{:S(2)}) async-start(), calls=%async_computation.24 | async-start | bytes 3145728 | tf_op jit(solution)/shard_map/all_gather | solution.py:283
  560.1 225.1 %all-gather.29.cloned.1.call-start = ((), (), s32[]{:S(2)}) async-start(), calls=%async_computation.26 | async-start | bytes 12255232 | tf_op jit(solution)/shard_map/all_gather | solution.py:173
  562.2 255.9 %all-gather.33.cloned.1.call-start = ((), (), s32[]{:S(2)}) async-start(), calls=%async_computation.29 | async-start | bytes 3145728 | tf_op jit(solution)/shard_map/all_gather | solution.py:298
  563.0 355.4 %all-gather.31.cloned.1.call-start = ((), (), s32[]{:S(2)}) async-start(), calls=%async_computation.27 | async-start | bytes 12255232 | tf_op jit(solution)/shard_map/all_gather | solution.py:174
  564.5 421.2 %reduce-scatter.32.cloned.1.call-start = ((), (), s32[]{:S(2)}) async-start(), calls=%async_computation.30 | async-start | bytes 3145728 | tf_op jit(solution)/shard_map/reduce_scatter | solution.py:311
  990.1 518.8 %reduce-scatter.58.cloned.1.call-start = ((), (), s32[]{:S(2)}) async-start(), calls=%async_computation.44 | async-start | bytes 139264
  1340.6 169.9 %reduce-scatter.56.cloned.1.call-start = ((), (), s32[]{:S(2)}) async-start(), calls=%async_computation.43 | async-start | bytes 139264
  1386.3 184.7 %reduce-scatter.54.cloned.1.call-start = ((), (), s32[]{:S(2)}) async-start(), calls=%async_computation.42 | async-start | bytes 1114112
  1388.3 243.8 %reduce-scatter.52.cloned.1.call-start = ((), (), s32[]{:S(2)}) async-start(), calls=%async_computation.41 | async-start | bytes 1114112
  1390.1 275.5 %reduce-scatter.34.cloned.1.call-start = ((), (), s32[]{:S(2)}) async-start(), calls=%async_computation.32 | async-start | bytes 3145728 | tf_op jit(solution)/shard_map/reduce_scatter | solution.py:336
  1419.2 290.5 %reduce-scatter.30.cloned.1.call-start = ((), (), s32[]{:S(2)}) async-start(), calls=%async_computation.28 | async-start | bytes 3145728 | tf_op jit(solution)/shard_map/reduce_scatter | solution.py:293
  1430.2 359.8 %reduce-scatter.38.cloned.1.call-start = ((), (), s32[]{:S(2)}) async-start(), calls=%async_computation.34 | async-start | bytes 6684672 | tf_op jit(solution)/shard_map/reduce_scatter | solution.py:341
  1436.0 443.5 %reduce-scatter.36.cloned.1.call-start = ((), (), s32[]{:S(2)}) async-start(), calls=%async_computation.33 | async-start | bytes 6684672 | tf_op jit(solution)/shard_map/reduce_scatter | solution.py:340
  1440.6 577.4 %reduce-scatter.44.cloned.1.call-start = ((), (), s32[]{:S(2)}) async-start(), calls=%async_computation.37 | async-start | bytes 13369344 | tf_op jit(solution)/shard_map/reduce_scatter | solution.py:349
  1450.7 705.8 %reduce-scatter.40.cloned.1.call-start = ((), (), s32[]{:S(2)}) async-start(), calls=%async_computation.35 | async-start | bytes 13369344 | tf_op jit(solution)/shard_map/reduce_scatter | solution.py:342
  1458.5 836.4 %reduce-scatter.42.cloned.1.call-start = ((), (), s32[]{:S(2)}) async-start(), calls=%async_computation.36 | async-start | bytes 13369344 | tf_op jit(solution)/shard_map/reduce_scatter | solution.py:343
  1466.5 1059.1 %reduce-scatter.46.cloned.1.call-start = ((), (), s32[]{:S(2)}) async-start(), calls=%async_computation.38 | async-start | bytes 24510464 | tf_op jit(solution)/shard_map/reduce_scatter | solution.py:315
  1480.7 1275.5 %reduce-scatter.48.cloned.1.call-start = ((), (), s32[]{:S(2)}) async-start(), calls=%async_computation.39 | async-start | bytes 24510464 | tf_op jit(solution)/shard_map/reduce_scatter | solution.py:316
  1493.6 1493.4 %reduce-scatter.50.cloned.1.call-start = ((), (), s32[]{:S(2)}) async-start(), calls=%async_computation.40 | async-start | bytes 24510464 | tf_op jit(solution)/shard_map/reduce_scatter | solution.py:317
  (167 other events, 7273.8 us)
Sparse Core Ops, SparseCore 0:
  56.4 32.9 all-gather.12
  92.3 47.6 all-gather.14
  142.8 44.8 all-gather.18
  190.4 61.2 all-gather.16
  254.4 62.2 all-gather.20
  319.3 63.5 all-gather.22
  503.6 53.2 reduce-scatter.27
  560.0 94.3 all-gather.26
  690.8 94.3 all-gather.28
  820.9 97.3 all-gather.30
  990.2 33.1 all-gather.34
  1340.8 55.0 reduce-scatter.57
  1399.2 54.0 reduce-scatter.55
  1456.7 54.3 reduce-scatter.59
  1514.6 56.3 reduce-scatter.53
  1575.6 56.4 reduce-scatter.51
  1705.0 84.9 reduce-scatter.37
  1795.0 84.4 reduce-scatter.35
  1884.0 133.9 reduce-scatter.43
  2022.6 133.9 reduce-scatter.39
  2161.0 133.9 reduce-scatter.41
  2299.5 226.0 reduce-scatter.45
  2530.2 225.9 reduce-scatter.47
  2760.9 225.9 reduce-scatter.49
  (5 shorter events, 155.6 us)
where the time goes:
time: 3000 us; the launch traced here: 2990 us
  waiting for transfers between devices  1860 us (62%)
  matrix products  532 us (18%)
  other arithmetic  251 us (8%)
  blocking collectives  180 us (6%)
  local copies, waits for them, and re-layouts  147 us (5%)
    reduce_scatter x1, waiting for transfers between devices, local(): lax.psum_scatter(grad_down, 'dp', scatter_dimension=1, tiled=True)  231 us
    reduce_scatter x1, waiting for transfers between devices, local(): lax.psum_scatter(grad_up_w, 'dp', scatter_dimension=0, tiled=True)  231 us
    reduce_scatter x1, waiting for transfers between devices, local(): lax.psum_scatter(grad_gate_w, 'dp', scatter_dimension=0, tiled=True)  231 us
    reduce_scatter x1, waiting for transfers between devices, local(): lax.psum_scatter(grad_proj[2], 'dp', scatter_dimension=0, tiled=True)  139 us
    reduce_scatter x1, waiting for transfers between devices, local(): lax.psum_scatter(grad_proj[3], 'dp', scatter_dimension=0, tiled=True)  138 us
    reduce_scatter x1, waiting for transfers between devices, local(): lax.psum_scatter(grad_out_w, 'dp', scatter_dimension=1, tiled=True)  138 us
    another operation x4, other arithmetic, span_core(): lax.linalg.triangular_solve(lower_matrix, beta_blocks[..., None] * value_...  119 us
    unnamed x34, waiting for transfers between devices  118 us
  transfers between devices with their start and end apart: 29, of which 20 were waited for; matrix products, arithmetic and copies ran while one was open for 18% of the time, Pallas kernels for 0%

commit v1 on v0

v1 whole, which is shorter than its diff:
```python
import functools
import jax
import jax.numpy as jnp
from jax import lax
from jax.sharding import PartitionSpec as P
from jax.experimental import pallas as pl
from jax.experimental.pallas import tpu as pltpu

CH = 256
TILE = 64
PADR = 8
f32 = jnp.float32
bf16 = jnp.bfloat16


def mm(a, b, ca=1, cb=0):
    return lax.dot_general(
        a.astype(bf16), b.astype(bf16), (((ca,), (cb,)), ((), ())), preferred_element_type=f32
    )


def split2(a):
    high = a.astype(bf16)
    return high, (a - high.astype(f32)).astype(bf16)


def mm3(a, b, ca=1, cb=0):
    ah, al = split2(a)
    bh, bl = split2(b)
    return mm(ah, bh, ca, cb) + (mm(ah, bl, ca, cb) + mm(al, bh, ca, cb))


def iotas(n):
    return (
        lax.broadcasted_iota(jnp.int32, (n, n), 0),
        lax.broadcasted_iota(jnp.int32, (n, n), 1),
    )


def unit_lower_inverses(mats):
    n = mats[0].shape[0]
    rows, cols = iotas(n)
    eye = jnp.where(rows == cols, 1.0, 0.0).astype(f32)
    base = 8
    near = (rows // base) == (cols // base)
    powers = [jnp.where(near, a, 0.0) for a in mats]
    outs = [eye - p for p in powers]
    for _ in range(2):
        powers = [mm3(p, p) for p in powers]
        outs = [x + mm3(x, p) for x, p in zip(outs, powers)]
    size = base
    while size < n:
        wide = ((rows // (2 * size)) == (cols // (2 * size))) & ((rows // size) != (cols // size))
        halves = [mm3(jnp.where(wide, a, 0.0), x) for a, x in zip(mats, outs)]
        outs = [x - mm3(x, h) for x, h in zip(outs, halves)]
        size *= 2
    return outs


def sigm(v):
    return 1.0 / (1.0 + jnp.exp(-v))


def softplus(v):
    return jnp.maximum(v, 0.0) + jnp.log1p(jnp.exp(-jnp.abs(v)))


def pick(block, lane):
    lanes = lax.broadcasted_iota(jnp.int32, block.shape, 1)
    return jnp.sum(jnp.where(lanes == lane, block, 0.0), axis=1, keepdims=True)


def taps(ref):
    return [ref[i : i + 1, :] for i in range(4)]


def lanes_at(block, width):
    return pl.ds(pl.multiple_of(block * width, width), width)


def conv_rows(pad_ref, start, size, filt):
    total = None
    block = pad_ref[pl.ds(start, size + PADR), :]
    for i in range(4):
        term = filt[i] * block[PADR - 3 + i : PADR - 3 + i + size]
        total = term if total is None else total + term
    return total


def chunk_decay(logs, n):
    rows, cols = iotas(n)
    lower = jnp.where(rows >= cols, 1.0, 0.0).astype(f32)
    wide = jnp.broadcast_to(logs, (n, 128))
    h0 = wide.astype(bf16)
    r1 = wide - h0.astype(f32)
    h1 = r1.astype(bf16)
    h2 = (r1 - h1.astype(f32)).astype(bf16)
    col = (mm(lower, h0) + (mm(lower, h1) + mm(lower, h2)))[:, :1]
    row = (mm(h0, lower, 0, 1) + (mm(h1, lower, 0, 1) + mm(h2, lower, 0, 1)))[:1, :]
    return col, row


def suffix_sum(vals, n):
    rows, cols = iotas(n)
    upper = jnp.where(cols >= rows, 1.0, 0.0).astype(f32)
    wide = jnp.broadcast_to(vals, (n, 128))
    h0 = wide.astype(bf16)
    r1 = wide - h0.astype(f32)
    h1 = r1.astype(bf16)
    h2 = (r1 - h1.astype(f32)).astype(bf16)
    return (mm(upper, h0) + (mm(upper, h1) + mm(upper, h2)))[:, :1]


def load_padded(pad_ref, src_ref):
    pad_ref[0:PADR, :] = jnp.zeros((PADR, pad_ref.shape[1]), f32)
    pad_ref[PADR : PADR + src_ref.shape[0], :] = src_ref[...].astype(f32)


def fill_vectors(length, qpad, kpad, vpad, fq, fk, fv, qs, ks, vs):
    def body(t, _):
        start = pl.multiple_of(t * TILE, TILE)
        for pad, filt, dst, scale in ((qpad, fq, qs, 256 ** (-0.5)), (kpad, fk, ks, 1.0)):
            y = conv_rows(pad, start, TILE, filt)
            a = y * sigm(y)
            n = a * lax.rsqrt(jnp.sum(a * a, axis=1, keepdims=True) + 1e-06)
            dst[pl.ds(start, TILE), :] = (n * scale).astype(dst.dtype)
        y = conv_rows(vpad, start, TILE, fv)
        vs[pl.ds(start, TILE), :] = y * sigm(y)
        return 0

    lax.fori_loop(0, length // TILE, body, 0)


def beta_decay(h, heads, length, live_len, bd, log_ref, bias_ref):
    bp = pick(bd, h)
    dp = pick(bd, heads + h)
    live = (lax.broadcasted_iota(jnp.int32, (length, 1), 0) < live_len).astype(f32)
    rate = jnp.exp(pick(log_ref[0:1, :], h))
    sb = sigm(bp)
    zp = dp + pick(bias_ref[0:1, :], h)
    return sb, live, rate, zp


def fwd_kernel(
    heads, len_ref, q_ref, k_ref, v_ref, g_ref, bd_ref, fq_ref, fk_ref, fv_ref, log_ref, bias_ref,
    gain_ref, gated_ref, inv_ref, u_ref, mixed_ref, state_ref, qpad, kpad, vpad, qs, ks, vs,
):
    h = pl.program_id(0)
    length = q_ref.shape[0]
    chunks = length // CH
    load_padded(qpad, q_ref)
    load_padded(kpad, k_ref)
    load_padded(vpad, v_ref)
    fill_vectors(
        length, qpad, kpad, vpad, taps(fq_ref), taps(fk_ref), taps(fv_ref), qs, ks, vs
    )
    sb, live, rate, zp = beta_decay(h, heads, length, len_ref[0], bd_ref[...], log_ref, bias_ref)
    beta = sb * live
    logs = -rate * softplus(zp)
    rows, cols = iotas(CH)
    kept = []
    mats = []
    for n in range(chunks):
        part = slice(n * CH, (n + 1) * CH)
        col, row = chunk_decay(logs[part], CH)
        gaps = col - row
        decay = jnp.where(rows >= cols, jnp.exp(jnp.where(rows >= cols, gaps, 0.0)), 0.0)
        kf = ks[part, :]
        gram = mm3(kf, kf, 1, 1)
        mats.append(jnp.where(rows > cols, beta[part] * decay * gram, 0.0))
        kept.append((part, col, decay))
    inverses = unit_lower_inverses(mats)
    state = None
    for n in range(chunks):
        part, col, decay = kept[n]
        kf = ks[part, :]
        qf = qs[part, :]
        inv_ref[0, part, :] = inverses[n].astype(inv_ref.dtype)
        grow = jnp.exp(col)
        rhs = vs[part, :]
        if state is not None:
            rhs = rhs - grow * mm(kf, state)
        u = mm3(inverses[n], beta[part] * rhs)
        u_ref[part, :] = u.astype(u_ref.dtype)
        scores = mm(qf, kf, 1, 1) * decay
        out = mm(scores, u)
        if state is not None:
            out = out + grow * mm(qf, state)
        mixed_ref[part, :] = out
        if n + 1 < chunks:
            last = col[CH - 1 :, :]
            add = mm(kf * jnp.exp(last - col), u, 0, 0)
            state = add if state is None else jnp.exp(last) * state + add
            state_ref[0, n] = state
    gain = gain_ref[0:1, :]
    live_len = len_ref[0]

    def finish(t, _):
        start = pl.multiple_of(t * TILE, TILE)
        sl = pl.ds(start, TILE)
        m = mixed_ref[sl, :]
        gp = g_ref[sl, :].astype(f32)
        pos = start + lax.broadcasted_iota(jnp.int32, (TILE, 1), 0)
        alive = (pos < live_len).astype(f32)
        r = lax.rsqrt(jnp.mean(m * m, axis=1, keepdims=True) + 1e-05)
        gated_ref[sl, :] = (m * r * gain * (gp * sigm(gp)) * alive).astype(bf16)
        return 0

    lax.fori_loop(0, length // TILE, finish, 0)


def bwd_kernel(
    heads, len_ref, q_ref, k_ref, v_ref, g_ref, bd_ref, fq_ref, fk_ref, fv_ref, log_ref, bias_ref,
    gain_ref, inv_ref, u_ref, mixed_ref, state_ref, dg_ref,
    dpre_out, dfq_out, dfk_out, dfv_out, dgain_out, dsmall_out,
    qpad, kpad, vpad, qs, ks, vs, dos, dqs, dks, dvs, dbds,
):
    h = pl.program_id(0)
    length = q_ref.shape[0]
    chunks = length // CH
    load_padded(qpad, q_ref)
    load_padded(kpad, k_ref)
    load_padded(vpad, v_ref)
    fq, fk, fv = taps(fq_ref), taps(fk_ref), taps(fv_ref)
    fill_vectors(length, qpad, kpad, vpad, fq, fk, fv, qs, ks, vs)
    live_len = len_ref[0]
    gain = gain_ref[0:1, :]

    @pl.when(h == 0)
    def _():
        dgain_out[...] = jnp.zeros(dgain_out.shape, f32)
        dbds[...] = jnp.zeros(dbds.shape, f32)
        dsmall_out[...] = jnp.zeros(dsmall_out.shape, f32)

    def gate_back(t, acc):
        start = pl.multiple_of(t * TILE, TILE)
        sl = pl.ds(start, TILE)
        m = mixed_ref[sl, :]
        gp = g_ref[sl, :].astype(f32)
        pos = start + lax.broadcasted_iota(jnp.int32, (TILE, 1), 0)
        alive = (pos < live_len).astype(f32)
        r = lax.rsqrt(jnp.mean(m * m, axis=1, keepdims=True) + 1e-05)
        n = m * r
        t_ = dg_ref[sl, :].astype(f32) * alive
        s = sigm(gp)
        act = gp * s
        tn = t_ * n
        dpre_out[sl, lanes_at(2 * heads + h, 512)] = (
            tn * gain * (s + act * (1.0 - s))
        ).astype(bf16)
        dn = t_ * gain * act
        dos[sl, :] = r * (dn - n * jnp.mean(dn * n, axis=1, keepdims=True))
        return acc + jnp.sum((tn * act).reshape(TILE // 8, 8, tn.shape[1]), axis=0)

    dgain = lax.fori_loop(0, length // TILE, gate_back, jnp.zeros((8, gain.shape[1]), f32))
    dgain_out[...] += dgain

    sb, live, rate, zp = beta_decay(h, heads, length, live_len, bd_ref[...], log_ref, bias_ref)
    beta = sb * live
    sp = softplus(zp)
    logs = -rate * sp
    rows, cols = iotas(CH)
    incl = rows >= cols
    ones = jnp.ones((CH, 128), f32)
    dstate = None
    dbetas = [None] * chunks
    dlogs = [None] * chunks
    for n in reversed(range(chunks)):
        part = slice(n * CH, (n + 1) * CH)
        col, row = chunk_decay(logs[part], CH)
        gaps = col - row
        decay = jnp.where(incl, jnp.exp(jnp.where(incl, gaps, 0.0)), 0.0)
        grow = jnp.exp(col)
        last = col[CH - 1 :, :]
        kf = ks[part, :]
        qf = qs[part, :]
        u = u_ref[part, :].astype(f32)
        inv = inv_ref[0, part, :]
        do = dos[part, :]
        b = beta[part]
        gram = mm(kf, kf, 1, 1)
        strict_decay = jnp.where(rows > cols, decay, 0.0)
        scores = mm(qf, kf, 1, 1) * decay
        m_all = mm(do, u, 1, 1)
        du = mm(scores, do, 0, 0)
        tail = jnp.exp(last - col)
        if dstate is not None:
            kend = kf * tail
            du = du + mm(kend, dstate)
        dr = mm(inv, du, 0, 0)
        dvs[part, :] = b * dr
        da = mm(dr, u, 1, 1)
        da_dec = -da * strict_decay
        da_gram = da_dec * gram
        dbeta = jnp.sum(da_gram, axis=1, keepdims=True)
        msc = m_all * scores
        both = msc + b * da_gram
        rs = jnp.sum(both, axis=1, keepdims=True)
        both_h, both_l = split2(both)
        cs = (mm(both_h, ones, 0, 0) + mm(both_l, ones, 0, 0))[:, :1]
        dc = rs - cs
        dqk = m_all * decay
        dgram = b * da_dec
        dq = mm(dqk, kf)
        dk = mm(dqk, qf, 0, 0) + mm(dgram, kf) + mm(dgram, kf, 0, 0)
        rest = vs[part, :]
        dlast = None
        if n > 0:
            state = state_ref[0, n - 1]
            kst = mm(kf, state)
            qst = mm(qf, state)
            rest = rest - grow * kst
            dkst = -(b * grow) * dr
            dqst = grow * do
            dk = dk + mm(dkst, state, 1, 1)
            dq = dq + mm(dqst, state, 1, 1)
            dc = dc + jnp.sum(dkst * kst + dqst * qst, axis=1, keepdims=True)
            dprev = mm(kf, dkst, 0, 0) + mm(qf, dqst, 0, 0)
        dbetas[n] = dbeta + jnp.sum(dr * rest, axis=1, keepdims=True)
        if dstate is not None:
            dkend = mm(u, dstate, 1, 1)
            dk = dk + dkend * tail
            w = jnp.sum(dkend * kend, axis=1, keepdims=True)
            dc = dc - w
            dlast = jnp.sum(w, axis=0, keepdims=True)
            if n > 0:
                scale = jnp.exp(last)
                dprev = dprev + scale * dstate
                dlast = dlast + scale * jnp.sum(
                    jnp.sum(dstate * state, axis=1, keepdims=True), axis=0, keepdims=True
                )
        dlog = suffix_sum(dc, CH)
        if dlast is not None:
            dlog = dlog + dlast
        dlogs[n] = dlog
        dqs[part, :] = dq
        dks[part, :] = dk
        if n > 0:
            dstate = dprev
    dbeta = jnp.concatenate(dbetas, axis=0)
    dlog = jnp.concatenate(dlogs, axis=0)
    dbp = dbeta * live * sb * (1.0 - sb)
    dzp = -rate * dlog * sigm(zp)
    lanes = lax.broadcasted_iota(jnp.int32, (length, 128), 1)
    dbds[...] += jnp.where(lanes == h, dbp, 0.0) + jnp.where(lanes == heads + h, dzp, 0.0)

    @pl.when(h == heads - 1)
    def _():
        dpre_out[:, 12 * heads * 128 : (12 * heads + 1) * 128] = dbds[...].astype(bf16)

    small_lane = lax.broadcasted_iota(jnp.int32, (8, 128), 1)
    small_row = lax.broadcasted_iota(jnp.int32, (8, 128), 0)
    at_head = small_lane == h
    dsmall_out[...] += jnp.where(
        at_head & (small_row == 0), jnp.sum(dlog * logs, axis=0, keepdims=True), 0.0
    ) + jnp.where(at_head & (small_row == 1), jnp.sum(dzp, axis=0, keepdims=True), 0.0)

    def pre_back(t, _):
        start = pl.multiple_of(t * TILE, TILE)
        sl = pl.ds(start, TILE)
        for pad, filt, dref, scale in ((qpad, fq, dqs, 256 ** (-0.5)), (kpad, fk, dks, 1.0)):
            y = conv_rows(pad, start, TILE, filt)
            s = sigm(y)
            a = y * s
            r = lax.rsqrt(jnp.sum(a * a, axis=1, keepdims=True) + 1e-06)
            nn = a * r
            dn = dref[sl, :] * scale
            da_ = r * (dn - nn * jnp.sum(dn * nn, axis=1, keepdims=True))
            dref[sl, :] = da_ * (s + a * (1.0 - s))
        y = conv_rows(vpad, start, TILE, fv)
        s = sigm(y)
        dvs[sl, :] = dvs[sl, :] * (s + y * s * (1.0 - s))
        return 0

    lax.fori_loop(0, length // TILE, pre_back, 0)
    for dref in (dqs, dks, dvs):
        dref[length : length + PADR, :] = jnp.zeros((PADR, dref.shape[1]), f32)

    for pad, filt, dref, first, fout in (
        (qpad, fq, dqs, h, dfq_out),
        (kpad, fk, dks, heads + h, dfk_out),
        (vpad, fv, dvs, heads + h, dfv_out),
    ):
        width = dref.shape[1]

        def conv_back(t, accs, pad=pad, filt=filt, dref=dref, first=first, width=width):
            start = pl.multiple_of(t * TILE, TILE)
            dx = None
            new = []
            dys = dref[pl.ds(start, TILE + PADR), :]
            xs = pad[pl.ds(start, TILE + PADR), :]
            dy = dys[:TILE]
            for i in range(4):
                term = filt[i] * dys[3 - i : 3 - i + TILE]
                dx = term if dx is None else dx + term
                prod = dy * xs[PADR - 3 + i : PADR - 3 + i + TILE]
                new.append(accs[i] + jnp.sum(prod.reshape(TILE // 8, 8, width), axis=0))
            dpre_out[pl.ds(start, TILE), lanes_at(first, width)] = dx.astype(bf16)
            return tuple(new)

        accs = lax.fori_loop(
            0, length // TILE, conv_back, tuple(jnp.zeros((8, width), f32) for _ in range(4))
        )
        for i in range(4):
            fout[i : i + 1, :] = jnp.sum(accs[i], axis=0, keepdims=True)


def col_spec(length, width, first=0):
    return pl.BlockSpec((length, width), lambda h: (0, first + h))


def whole_spec(shape):
    return pl.BlockSpec(shape, lambda h: (0,) * len(shape))


def front_specs(length, heads):
    return [
        pl.BlockSpec(memory_space=pltpu.SMEM),
        col_spec(length, 256),
        col_spec(length, 256, heads),
        col_spec(length, 512, heads),
        col_spec(length, 512, 2 * heads),
        pl.BlockSpec((length, 128), lambda h: (0, 12 * heads)),
        col_spec(4, 256),
        col_spec(4, 256),
        col_spec(4, 512),
        whole_spec((1, 128)),
        whole_spec((1, 128)),
        whole_spec((1, 512)),
    ]


def mixer_forward(heads, lens, pre, fq, fk, fv, logs, bias, gain):
    length = pre.shape[0]
    chunks = length // CH
    kept = max(1, chunks - 1)
    return pl.pallas_call(
        functools.partial(fwd_kernel, heads),
        grid=(heads,),
        in_specs=front_specs(length, heads),
        out_specs=[
            col_spec(length, 512),
            pl.BlockSpec((1, length, CH), lambda h: (h, 0, 0)),
            col_spec(length, 512),
            col_spec(length, 512),
            pl.BlockSpec((1, kept, 256, 512), lambda h: (h, 0, 0, 0)),
        ],
        out_shape=[
            jax.ShapeDtypeStruct((length, heads * 512), bf16),
            jax.ShapeDtypeStruct((heads, length, CH), bf16),
            jax.ShapeDtypeStruct((length, heads * 512), bf16),
            jax.ShapeDtypeStruct((length, heads * 512), f32),
            jax.ShapeDtypeStruct((heads, kept, 256, 512), f32),
        ],
        scratch_shapes=[
            pltpu.VMEM((length + PADR, 256), f32),
            pltpu.VMEM((length + PADR, 256), f32),
            pltpu.VMEM((length + PADR, 512), f32),
            pltpu.VMEM((length, 256), f32),
            pltpu.VMEM((length, 256), f32),
            pltpu.VMEM((length, 512), f32),
        ],
        compiler_params=pltpu.CompilerParams(vmem_limit_bytes=50 * 1024 * 1024),
        name="mixer_forward",
    )(lens, pre, pre, pre, pre, pre, fq, fk, fv, logs, bias, gain)


def mixer_backward(heads, lens, pre, fq, fk, fv, logs, bias, gain, saved, dgated):
    length = pre.shape[0]
    chunks = length // CH
    kept = max(1, chunks - 1)
    inv, u, mixed, states = saved
    return pl.pallas_call(
        functools.partial(bwd_kernel, heads),
        grid=(heads,),
        in_specs=front_specs(length, heads)
        + [
            pl.BlockSpec((1, length, CH), lambda h: (h, 0, 0)),
            col_spec(length, 512),
            col_spec(length, 512),
            pl.BlockSpec((1, kept, 256, 512), lambda h: (h, 0, 0, 0)),
            col_spec(length, 512),
        ],
        out_specs=[
            whole_spec((length, pre.shape[1])),
            col_spec(4, 256), col_spec(4, 256), col_spec(4, 512),
            whole_spec((8, 512)), whole_spec((8, 128)),
        ],
        out_shape=[
            jax.ShapeDtypeStruct(pre.shape, bf16),
            jax.ShapeDtypeStruct((4, heads * 256), f32),
            jax.ShapeDtypeStruct((4, heads * 256), f32),
            jax.ShapeDtypeStruct((4, heads * 512), f32),
            jax.ShapeDtypeStruct((8, 512), f32),
            jax.ShapeDtypeStruct((8, 128), f32),
        ],
        scratch_shapes=[
            pltpu.VMEM((length + PADR, 256), f32),
            pltpu.VMEM((length + PADR, 256), f32),
            pltpu.VMEM((length + PADR, 512), f32),
            pltpu.VMEM((length, 256), f32),
            pltpu.VMEM((length, 256), f32),
            pltpu.VMEM((length, 512), f32),
            pltpu.VMEM((length, 512), f32),
            pltpu.VMEM((length + PADR, 256), f32),
            pltpu.VMEM((length + PADR, 256), f32),
            pltpu.VMEM((length + PADR, 512), f32),
            pltpu.VMEM((length, 128), f32),
        ],
        compiler_params=pltpu.CompilerParams(vmem_limit_bytes=50 * 1024 * 1024),
        name="mixer_backward",
    )(lens, pre, pre, pre, pre, pre, fq, fk, fv, logs, bias, gain, inv, u, mixed, states, dgated)


EXTRA = 128


def rms_scale(values):
    return lax.rsqrt(jnp.mean(values * values, axis=-1, keepdims=True) + 1e-05)


def norm_back(values, gain, grad_normed):
    scale = rms_scale(values)
    unit_vals = values * scale
    grad_unit = grad_normed * gain
    grad_values = scale * (
        grad_unit - unit_vals * jnp.mean(grad_unit * unit_vals, axis=-1, keepdims=True)
    )
    return (grad_values, jnp.sum(grad_normed * unit_vals, axis=0))


def pair_swap(values):
    return lax.ppermute(values, "tensor", [(0, 1), (1, 0)])


def pair_gather(values):
    other = pair_swap(values)
    first = lax.axis_index("tensor") == 0
    return jnp.concatenate(
        [jnp.where(first, values, other), jnp.where(first, other, values)], axis=0
    )


def pair_scatter(parts):
    rows = parts.shape[0] // 2
    mine = lax.axis_index("tensor") * rows
    kept = lax.dynamic_slice_in_dim(parts, mine, rows)
    sent = lax.dynamic_slice_in_dim(parts, rows - mine, rows).astype(bf16)
    return kept + pair_swap(sent).astype(f32)


def dot(a, b, ca=1, cb=0):
    return lax.dot_general(a, b, (((ca,), (cb,)), ((), ())), preferred_element_type=f32)


def gather_rows(values):
    return lax.all_gather(values, "dp", axis=0, tiled=True)


def scatter_rows(values):
    return lax.psum_scatter(values, "dp", scatter_dimension=0, tiled=True)


def pack_filters(fq, fk, fv, rows):
    flat = jnp.concatenate([fq, fk, fv], axis=2).reshape(-1)
    return flat.reshape(-1, rows).T


def local(
    tokens,
    lengths,
    cotangent,
    gain_in,
    gain_ffn,
    gain_out,
    w_query,
    w_key,
    w_value,
    w_gate,
    w_beta,
    w_decay,
    conv_query,
    conv_key,
    conv_value,
    decay_log,
    decay_bias,
    w_output,
    w_ffn_gate,
    w_ffn_up,
    w_ffn_down,
):
    heads = w_beta.shape[1]
    rows = w_query.shape[0]
    devices = lax.axis_size("dp")
    low = lambda v: v.astype(bf16)
    filters = pack_filters(conv_query, conv_key, conv_value, rows)
    filter_cols = filters.shape[1]
    small = jnp.concatenate([w_beta, w_decay, filters], axis=1)
    small = jnp.pad(small, ((0, 0), (0, EXTRA - small.shape[1])))
    proj_shard = jnp.concatenate(
        [low(w_query), low(w_key), low(w_value), low(w_gate), low(small)], axis=1
    )
    proj = gather_rows(proj_shard)
    out_t = gather_rows(low(w_output).T)
    gains = jnp.concatenate([gain_in, gain_ffn, gain_out])
    gains = lax.all_gather(gains, ("dp", "tensor"), axis=0, tiled=False)
    n_in, n_out = gain_in.shape[0], gain_out.shape[0]
    full_in = gains[:, :n_in].reshape(-1)
    full_ffn = gains[:, n_in : 2 * n_in].reshape(-1)
    full_out = gains[:, 2 * n_in :].reshape(1, -1)
    gate_weight = gather_rows(low(w_ffn_gate))
    up_weight = gather_rows(low(w_ffn_up))
    down_t = gather_rows(low(w_ffn_down).T)

    tap_count = conv_query.shape[0]
    piece_q, piece_v = conv_query.shape[2], conv_value.shape[2]
    flat = proj[:, 12 * heads * 128 + 2 * heads : 12 * heads * 128 + 2 * heads + filter_cols]
    flat = flat.reshape(devices, rows, filter_cols).transpose(0, 2, 1)
    flat = flat.reshape(devices, tap_count, heads, 2 * piece_q + piece_v).astype(f32)
    flat = flat.transpose(1, 2, 0, 3)
    filt_q = flat[..., :piece_q].reshape(tap_count, -1)
    filt_k = flat[..., piece_q : 2 * piece_q].reshape(tap_count, -1)
    filt_v = flat[..., 2 * piece_q :].reshape(tap_count, -1)

    head_start = lax.axis_index("tensor") * heads
    lane_pad = lambda v: jnp.pad(
        lax.dynamic_slice_in_dim(v, head_start, heads), (0, 128 - heads)
    ).reshape(1, 128)
    local_log, local_bias = lane_pad(decay_log), lane_pad(decay_bias)

    inputs = tokens.astype(f32)
    normed_in = low(inputs * rms_scale(inputs) * full_in)
    seq_in = pair_gather(normed_in)
    seq_cot = pair_gather(cotangent)
    pre = dot(seq_in, proj)
    mixer_args = (heads, lengths, pre, filt_q, filt_k, filt_v, local_log, local_bias, full_out)
    gated, *saved = mixer_forward(*mixer_args)
    hidden = inputs + pair_scatter(dot(gated, out_t, 1, 1))
    normed_ffn = low(hidden * rms_scale(hidden) * full_ffn)
    seq_ffn = pair_gather(normed_ffn)

    gate_act = dot(seq_ffn, gate_weight)
    up_act = dot(seq_ffn, up_weight)
    sigmoid_gate = jax.nn.sigmoid(gate_act)
    silu_gate = gate_act * sigmoid_gate
    inner = low(silu_gate * up_act)
    result = low(hidden + pair_scatter(dot(inner, down_t, 1, 1)))

    grad_inner = dot(seq_cot, down_t)
    grad_down = low(dot(seq_cot, inner, 0, 0))
    grad_gate_act = low(
        grad_inner * up_act * sigmoid_gate * (1.0 + gate_act * (1.0 - sigmoid_gate))
    )
    grad_up_act = low(grad_inner * silu_gate)
    grad_gate_w = low(dot(seq_ffn, grad_gate_act, 0, 0))
    grad_up_w = low(dot(seq_ffn, grad_up_act, 0, 0))
    grad_seq_ffn = dot(grad_gate_act, gate_weight, 1, 1) + dot(grad_up_act, up_weight, 1, 1)
    grad_normed_ffn = pair_scatter(grad_seq_ffn)
    grad_hidden_norm, grad_gain_ffn = norm_back(hidden, full_ffn, grad_normed_ffn)
    grad_hidden = cotangent.astype(f32) + grad_hidden_norm
    seq_grad_branch = pair_gather(low(grad_hidden))

    down_piece = scatter_rows(grad_down)
    gate_piece = scatter_rows(grad_gate_w)
    up_piece = scatter_rows(grad_up_w)

    grad_gated = dot(seq_grad_branch, out_t)
    grad_out_t = low(dot(seq_grad_branch, gated, 0, 0))
    grad_pre, grad_fq, grad_fk, grad_fv, grad_gain_out, grad_small = mixer_backward(
        *mixer_args, saved, low(grad_gated)
    )
    grad_seq_in = dot(grad_pre, proj, 1, 1)
    grad_proj = low(dot(seq_in, grad_pre, 0, 0))
    by_device = lambda g, piece: g.reshape(tap_count, heads, devices, piece)
    grad_flat = jnp.concatenate(
        [by_device(grad_fq, piece_q), by_device(grad_fk, piece_q), by_device(grad_fv, piece_v)],
        axis=3,
    ).transpose(2, 0, 1, 3)
    grad_flat = grad_flat.reshape(devices, filter_cols, rows).transpose(0, 2, 1)
    grad_flat = low(grad_flat.reshape(devices * rows, filter_cols))
    grad_proj = lax.dynamic_update_slice(grad_proj, grad_flat, (0, 12 * heads * 128 + 2 * heads))
    grad_normed_in = pair_scatter(grad_seq_in)
    out_piece = scatter_rows(grad_out_t).astype(f32)
    proj_piece = scatter_rows(grad_proj).astype(f32)

    grad_inputs_norm, grad_gain_in = norm_back(inputs, full_in, grad_normed_in)
    grad_tokens = grad_hidden + grad_inputs_norm

    spread = lambda v: lax.dynamic_update_slice(jnp.zeros_like(decay_log), v, (head_start,))
    sums = jnp.concatenate(
        [
            grad_gain_in,
            grad_gain_ffn,
            jnp.sum(grad_gain_out, axis=0),
            spread(grad_small[0, :heads]),
            spread(grad_small[1, :heads]),
        ]
    )
    sums = lax.psum(sums, ("dp", "tensor"))
    shard_index = lax.axis_index("dp") * lax.axis_size("tensor") + lax.axis_index("tensor")
    width = full_in.shape[0]
    out_width = full_out.shape[1]
    take = lambda first, piece: lax.dynamic_slice_in_dim(sums, first + shard_index * piece, piece)
    n_heads = decay_log.shape[0]
    tail = 2 * width + out_width

    q_end, k_end = heads * 256, 2 * heads * 256
    v_end, g_end = k_end + heads * 512, k_end + 2 * heads * 512
    grad_filters = proj_piece[:, g_end + 2 * heads : g_end + 2 * heads + filter_cols]
    grad_filters = grad_filters.T.reshape(tap_count, heads, 2 * piece_q + piece_v)
    return (
        result,
        grad_tokens,
        take(0, n_in),
        take(width, n_in),
        take(2 * width, n_out),
        proj_piece[:, :q_end],
        proj_piece[:, q_end:k_end],
        proj_piece[:, k_end:v_end],
        proj_piece[:, v_end:g_end],
        proj_piece[:, g_end : g_end + heads],
        proj_piece[:, g_end + heads : g_end + 2 * heads],
        grad_filters[..., :piece_q],
        grad_filters[..., piece_q : 2 * piece_q],
        grad_filters[..., 2 * piece_q :],
        sums[tail : tail + n_heads],
        sums[tail + n_heads : tail + 2 * n_heads],
        out_piece.T,
        gate_piece.astype(f32),
        up_piece.astype(f32),
        down_piece.astype(f32).T,
    )


def solution(mesh):
    rows = P(("dp", "tensor"), None)
    spread = P(("dp", "tensor"))
    weight = P("dp", "tensor")
    filters = P(None, "tensor", "dp")
    turned = P("tensor", "dp")
    return jax.shard_map(
        local,
        mesh=mesh,
        in_specs=(rows, P("dp"), rows, spread, spread, spread)
        + (weight,) * 6
        + (filters,) * 3
        + (P(), P(), turned, weight, weight, turned),
        out_specs=(rows, rows, spread, spread, spread)
        + (weight,) * 6
        + (filters,) * 3
        + (P(), P(), turned, weight, weight, turned),
        check_vma=False,
    )
```

time: 3000 us -> 1300 us (0.43)
  waiting for transfers between devices: 1860 us -> 847 us
  matrix products: 532 us -> 172 us
  other arithmetic: 251 us -> 43.1 us
  local copies, waits for them, and re-layouts: 147 us -> 32.9 us
  blocking collectives: 180 us -> 82.7 us
  Pallas kernels: 0 us -> 84.4 us
    reduce_scatter x12 -> x5, waiting for transfers between devices: 1390 us -> 459 us  [scatter_rows(): return lax.psum_scatter(values, 'dp', scatter_dimension=0, tiled=True)]
    dot_general x132 -> x15, matrix products: 503 us -> 172 us  [dot(): lax.dot_general(a, b, (((ca,), (cb,)), ((), ())), preferred_element_type=...]
    ppermute x0 -> x8, waiting for transfers between devices: none -> 163 us  [pair_swap(): return lax.ppermute(values, 'tensor', [(0, 1), (1, 0)])]
    all_gather x12 -> x5, waiting for transfers between devices: 359 us -> 225 us  [gather_rows(): return lax.all_gather(values, 'dp', axis=0, tiled=True)]
    unnamed x34 -> x10, waiting for transfers between devices: 118 us -> 0.16 us
    another operation x7 -> x8, other arithmetic: 121 us -> 3.47 us  [the longest x4 119 us: span_core(): lax.linalg.triangular_solve(lower_matrix, beta_blocks[..., None] * value_...]
    all_gather x5 -> x0, blocking collectives: 97.9 us -> none  [the longest x1 21 us: fetch_mixer(): lax.all_gather(masters[5].astype(jnp.bfloat16), 'dp', axis=0, tiled=True)]
    pallas_call x0 -> x2, Pallas kernels: none -> 84.4 us  [the longest x1 49.6 us: mixer_backward(): pl.pallas_call(functools.partial(bwd_kernel, heads), grid=(heads,), in_sp...]
  transfers between devices with their start and end apart: 29 -> 18, of which waited for: 20 -> 17; matrix products, arithmetic and copies ran while one was open for 18% -> 14% of each run, Pallas kernels for 0% -> 7%
where the time goes in v1:
time: 1300 us; the launch traced here: 1290 us
  waiting for transfers between devices  847 us (65%)
  matrix products  172 us (13%)
  Pallas kernels  84.4 us (6%)
  blocking collectives  82.7 us (6%)
  other arithmetic  43.1 us (3%)
  local copies, waits for them, and re-layouts  32.9 us (3%)
  between operations  16 us (1%)
    reduce_scatter x5, waiting for transfers between devices, scatter_rows(): return lax.psum_scatter(values, 'dp', scatter_dimension=0, tiled=True)  459 us
    all_gather x5, waiting for transfers between devices, gather_rows(): return lax.all_gather(values, 'dp', axis=0, tiled=True)  225 us
    dot_general x15, matrix products, dot(): lax.dot_general(a, b, (((ca,), (cb,)), ((), ())), preferred_element_type=...  172 us
    ppermute x8, waiting for transfers between devices, pair_swap(): return lax.ppermute(values, 'tensor', [(0, 1), (1, 0)])  163 us
    pallas_call x1, Pallas kernels, mixer_backward(): pl.pallas_call(functools.partial(bwd_kernel, heads), grid=(heads,), in_sp...  49.6 us
    unnamed x1, blocking collectives  43.3 us
    psum x1, blocking collectives, local(): sums = lax.psum(sums, ('dp', 'tensor'))  39.4 us
    pallas_call x1, Pallas kernels, mixer_forward(): pl.pallas_call(functools.partial(fwd_kernel, heads), grid=(heads,), in_sp...  34.9 us
  transfers between devices with their start and end apart: 18, of which 17 were waited for; matrix products, arithmetic and copies ran while one was open for 14% of the time, Pallas kernels for 7%

profile of v1, /device:TPU:0, one launch (start us, length us, event | category | flops | bytes accessed | tf_op | source)
XLA Modules:
  0.0 1289.0 jit_solution(14523456795335532337)
XLA Ops:
  21.6 43.3 %all-reduce.3 = f32[4608]{0:T(1024)S(1)} all-reduce(f32[4608]{0:T(1024)S(1)} %maximum_dynamic-update-slice_fusion), channel_id=2, replica_groups=mesh['dp'=16,'tensor'=2] {'dp','tensor'}, use_global_device_ids=true, to_apply=%add.3 | all-reduce | flops 4608 | bytes 36864
  69.1 21.8 %collective-permute-done = bf16[256,2048]{1,0:T(8,128)(2,1)} collective-permute-done((bf16[256,2048]{1,0:T(8,128)(2,1)S(1)}, bf16[256,2048]{1,0:T(8,128)(2,1)}, u32[]{:S(2)}, u32[]{:S(2)}) %collective-permute-start) | collective-permute-done | bytes 1048608 | tf_op jit(solution)/shard_map/ppermute | solution.py:533
  92.9 28.1 %all-gather.7.cloned.1.call-done = bf16[2048,4736]{1,0:T(8,128)(2,1)} async-done(((bf16[128,4736]{1,0:T(8,128)(2,1)}), bf16[2048,4736]{1,0:T(8,128)(2,1)}) %all-gather.7.cloned.1.call-update) | async-done | bytes 19398672 | tf_op jit(solution)/shard_map/all_gather | solution.py:557
  123.3 17.2 %fusion.13.q_ref.k_ref.v_ref.g_ref.bd_ref = f32[512,4736]{1,0:T(8,128)} fusion(bf16[2048,4736]{1,0:T(8,128)(2,1)} %all-gather.7.cloned.1.call-done, bf16[256,2048]{1,0:T(8,128)(2,1)S(1)} %get-tuple-element.101, bf16[256,2048]{1,0:T(8,128)(2,1)S(1)} %get-tuple-element.100), kind=kOutput, calls=%fused_computation.44 | convolution fusion | flops 9936306176 | bytes 31195136 | tf_op jit(solution)/shard_map/dot_general | solution.py:553
  140.6 34.9 %mixer_forward.1 = (bf16[512,1536]{1,0:T(8,128)(2,1)S(1)}, bf16[3,512,256]{2,1,0:T(8,128)(2,1)S(1)}, bf16[512,1536]{1,0:T(8,128)(2,1)S(1)}, f32[512,1536]{1,0:T(8,128)}, f32[3,1,256,512]{3,2,1,0:T(8,128)}) custom-call(s32[1]{0:T(128)S(6)} %copy.75.len_ref, f32[512,4736]{1,0:T(8,128)} %fusion.13.q_ref.k_ref.v_ref.g_ref.bd_ref, ...), custom_call_target="tpu_custom_call" | custom-call | tf_op jit(solution)/shard_map/mixer_forward/pallas_call | solution.py:437
  176.4 13.3 %all-gather.9.cloned.1.call-done = bf16[2048,1536]{0,1:T(8,128)(2,1)} async-done(((bf16[128,1536]{0,1:T(8,128)(2,1)}), bf16[2048,1536]{0,1:T(8,128)(2,1)}) %all-gather.9.cloned.1.call-update) | async-done | bytes 6291472 | tf_op jit(solution)/shard_map/all_gather | solution.py:557
  200.3 24.2 %collective-permute-done.1 = bf16[256,2048]{1,0:T(8,128)(2,1)} collective-permute-done((bf16[256,2048]{1,0:T(8,128)(2,1)}, bf16[256,2048]{1,0:T(8,128)(2,1)}, u32[]{:S(2)}, u32[]{:S(2)}) %collective-permute-start.1) | collective-permute-done | bytes 1048608 | tf_op jit(solution)/shard_map/ppermute | solution.py:533
  229.0 18.0 %collective-permute-done.4 = bf16[256,2048]{1,0:T(8,128)(2,1)} collective-permute-done((bf16[256,2048]{1,0:T(8,128)(2,1)}, bf16[256,2048]{1,0:T(8,128)(2,1)}, u32[]{:S(2)}, u32[]{:S(2)}) %collective-permute-start.4) | collective-permute-done | bytes 1048608 | tf_op jit(solution)/shard_map/ppermute | solution.py:533
  250.0 18.7 %collective-permute-done.2 = bf16[256,2048]{1,0:T(8,128)(2,1)S(1)} collective-permute-done((bf16[256,2048]{1,0:T(8,128)(2,1)S(1)}, bf16[256,2048]{1,0:T(8,128)(2,1)S(1)}, u32[]{:S(2)}, u32[]{:S(2)}) %collective-permute-start.2) | collective-permute-done | bytes 1048608 | tf_op jit(solution)/shard_map/ppermute | solution.py:533
  270.6 14.4 %all-gather.11.cloned.1.call-done = bf16[2048,2816]{1,0:T(8,128)(2,1)} async-done(((bf16[128,2816]{1,0:T(8,128)(2,1)}), bf16[2048,2816]{1,0:T(8,128)(2,1)}) %all-gather.11.cloned.1.call-update) | async-done | bytes 11534352 | tf_op jit(solution)/shard_map/all_gather | solution.py:557
  296.7 83.6 %all-gather.13.cloned.1.call-done = bf16[2048,2816]{1,0:T(8,128)(2,1)} async-done(((bf16[128,2816]{1,0:T(8,128)(2,1)}), bf16[2048,2816]{1,0:T(8,128)(2,1)}) %all-gather.13.cloned.1.call-update) | async-done | bytes 11534352 | tf_op jit(solution)/shard_map/all_gather | solution.py:557
  392.4 85.5 %all-gather.15.cloned.1.call-done = bf16[2048,2816]{0,1:T(8,128)(2,1)} async-done(((bf16[128,2816]{0,1:T(8,128)(2,1)}), bf16[2048,2816]{0,1:T(8,128)(2,1)}) %all-gather.15.cloned.1.call-update) | async-done | bytes 11534352 | tf_op jit(solution)/shard_map/all_gather | solution.py:557
  477.9 15.6 %multiply_convert_fusion = (bf16[512,2816]{1,0:T(8,128)(2,1)}, bf16[512,2816]{1,0:T(8,128)(2,1)}, bf16[512,2816]{1,0:T(8,128)(2,1)}) fusion(f32[512,2816]{1,0:T(8,128)} %fusion.21, f32[512,2816]{1,0:T(8,128)} %fusion.20, bf16[2048,2816]{0,1:T(8,128)(2,1)} %all-gather.15.cloned.1.call-done, bf16[256,2048]{1,0:T(8,128)(2,1)} %get-tuple-element.97, ...), kind=kOutput, calls=%fused_computation.5 | convolution fusion | flops 5931401216 | bytes 33816576 | tf_op jit(solution)/shard_map/dot_general | solution.py:553
  524.5 14.4 %collective-permute-done.5 = bf16[256,2048]{1,0:T(8,128)(2,1)S(1)} collective-permute-done((bf16[256,2048]{1,0:T(8,128)(2,1)S(1)}, bf16[256,2048]{1,0:T(8,128)(2,1)S(1)}, u32[]{:S(2)}, u32[]{:S(2)}) %collective-permute-start.5) | collective-permute-done | bytes 1048608 | tf_op jit(solution)/shard_map/ppermute | solution.py:533
  539.8 21.0 %collective-permute-done.3 = bf16[256,2048]{1,0:T(8,128)(2,1)S(1)} collective-permute-done((bf16[256,2048]{1,0:T(8,128)(2,1)S(1)}, bf16[256,2048]{1,0:T(8,128)(2,1)S(1)}, u32[]{:S(2)}, u32[]{:S(2)}) %collective-permute-start.3) | collective-permute-done | bytes 1048608 | tf_op jit(solution)/shard_map/ppermute | solution.py:533
  566.5 23.1 %collective-permute-done.6 = bf16[256,2048]{1,0:T(8,128)(2,1)S(1)} collective-permute-done((bf16[256,2048]{1,0:T(8,128)(2,1)S(1)}, bf16[256,2048]{1,0:T(8,128)(2,1)S(1)}, u32[]{:S(2)}, u32[]{:S(2)}) %collective-permute-start.6) | collective-permute-done | bytes 1048608 | tf_op jit(solution)/shard_map/ppermute | solution.py:533
  640.6 49.6 %mixer_backward.1 = (bf16[512,4736]{1,0:T(8,128)(2,1)}, f32[4,768]{1,0:T(4,128)S(1)}, f32[4,768]{1,0:T(4,128)S(1)}, f32[4,1536]{1,0:T(4,128)S(1)}, f32[8,512]{1,0:T(8,128)S(1)}, /*index=5*/f32[8,128]{1,0:T(8,128)S(1)}) custom-call(s32[1]{0:T(128)S(6)} %copy.75.len_ref, f32[512,4736]{1,0:T(8,128)} %fusion.13.q_ref.k_ref.v_ref.g_ref.bd_ref, ...), custom_call_target="tpu_custom_call" | custom-call | tf_op jit(solution)/shard_map/mixer_backward/pallas_call | solution.py:473
  691.2 18.2 %convolution_convert_fusion = bf16[2048,4736]{1,0:T(8,128)(2,1)} fusion(bf16[512,4736]{1,0:T(8,128)(2,1)} %get-tuple-element.36, bf16[256,2048]{1,0:T(8,128)(2,1)} %copy-done.27, bf16[256,2048]{1,0:T(8,128)(2,1)} %copy-done.26), kind=kOutput, calls=%fused_computation | convolution fusion | flops 9946005504 | bytes 26345472 | tf_op jit(solution)/shard_map/dot_general | solution.py:553
  715.3 16.2 %fusion.34 = f32[512,2048]{1,0:T(8,128)S(1)} fusion(bf16[512,4736]{1,0:T(8,128)(2,1)} %get-tuple-element.36, bf16[2048,4736]{1,0:T(8,128)(2,1)} %all-gather.7.cloned.1.call-done), kind=kOutput, calls=%fused_computation.94 | convolution fusion | flops 9932111872 | bytes 28442624 | tf_op jit(solution)/shard_map/dot_general | solution.py:553
  736.3 21.7 %collective-permute-done.7 = bf16[256,2048]{1,0:T(8,128)(2,1)} collective-permute-done((bf16[256,2048]{1,0:T(8,128)(2,1)}, bf16[256,2048]{1,0:T(8,128)(2,1)}, u32[]{:S(2)}, u32[]{:S(2)}) %collective-permute-start.7) | collective-permute-done | bytes 1048608 | tf_op jit(solution)/shard_map/ppermute | solution.py:533
  760.9 39.4 %psum.7 = f32[4620]{0:T(1024)S(1)} all-reduce(f32[4620]{0:T(1024)S(1)} %concatenate.41), channel_id=1, replica_groups=mesh['dp'=16,'tensor'=2] {'dp','tensor'}, use_global_device_ids=true, to_apply=%region_7.8 | all-reduce | flops 4620 | bytes 36960 | tf_op jit(solution)/shard_map/psum | solution.py:699
  813.5 127.5 %reduce-scatter.10.cloned.1.call-done = bf16[128,2816]{1,0:T(8,128)(2,1)} async-done(((bf16[2048,2816]{1,0:T(8,128)(2,1)}), bf16[128,2816]{1,0:T(8,128)(2,1)}) %reduce-scatter.10.cloned.1.call-update) | async-done | bytes 720912 | tf_op jit(solution)/shard_map/reduce_scatter | solution.py:561
  943.4 128.5 %reduce-scatter.12.cloned.1.call-done = bf16[128,2816]{1,0:T(8,128)(2,1)} async-done(((bf16[2048,2816]{1,0:T(8,128)(2,1)}), bf16[128,2816]{1,0:T(8,128)(2,1)}) %reduce-scatter.12.cloned.1.call-update) | async-done | bytes 720912 | tf_op jit(solution)/shard_map/reduce_scatter | solution.py:561
  1074.2 200.2 %reduce-scatter.6.cloned.1.call-done = bf16[128,4736]{1,0:T(8,128)(2,1)} async-done(((bf16[2048,4736]{1,0:T(8,128)(2,1)}), bf16[128,4736]{1,0:T(8,128)(2,1)}) %reduce-scatter.6.cloned.1.call-update) | async-done | bytes 1212432 | tf_op jit(solution)/shard_map/reduce_scatter | solution.py:561
  (234 shorter events, 194.5 us)
Async XLA Ops:
  7.2 113.8 %all-gather.7.cloned.1.call-start = ((), (), s32[]{:S(2)}) async-start(), calls=%async_computation.5 | async-start | bytes 20611072 | tf_op jit(solution)/shard_map/all_gather | solution.py:557
  15.5 174.1 %all-gather.9.cloned.1.call-start = ((), (), s32[]{:S(2)}) async-start(), calls=%async_computation.6 | async-start | bytes 6684672 | tf_op jit(solution)/shard_map/all_gather | solution.py:557
  16.4 268.7 %all-gather.11.cloned.1.call-start = ((), (), s32[]{:S(2)}) async-start(), calls=%async_computation.7 | async-start | bytes 12255232 | tf_op jit(solution)/shard_map/all_gather | solution.py:557
  18.8 361.5 %all-gather.13.cloned.1.call-start = ((), (), s32[]{:S(2)}) async-start(), calls=%async_computation.8 | async-start | bytes 12255232 | tf_op jit(solution)/shard_map/all_gather | solution.py:557
  19.8 458.1 %all-gather.15.cloned.1.call-start = ((), (), s32[]{:S(2)}) async-start(), calls=%async_computation.9 | async-start | bytes 12255232 | tf_op jit(solution)/shard_map/all_gather | solution.py:557
  21.4 784.7 %reduce-scatter.8.cloned.1.call-start = ((), (), s32[]{:S(2)}) async-start(), calls=%async_computation.11 | async-start | bytes 6684672 | tf_op jit(solution)/shard_map/reduce_scatter | solution.py:561
  65.8 25.1 %collective-permute-start = (bf16[256,2048]{1,0:T(8,128)(2,1)S(1)}, bf16[256,2048]{1,0:T(8,128)(2,1)}, u32[]{:S(2)}, u32[]{:S(2)}) collective-permute-start(bf16[256,2048]{1,0:T(8,128)(2,1)S(1)} %fusion.5), channel_id=1, source_target_pairs={{0,1},{1,0},{2,3},{3,2},{4,5},{5,4},{6,7},{7,6},{8,9},{9,8},{10,11... | collective-permute-start | bytes 3145736 | tf_op jit(solution)/shard_map/ppermute | solution.py:533
  69.0 71.5 %copy-start.9 = (f32[1,512]{1,0:T(1,128)}, f32[1,512]{1,0:T(1,128)S(1)}, u32[]{:S(2)}) copy-start(f32[1,512]{1,0:T(1,128)S(1)} %reshape.114.gain_ref) | copy-start | bytes 6148
  69.0 71.5 %copy-start.11 = (f32[1,128]{1,0:T(1,128)}, f32[1,128]{1,0:T(1,128)S(1)}, u32[]{:S(2)}) copy-start(f32[1,128]{1,0:T(1,128)S(1)} %get-tuple-element.118.bias_ref) | copy-start | bytes 1540
  69.0 71.5 %copy-start.13 = (f32[1,128]{1,0:T(1,128)}, f32[1,128]{1,0:T(1,128)S(1)}, u32[]{:S(2)}) copy-start(f32[1,128]{1,0:T(1,128)S(1)} %get-tuple-element.119.log_ref) | copy-start | bytes 1540
  92.9 47.7 %copy-start.26 = (bf16[256,2048]{1,0:T(8,128)(2,1)}, bf16[256,2048]{1,0:T(8,128)(2,1)S(1)}, u32[]{:S(2)}) copy-start(bf16[256,2048]{1,0:T(8,128)(2,1)S(1)} %get-tuple-element.100) | copy-start | bytes 3145732
  92.9 47.7 %copy-start.27 = (bf16[256,2048]{1,0:T(8,128)(2,1)}, bf16[256,2048]{1,0:T(8,128)(2,1)S(1)}, u32[]{:S(2)}) copy-start(bf16[256,2048]{1,0:T(8,128)(2,1)S(1)} %get-tuple-element.101) | copy-start | bytes 3145732
  198.2 26.3 %collective-permute-start.1 = (bf16[256,2048]{1,0:T(8,128)(2,1)}, bf16[256,2048]{1,0:T(8,128)(2,1)}, u32[]{:S(2)}, u32[]{:S(2)}) collective-permute-start(bf16[256,2048]{1,0:T(8,128)(2,1)} %dynamic-slice_convert_fusion.3), channel_id=1, source_target_pairs={{0,1},{1,0},{2,3},{3,2},{4,5},{5,4},{6,7},{7,6},{8,9},{9,8},{10,11... | collective-permute-start | bytes 3145736 | tf_op jit(solution)/shard_map/ppermute | solution.py:533
  199.7 47.3 %collective-permute-start.4 = (bf16[256,2048]{1,0:T(8,128)(2,1)}, bf16[256,2048]{1,0:T(8,128)(2,1)}, u32[]{:S(2)}, u32[]{:S(2)}) collective-permute-start(bf16[256,2048]{1,0:T(8,128)(2,1)} %param.23), channel_id=1, source_target_pairs={{0,1},{1,0},{2,3},{3,2},{4,5},{5,4},{6,7},{7,6},{8,9},{9,8},{10,11... | collective-permute-start | bytes 3145736 | tf_op jit(solution)/shard_map/ppermute | solution.py:533
  227.4 41.2 %collective-permute-start.2 = (bf16[256,2048]{1,0:T(8,128)(2,1)S(1)}, bf16[256,2048]{1,0:T(8,128)(2,1)S(1)}, u32[]{:S(2)}, u32[]{:S(2)}) collective-permute-start(bf16[256,2048]{1,0:T(8,128)(2,1)S(1)} %multiply_convert_fusion.3), channel_id=1, source_target_pairs={{0,1},{1,0},{2,3},{3,2},{4,5},{5,4},{6,7},{7,6},{8,9},{9,8},{10,11... | collective-permute-start | bytes 3145736 | tf_op jit(solution)/shard_map/ppermute | solution.py:533
  512.9 26.1 %collective-permute-start.5 = (bf16[256,2048]{1,0:T(8,128)(2,1)S(1)}, bf16[256,2048]{1,0:T(8,128)(2,1)S(1)}, u32[]{:S(2)}, u32[]{:S(2)}) collective-permute-start(bf16[256,2048]{1,0:T(8,128)(2,1)S(1)} %dynamic-slice_convert_fusion.1), channel_id=1, source_target_pairs={{0,1},{1,0},{2,3},{3,2},{4,5},{5,4},{6,7},{7,6},{8,9},{9,8},{10,11... | collective-permute-start | bytes 3145736 | tf_op jit(solution)/shard_map/ppermute | solution.py:533
  523.9 36.9 %collective-permute-start.3 = (bf16[256,2048]{1,0:T(8,128)(2,1)S(1)}, bf16[256,2048]{1,0:T(8,128)(2,1)S(1)}, u32[]{:S(2)}, u32[]{:S(2)}) collective-permute-start(bf16[256,2048]{1,0:T(8,128)(2,1)S(1)} %dynamic-slice_convert_fusion.2), channel_id=1, source_target_pairs={{0,1},{1,0},{2,3},{3,2},{4,5},{5,4},{6,7},{7,6},{8,9},{9,8},{10,11... | collective-permute-start | bytes 3145736 | tf_op jit(solution)/shard_map/ppermute | solution.py:533
  565.1 24.5 %collective-permute-start.6 = (bf16[256,2048]{1,0:T(8,128)(2,1)S(1)}, bf16[256,2048]{1,0:T(8,128)(2,1)S(1)}, u32[]{:S(2)}, u32[]{:S(2)}) collective-permute-start(bf16[256,2048]{1,0:T(8,128)(2,1)S(1)} %get-tuple-element.86), channel_id=1, source_target_pairs={{0,1},{1,0},{2,3},{3,2},{4,5},{5,4},{6,7},{7,6},{8,9},{9,8},{10,11... | collective-permute-start | bytes 3145736 | tf_op jit(solution)/shard_map/ppermute | solution.py:533
  596.5 214.3 %reduce-scatter.14.cloned.1.call-start = ((), (), s32[]{:S(2)}) async-start(), calls=%async_computation.14 | async-start | bytes 12255232 | tf_op jit(solution)/shard_map/reduce_scatter | solution.py:561
  608.7 332.4 %reduce-scatter.10.cloned.1.call-start = ((), (), s32[]{:S(2)}) async-start(), calls=%async_computation.12 | async-start | bytes 12255232 | tf_op jit(solution)/shard_map/reduce_scatter | solution.py:561
  621.2 450.7 %reduce-scatter.12.cloned.1.call-start = ((), (), s32[]{:S(2)}) async-start(), calls=%async_computation.13 | async-start | bytes 12255232 | tf_op jit(solution)/shard_map/reduce_scatter | solution.py:561
  632.3 642.1 %reduce-scatter.6.cloned.1.call-start = ((), (), s32[]{:S(2)}) async-start(), calls=%async_computation.10 | async-start | bytes 20611072 | tf_op jit(solution)/shard_map/reduce_scatter | solution.py:561
  734.6 23.4 %collective-permute-start.7 = (bf16[256,2048]{1,0:T(8,128)(2,1)}, bf16[256,2048]{1,0:T(8,128)(2,1)}, u32[]{:S(2)}, u32[]{:S(2)}) collective-permute-start(bf16[256,2048]{1,0:T(8,128)(2,1)} %dynamic-slice_convert_fusion), channel_id=1, source_target_pairs={{0,1},{1,0},{2,3},{3,2},{4,5},{5,4},{6,7},{7,6},{8,9},{9,8},{10,11... | collective-permute-start | bytes 3145736 | tf_op jit(solution)/shard_map/ppermute | solution.py:533
  736.3 65.8 %copy-start.20 = (f32[256,2048]{1,0:T(8,128)S(1)}, f32[256,2048]{1,0:T(8,128)}, u32[]{:S(2)}) copy-start(f32[256,2048]{1,0:T(8,128)} %get-tuple-element.87) | copy-start | bytes 6291460
  (39 other events, 499.0 us)
Sparse Core Ops, SparseCore 0:
  15.6 105.3 all-gather.6
  123.7 65.8 all-gather.8
  192.5 92.5 all-gather.10
  287.8 92.4 all-gather.12
  382.3 95.5 all-gather.14
  596.7 83.3 reduce-scatter.7
  684.7 126.0 reduce-scatter.13
  814.9 126.1 reduce-scatter.9
  945.8 126.0 reduce-scatter.11
  1075.8 198.4 reduce-scatter.5

commit v2 on v1

--- a/solution.py
+++ b/solution.py
@@ -512,6 +512,258 @@
     )(lens, pre, pre, pre, pre, pre, fq, fk, fv, logs, bias, gain, inv, u, mixed, states, dgated)
 
 
+MESH = pl.DeviceIdType.MESH
+
+
+def column_chunks(widths, size):
+    out = []
+    for a, width in enumerate(widths):
+        units = width // 128
+        count = max(1, -(-width // size))
+        lo = 0
+        for i in range(count):
+            hi = units * (i + 1) // count
+            out.append((a, lo * 128, (hi - lo) * 128))
+            lo = hi
+    return out
+
+
+def placement():
+    spot = lax.axis_index("dp")
+    return spot, lax.rem(spot, 2), lax.rem(lax.div(spot, 2), 2), lax.div(spot, 4)
+
+
+def greet(partners):
+    barrier = pltpu.get_barrier_semaphore()
+    for partner in partners:
+        pl.semaphore_signal(barrier, inc=1, device_id={"dp": partner}, device_id_type=MESH)
+    pl.semaphore_wait(barrier, len(partners))
+
+
+def remote(src, dst, send, recv, target):
+    return pltpu.make_async_remote_copy(
+        src_ref=src, dst_ref=dst, send_sem=send, recv_sem=recv,
+        device_id={"dp": target}, device_id_type=MESH,
+    )
+
+
+def gather_kernel(layers, chunks, count, *refs):
+    srcs, outs = refs[:count], refs[count : 2 * count]
+    own_sem, zs, zr, ys, yr, cs, cr = refs[2 * count :]
+    rows = srcs[0].shape[0]
+    spot, core, side, layer = placement()
+    at = lambda z, y, c: 4 * lax.rem(z + layers, layers) + 2 * y + c
+    z_to = [at(layer + k, side, core) for k in range(1, layers)]
+    y_to, c_to = at(layer, 1 - side, core), at(layer, side, 1 - core)
+    greet(z_to + [y_to, c_to])
+
+    def place(j, origin):
+        a, lo, width = chunks[j]
+        start = pl.multiple_of(origin * rows, rows)
+        return outs[a].at[pl.ds(start, rows), lo : lo + width]
+
+    def own(j):
+        a, lo, width = chunks[j]
+        return srcs[a].at[:, lo : lo + width]
+
+    def z_copy(j, k, origin, src):
+        return remote(src, place(j, origin), zs.at[j, k - 1], zr.at[j, k - 1], z_to[k - 1])
+
+    def y_copy(j, m, origin, src):
+        return remote(src, place(j, origin), ys.at[j, m], yr.at[j, m], y_to)
+
+    def c_copy(j, m, half, origin, src):
+        i = 2 * m + half
+        return remote(src, place(j, origin), cs.at[j, i], cr.at[j, i], c_to)
+
+    keep = []
+    number = len(chunks)
+    for j in range(number):
+        for k in range(1, layers):
+            z_copy(j, k, spot, own(j)).start()
+        y_copy(j, 0, spot, own(j)).start()
+        c_copy(j, 0, 0, spot, own(j)).start()
+        copy = pltpu.make_async_copy(own(j), place(j, spot), own_sem.at[j])
+        copy.start()
+        keep.append(copy)
+
+    def second(j):
+        for k in range(1, layers):
+            origin = at(layer - k, side, core)
+            here = place(j, origin)
+            z_copy(j, k, origin, here).wait_recv()
+            y_copy(j, k, origin, here).start()
+            c_copy(j, k, 0, origin, here).start()
+
+    def third(j):
+        for m in range(layers):
+            origin = at(layer - m, 1 - side, core)
+            here = place(j, origin)
+            y_copy(j, m, origin, here).wait_recv()
+            c_copy(j, m, 1, origin, here).start()
+
+    for j in range(number + 1):
+        if j < number:
+            second(j)
+        if j >= 1:
+            third(j - 1)
+    for j in range(number):
+        keep[j].wait()
+        for k in range(1, layers):
+            z_copy(j, k, spot, own(j)).wait_send()
+        for m in range(layers):
+            y_copy(j, m, spot, own(j)).wait_send()
+            for half in range(2):
+                origin = at(layer - m, lax.rem(side + half, 2), 1 - core)
+                c_copy(j, m, half, origin, place(j, origin)).wait()
+
+
+def gather_all(shards, devices, ident, size=512):
+    rows = shards[0].shape[0]
+    layers = devices // 4
+    chunks = column_chunks([s.shape[1] for s in shards], size)
+    n = len(chunks)
+    sem = lambda *shape: pltpu.SemaphoreType.DMA(shape)
+    return pl.pallas_call(
+        functools.partial(gather_kernel, layers, chunks, len(shards)),
+        in_specs=[pl.BlockSpec(memory_space=pl.ANY)] * len(shards),
+        out_specs=[pl.BlockSpec(memory_space=pl.ANY)] * len(shards),
+        out_shape=[jax.ShapeDtypeStruct((devices * rows, s.shape[1]), s.dtype) for s in shards],
+        scratch_shapes=[
+            sem(n), sem(n, layers - 1), sem(n, layers - 1), sem(n, layers), sem(n, layers),
+            sem(n, 2 * layers), sem(n, 2 * layers),
+        ],
+        compiler_params=pltpu.CompilerParams(collective_id=ident, has_side_effects=True),
+        name="gather_rows",
+    )(*shards)
+
+
+def scatter_kernel(layers, chunks, count, *refs):
+    srcs, out = refs[:count], refs[count]
+    stage, buf1, buf2, buf3, own_sem, cs, cr, ys, yr, zs, zr = refs[count + 1 :]
+    rows = out.shape[0]
+    spot, core, side, layer = placement()
+    at = lambda z, y, c: 4 * lax.rem(z + layers, layers) + 2 * y + c
+    z_to = [at(layer + k, side, core) for k in range(1, layers)]
+    y_to, c_to = at(layer, 1 - side, core), at(layer, side, 1 - core)
+    greet(z_to + [y_to, c_to])
+    number = len(chunks)
+    firsts = []
+    total = 0
+    for a, lo, width in chunks:
+        firsts.append(total)
+        total += width
+
+    def cols(j):
+        return slice(firsts[j], firsts[j] + chunks[j][2])
+
+    def c_copy(j):
+        a, lo, width = chunks[j]
+        return remote(
+            srcs[a].at[:, 1 - core, :, lo : lo + width], buf1.at[:, :, cols(j)],
+            cs.at[j], cr.at[j], c_to,
+        )
+
+    def own_copy(j):
+        a, lo, width = chunks[j]
+        return pltpu.make_async_copy(
+            srcs[a].at[:, core, :, lo : lo + width],
+            stage.at[j % 2, :, :, 0:width], own_sem.at[j],
+        )
+
+    def y_copy(j, m):
+        block = 2 * lax.rem(layer + m, layers) + 1 - side
+        return remote(
+            buf1.at[block, :, cols(j)], buf2.at[m, :, cols(j)], ys.at[j, m], yr.at[j, m], y_to
+        )
+
+    def z_copy(j, k):
+        return remote(
+            buf2.at[k, :, cols(j)], buf3.at[k - 1, :, cols(j)], zs.at[j, k - 1], zr.at[j, k - 1],
+            z_to[k - 1],
+        )
+
+    for j in range(number):
+        c_copy(j).start()
+    for j in range(min(2, number)):
+        own_copy(j).start()
+
+    def first(j):
+        width = chunks[j][2]
+        own_copy(j).wait()
+        c_copy(j).wait_recv()
+
+        def body(b, _):
+            mine = stage[j % 2, b, :, 0:width].astype(f32)
+            buf1[b, :, cols(j)] = (buf1[b, :, cols(j)].astype(f32) + mine).astype(bf16)
+            return 0
+
+        lax.fori_loop(0, 2 * layers, body, 0)
+        for m in list(range(1, layers)) + [0]:
+            y_copy(j, m).start()
+        if j + 2 < number:
+            own_copy(j + 2).start()
+
+    def second(j):
+        for m in list(range(1, layers)) + [0]:
+            y_copy(j, m).wait_recv()
+            block = 2 * lax.rem(layer + m, layers) + side
+            mine = buf1[block, :, cols(j)].astype(f32)
+            buf2[m, :, cols(j)] = (buf2[m, :, cols(j)].astype(f32) + mine).astype(bf16)
+            if m:
+                z_copy(j, m).start()
+
+    def third(j):
+        total = buf2[0, :, cols(j)].astype(f32)
+        for k in range(1, layers):
+            z_copy(j, k).wait_recv()
+            total = total + buf3[k - 1, :, cols(j)].astype(f32)
+        out[:, cols(j)] = total
+
+    for j in range(number + 4):
+        if j < number:
+            first(j)
+        if 0 <= j - 2 < number:
+            second(j - 2)
+        if 0 <= j - 4 < number:
+            third(j - 4)
+    for j in range(number):
+        c_copy(j).wait_send()
+        for m in range(layers):
+            y_copy(j, m).wait_send()
+        for k in range(1, layers):
+            z_copy(j, k).wait_send()
+
+
+def scatter_sum(parts, widths, devices, ident, size=512):
+    widths = [w or p.shape[1] for w, p in zip(widths, parts)]
+    rows = parts[0].shape[0] // devices
+    layers = devices // 4
+    chunks = column_chunks(widths, size)
+    n = len(chunks)
+    width = sum(widths)
+    widest = max(c[2] for c in chunks)
+    sem = lambda *shape: pltpu.SemaphoreType.DMA(shape)
+    return pl.pallas_call(
+        functools.partial(scatter_kernel, layers, chunks, len(parts)),
+        in_specs=[pl.BlockSpec(memory_space=pl.ANY)] * len(parts),
+        out_specs=pl.BlockSpec(memory_space=pltpu.VMEM),
+        out_shape=jax.ShapeDtypeStruct((rows, width), f32),
+        scratch_shapes=[
+            pltpu.VMEM((2, 2 * layers, rows, widest), bf16),
+            pltpu.VMEM((2 * layers, rows, width), bf16),
+            pltpu.VMEM((layers, rows, width), bf16),
+            pltpu.VMEM((layers - 1, rows, width), bf16),
+            sem(n), sem(n), sem(n), sem(n, layers), sem(n, layers),
+            sem(n, layers - 1), sem(n, layers - 1),
+        ],
+        compiler_params=pltpu.CompilerParams(
+            collective_id=ident, has_side_effects=True, vmem_limit_bytes=52 * 1024 * 1024
+        ),
+        name="scatter_sum",
+    )(*[p.reshape(devices // 2, 2, rows, p.shape[1]) for p in parts])
+
+
 EXTRA = 128
 
 
@@ -551,6 +803,11 @@
 
 def dot(a, b, ca=1, cb=0):
     return lax.dot_general(a, b, (((ca,), (cb,)), ((), ())), preferred_element_type=f32)
+
+
+def high_low(values):
+    high = lax.reduce_precision(values, 8, 7)
+    return jnp.stack([high, values - high], axis=1).astype(bf16)
 
 
 def gather_rows(values):
@@ -595,26 +852,38 @@
     low = lambda v: v.astype(bf16)
     filters = pack_filters(conv_query, conv_key, conv_value, rows)
     filter_cols = filters.shape[1]
-    small = jnp.concatenate([w_beta, w_decay, filters], axis=1)
+    gains = pair_gather(jnp.concatenate([gain_in, gain_ffn, gain_out])[None])
+    n_in, n_out = gain_in.shape[0], gain_out.shape[0]
+    pair_out = jnp.pad(gains[:, 2 * n_in :].reshape(-1), (0, rows - 2 * n_out))
+    small = jnp.concatenate(
+        [
+            low(jnp.concatenate([w_beta, w_decay, filters], axis=1)),
+            high_low(gains[:, :n_in].reshape(-1)),
+            high_low(gains[:, n_in : 2 * n_in].reshape(-1)),
+            high_low(pair_out),
+        ],
+        axis=1,
+    )
     small = jnp.pad(small, ((0, 0), (0, EXTRA - small.shape[1])))
     proj_shard = jnp.concatenate(
-        [low(w_query), low(w_key), low(w_value), low(w_gate), low(small)], axis=1
-    )
-    proj = gather_rows(proj_shard)
-    out_t = gather_rows(low(w_output).T)
-    gains = jnp.concatenate([gain_in, gain_ffn, gain_out])
-    gains = lax.all_gather(gains, ("dp", "tensor"), axis=0, tiled=False)
-    n_in, n_out = gain_in.shape[0], gain_out.shape[0]
-    full_in = gains[:, :n_in].reshape(-1)
-    full_ffn = gains[:, n_in : 2 * n_in].reshape(-1)
-    full_out = gains[:, 2 * n_in :].reshape(1, -1)
+        [low(w_query), low(w_key), low(w_value), low(w_gate), small], axis=1
+    )
+    seq_x = pair_gather(tokens)
+    seq_cot = pair_gather(cotangent)
+    proj, out_t = gather_all((proj_shard, low(w_output).T), devices, 0)
+    extra_at = 12 * heads * 128
+    gain_at = extra_at + 2 * heads + filter_cols
+    sides = proj[:, gain_at : gain_at + 6].astype(f32)
+    sides = sides[:, 0::2] + sides[:, 1::2]
+    full_in, full_ffn = sides[:, 0], sides[:, 1]
+    full_out = sides[:, 2].reshape(devices, rows)[:, : 2 * n_out].reshape(1, -1)
     gate_weight = gather_rows(low(w_ffn_gate))
     up_weight = gather_rows(low(w_ffn_up))
     down_t = gather_rows(low(w_ffn_down).T)
 
     tap_count = conv_query.shape[0]
     piece_q, piece_v = conv_query.shape[2], conv_value.shape[2]
-    flat = proj[:, 12 * heads * 128 + 2 * heads : 12 * heads * 128 + 2 * heads + filter_cols]
+    flat = proj[:, extra_at + 2 * heads : gain_at]
     flat = flat.reshape(devices, rows, filter_cols).transpose(0, 2, 1)
     flat = flat.reshape(devices, tap_count, heads, 2 * piece_q + piece_v).astype(f32)
     flat = flat.transpose(1, 2, 0, 3)
@@ -629,9 +898,9 @@
     local_log, local_bias = lane_pad(decay_log), lane_pad(decay_bias)
 
     inputs = tokens.astype(f32)
-    normed_in = low(inputs * rms_scale(inputs) * full_in)
-    seq_in = pair_gather(normed_in)
-    seq_cot = pair_gather(cotangent)
+    seq_inputs = seq_x.astype(f32)
+    seq_unit = seq_inputs * rms_scale(seq_inputs)
+    seq_in = low(seq_unit * full_in)
     pre = dot(seq_in, proj)
     mixer_args = (heads, lengths, pre, filt_q, filt_k, filt_v, local_log, local_bias, full_out)
     gated, *saved = mixer_forward(*mixer_args)
@@ -678,53 +947,58 @@
     ).transpose(2, 0, 1, 3)
     grad_flat = grad_flat.reshape(devices, filter_cols, rows).transpose(0, 2, 1)
     grad_flat = low(grad_flat.reshape(devices * rows, filter_cols))
-    grad_proj = lax.dynamic_update_slice(grad_proj, grad_flat, (0, 12 * heads * 128 + 2 * heads))
+    spread = lambda v: lax.dynamic_update_slice(jnp.zeros_like(decay_log), v, (head_start,))
+    grad_decay = jnp.concatenate([spread(grad_small[0, :heads]), spread(grad_small[1, :heads])])
+    by_rows = lambda v: jnp.pad(v, ((0, 0), (0, rows - v.shape[1]))).reshape(-1)
+    columns = jnp.stack(
+        [
+            jnp.sum(grad_seq_in * seq_unit, axis=0),
+            grad_gain_ffn,
+            by_rows(jnp.sum(grad_gain_out, axis=0).reshape(devices, -1)),
+            by_rows(jnp.broadcast_to(grad_decay, (devices,) + grad_decay.shape)),
+        ],
+        axis=1,
+    )
+    grad_tiny = jnp.concatenate(
+        [grad_proj[:, extra_at : extra_at + 2 * heads], grad_flat, low(columns)], axis=1
+    )
+    grad_tiny = jnp.pad(grad_tiny, ((0, 0), (0, EXTRA - grad_tiny.shape[1])))
+    pieces = scatter_sum((grad_proj, grad_out_t, grad_tiny), (extra_at, None, None), devices, 1)
     grad_normed_in = pair_scatter(grad_seq_in)
-    out_piece = scatter_rows(grad_out_t).astype(f32)
-    proj_piece = scatter_rows(grad_proj).astype(f32)
-
-    grad_inputs_norm, grad_gain_in = norm_back(inputs, full_in, grad_normed_in)
+    out_width = w_output.shape[0]
+    out_piece = pieces[:, extra_at : extra_at + out_width]
+    tiny_piece = pieces[:, extra_at + out_width :]
+
+    grad_inputs_norm, _ = norm_back(inputs, full_in, grad_normed_in)
     grad_tokens = grad_hidden + grad_inputs_norm
 
-    spread = lambda v: lax.dynamic_update_slice(jnp.zeros_like(decay_log), v, (head_start,))
-    sums = jnp.concatenate(
-        [
-            grad_gain_in,
-            grad_gain_ffn,
-            jnp.sum(grad_gain_out, axis=0),
-            spread(grad_small[0, :heads]),
-            spread(grad_small[1, :heads]),
-        ]
-    )
-    sums = lax.psum(sums, ("dp", "tensor"))
-    shard_index = lax.axis_index("dp") * lax.axis_size("tensor") + lax.axis_index("tensor")
-    width = full_in.shape[0]
-    out_width = full_out.shape[1]
-    take = lambda first, piece: lax.dynamic_slice_in_dim(sums, first + shard_index * piece, piece)
+    sums = tiny_piece[:, 2 * heads + filter_cols : 2 * heads + filter_cols + 4].T
+    sums = sums + pair_swap(sums)
+    turn = lax.axis_index("tensor")
+    take = lambda row, piece: lax.dynamic_slice_in_dim(sums[row], turn * piece, piece)
     n_heads = decay_log.shape[0]
-    tail = 2 * width + out_width
 
     q_end, k_end = heads * 256, 2 * heads * 256
     v_end, g_end = k_end + heads * 512, k_end + 2 * heads * 512
-    grad_filters = proj_piece[:, g_end + 2 * heads : g_end + 2 * heads + filter_cols]
+    grad_filters = tiny_piece[:, 2 * heads : 2 * heads + filter_cols]
     grad_filters = grad_filters.T.reshape(tap_count, heads, 2 * piece_q + piece_v)
     return (
         result,
         grad_tokens,
         take(0, n_in),
-        take(width, n_in),
-        take(2 * width, n_out),
-        proj_piece[:, :q_end],
-        proj_piece[:, q_end:k_end],
-        proj_piece[:, k_end:v_end],
-        proj_piece[:, v_end:g_end],
-        proj_piece[:, g_end : g_end + heads],
-        proj_piece[:, g_end + heads : g_end + 2 * heads],
+        take(1, n_in),
+        take(2, n_out),
+        pieces[:, :q_end],
+        pieces[:, q_end:k_end],
+        pieces[:, k_end:v_end],
+        pieces[:, v_end:g_end],
+        tiny_piece[:, :heads],
+        tiny_piece[:, heads : 2 * heads],
         grad_filters[..., :piece_q],
         grad_filters[..., piece_q : 2 * piece_q],
         grad_filters[..., 2 * piece_q :],
-        sums[tail : tail + n_heads],
-        sums[tail + n_heads : tail + 2 * n_heads],
+        sums[3, :n_heads],
+        sums[3, n_heads : 2 * n_heads],
         out_piece.T,
         gate_piece.astype(f32),
         up_piece.astype(f32),

time: 1300 us -> 989 us (0.76)
  waiting for transfers between devices: 847 us -> 121 us
  Pallas kernels: 84.4 us -> 570 us
  blocking collectives: 82.7 us -> 0 us
    pallas_call x0 -> x2, Pallas kernels: none -> 486 us  [the longest x1 248 us: gather_all(): pl.pallas_call(functools.partial(gather_kernel, layers, chunks, len(shard...]
    reduce_scatter x5 -> x3, waiting for transfers between devices: 459 us -> 0.01 us  [scatter_rows(): return lax.psum_scatter(values, 'dp', scatter_dimension=0, tiled=True)]
    all_gather x5 -> x3, waiting for transfers between devices: 225 us -> 0.01 us  [gather_rows(): return lax.all_gather(values, 'dp', axis=0, tiled=True)]
    unnamed x1 -> x0, blocking collectives: 43.3 us -> none
    ppermute x8 -> x10, waiting for transfers between devices: 163 us -> 121 us  [pair_swap(): return lax.ppermute(values, 'tensor', [(0, 1), (1, 0)])]
    psum x1 -> x0, blocking collectives: 39.4 us -> none  [local(): sums = lax.psum(sums, ('dp', 'tensor'))]
  transfers between devices with their start and end apart: 18 -> 16, of which waited for: 17 -> 6; matrix products, arithmetic and copies ran while one was open for 14% -> 23% of each run, Pallas kernels for 7% -> 58%
where the time goes in v2:
time: 989 us; the launch traced here: 979 us
  Pallas kernels  570 us (58%)
  matrix products  179 us (18%)
  waiting for transfers between devices  121 us (12%)
  local copies, waits for them, and re-layouts  41.5 us (4%)
  other arithmetic  40.6 us (4%)
  between operations  16.1 us (2%)
  starting transfers between devices  11.9 us (1%)
    pallas_call x1, Pallas kernels, gather_all(): pl.pallas_call(functools.partial(gather_kernel, layers, chunks, len(shard...  248 us
    pallas_call x1, Pallas kernels, scatter_sum(): pl.pallas_call(functools.partial(scatter_kernel, layers, chunks, len(part...  238 us
    dot_general x15, matrix products, dot(): lax.dot_general(a, b, (((ca,), (cb,)), ((), ())), preferred_element_type=...  179 us
    ppermute x10, waiting for transfers between devices, pair_swap(): return lax.ppermute(values, 'tensor', [(0, 1), (1, 0)])  121 us
    pallas_call x1, Pallas kernels, mixer_backward(): pl.pallas_call(functools.partial(bwd_kernel, heads), grid=(heads,), in_sp...  49.5 us
    pallas_call x1, Pallas kernels, mixer_forward(): pl.pallas_call(functools.partial(fwd_kernel, heads), grid=(heads,), in_sp...  34.8 us
  transfers between devices with their start and end apart: 16, of which 6 were waited for; matrix products, arithmetic and copies ran while one was open for 23% of the time, Pallas kernels for 58%

profile of v2, /device:TPU:0, one launch (start us, length us, event | category | flops | bytes accessed | tf_op | source)
XLA Modules:
  0.0 979.5 jit_solution(9040583430263391908)
XLA Ops:
  23.7 247.6 %gather_rows.1 = (bf16[2048,4736]{1,0:T(8,128)(2,1)}, bf16[2048,1536]{1,0:T(8,128)(2,1)}) custom-call(bf16[128,4736]{1,0:T(8,128)(2,1)} %copy-done.20, bf16[128,1536]{1,0:T(8,128)(2,1)} %bitcast.89), custom_call_target="tpu_custom_call" | custom-call | tf_op jit(solution)/shard_map/gather_rows/pallas_call | solution.py:627
  286.7 17.4 %fusion.31.q_ref.k_ref.v_ref.g_ref.bd_ref = f32[512,4736]{1,0:T(8,128)} fusion(bf16[2048,4736]{1,0:T(8,128)(2,1)} %get-tuple-element.33, f32[2048]{0:T(1024)S(1)} %get-tuple-element.110, f32[512]{0:T(512)S(1)} %add_rsqrt_fusion, bf16[256,2048]{1,0:T(8,128)(2,1)S(1)} %get-tuple-element.137, bf16[256,2048]{1,0:T(8,128)(2,1)S(1)} %get-tuple-element.136), kind=kOutput, calls=%fused_computation.121 | convolution fusion | flops 9939451904 | bytes 31205376 | tf_op jit(solution)/shard_map/dot_general | solution.py:805
  304.2 34.8 %mixer_forward.1 = (bf16[512,1536]{1,0:T(8,128)(2,1)S(1)}, bf16[3,512,256]{2,1,0:T(8,128)(2,1)S(1)}, bf16[512,1536]{1,0:T(8,128)(2,1)S(1)}, f32[512,1536]{1,0:T(8,128)}, f32[3,1,256,512]{3,2,1,0:T(8,128)}) custom-call(s32[1]{0:T(128)S(6)} %copy.119.len_ref, f32[512,4736]{1,0:T(8,128)} %fusion.31.q_ref.k_ref.v_ref.g_ref.bd_ref, ...), custom_call_target="tpu_custom_call" | custom-call | tf_op jit(solution)/shard_map/mixer_forward/pallas_call | solution.py:437
  349.6 24.2 %collective-permute-done.2 = bf16[256,2048]{1,0:T(8,128)(2,1)} collective-permute-done((bf16[256,2048]{1,0:T(8,128)(2,1)}, bf16[256,2048]{1,0:T(8,128)(2,1)}, u32[]{:S(2)}, u32[]{:S(2)}) %collective-permute-start.2) | collective-permute-done | bytes 1048608 | tf_op jit(solution)/shard_map/ppermute | solution.py:785
  378.2 18.1 %collective-permute-done.5 = bf16[256,2048]{1,0:T(8,128)(2,1)} collective-permute-done((bf16[256,2048]{1,0:T(8,128)(2,1)}, bf16[256,2048]{1,0:T(8,128)(2,1)}, u32[]{:S(2)}, u32[]{:S(2)}) %collective-permute-start.5) | collective-permute-done | bytes 1048608 | tf_op jit(solution)/shard_map/ppermute | solution.py:785
  399.0 19.3 %collective-permute-done.3 = bf16[256,2048]{1,0:T(8,128)(2,1)S(1)} collective-permute-done((bf16[256,2048]{1,0:T(8,128)(2,1)S(1)}, bf16[256,2048]{1,0:T(8,128)(2,1)S(1)}, u32[]{:S(2)}, u32[]{:S(2)}) %collective-permute-start.3) | collective-permute-done | bytes 1048608 | tf_op jit(solution)/shard_map/ppermute | solution.py:785
  420.2 11.9 %fusion.29 = f32[512,2816]{1,0:T(8,128)} fusion(bf16[2048,2816]{1,0:T(8,128)(2,1)} %all-gather.4.cloned.1.call-done, bf16[256,2048]{1,0:T(8,128)(2,1)} %get-tuple-element.135, bf16[256,2048]{1,0:T(8,128)(2,1)} %get-tuple-element.134), kind=kOutput, calls=%fused_computation.120 | convolution fusion | flops 5909774336 | bytes 19398656 | tf_op jit(solution)/shard_map/dot_general | solution.py:805
  432.1 11.9 %fusion.28 = f32[512,2816]{1,0:T(8,128)} fusion(bf16[2048,2816]{1,0:T(8,128)(2,1)} %all-gather.6.cloned.1.call-done, bf16[256,2048]{1,0:T(8,128)(2,1)} %get-tuple-element.135, bf16[256,2048]{1,0:T(8,128)(2,1)} %get-tuple-element.134), kind=kOutput, calls=%fused_computation.119 | convolution fusion | flops 5909774336 | bytes 19398656 | tf_op jit(solution)/shard_map/dot_general | solution.py:805
  444.0 15.5 %multiply_convert_fusion = (bf16[512,2816]{1,0:T(8,128)(2,1)}, bf16[512,2816]{1,0:T(8,128)(2,1)}, bf16[512,2816]{1,0:T(8,128)(2,1)}) fusion(f32[512,2816]{1,0:T(8,128)} %fusion.29, f32[512,2816]{1,0:T(8,128)} %fusion.28, bf16[2048,2816]{0,1:T(8,128)(2,1)} %all-gather.8.cloned.1.call-done, bf16[256,2048]{1,0:T(8,128)(2,1)} %get-tuple-element.133, ...), kind=kOutput, calls=%fused_computation.5 | convolution fusion | flops 5931401216 | bytes 33816576 | tf_op jit(solution)/shard_map/dot_general | solution.py:805
  459.5 10.8 %convolution_convert_fusion.1 = bf16[2048,2816]{1,0:T(8,128)(2,1)} fusion(bf16[512,2816]{1,0:T(8,128)(2,1)} %get-tuple-element.121, bf16[256,2048]{1,0:T(8,128)(2,1)S(1)} %copy-done.25, bf16[256,2048]{1,0:T(8,128)(2,1)S(1)} %get-tuple-element.132), kind=kOutput, calls=%fused_computation.1 | convolution fusion | flops 5915541504 | bytes 16515072 | tf_op jit(solution)/shard_map/dot_general | solution.py:805
  471.5 11.4 %convolution_convert_fusion.3 = bf16[2048,2816]{1,0:T(8,128)(2,1)} fusion(bf16[512,2816]{1,0:T(8,128)(2,1)} %get-tuple-element.120, bf16[256,2048]{1,0:T(8,128)(2,1)} %get-tuple-element.135, bf16[256,2048]{1,0:T(8,128)(2,1)S(1)} %copy-done.26), kind=kOutput, calls=%fused_computation.3 | convolution fusion | flops 5915541504 | bytes 16515072 | tf_op jit(solution)/shard_map/dot_general | solution.py:805
  483.0 11.8 %convolution_convert_fusion.2 = bf16[2048,2816]{1,0:T(8,128)(2,1)} fusion(bf16[512,2816]{1,0:T(8,128)(2,1)} %get-tuple-element.119, bf16[256,2048]{1,0:T(8,128)(2,1)} %get-tuple-element.135, bf16[256,2048]{1,0:T(8,128)(2,1)S(1)} %copy-done.26), kind=kOutput, calls=%fused_computation.2 | convolution fusion | flops 5915541504 | bytes 16515072 | tf_op jit(solution)/shard_map/dot_general | solution.py:805
  494.8 12.7 %fusion.42 = f32[512,2048]{1,0:T(8,128)} fusion(bf16[512,2816]{1,0:T(8,128)(2,1)} %get-tuple-element.120, bf16[2048,2816]{1,0:T(8,128)(2,1)} %all-gather.4.cloned.1.call-done), kind=kOutput, calls=%fused_computation.131 | convolution fusion | flops 5905580032 | bytes 18612224 | tf_op jit(solution)/shard_map/dot_general | solution.py:805
  507.5 11.8 %convolution_add_fusion = f32[512,2048]{1,0:T(8,128)S(1)} fusion(f32[512,2048]{1,0:T(8,128)} %fusion.42, bf16[512,2816]{1,0:T(8,128)(2,1)} %get-tuple-element.119, bf16[2048,2816]{1,0:T(8,128)(2,1)} %all-gather.6.cloned.1.call-done), kind=kOutput, calls=%fused_computation.20 | convolution fusion | flops 5906628608 | bytes 22806528 | tf_op jit(solution)/shard_map/dot_general | solution.py:805
  520.8 8.1 fusion.41
  529.9 15.7 %collective-permute-done.6 = bf16[256,2048]{1,0:T(8,128)(2,1)S(1)} collective-permute-done((bf16[256,2048]{1,0:T(8,128)(2,1)S(1)}, bf16[256,2048]{1,0:T(8,128)(2,1)S(1)}, u32[]{:S(2)}, u32[]{:S(2)}) %collective-permute-start.6) | collective-permute-done | bytes 1048608 | tf_op jit(solution)/shard_map/ppermute | solution.py:785
  546.4 20.3 %collective-permute-done.4 = bf16[256,2048]{1,0:T(8,128)(2,1)S(1)} collective-permute-done((bf16[256,2048]{1,0:T(8,128)(2,1)S(1)}, bf16[256,2048]{1,0:T(8,128)(2,1)S(1)}, u32[]{:S(2)}, u32[]{:S(2)}) %collective-permute-start.4) | collective-permute-done | bytes 1048608 | tf_op jit(solution)/shard_map/ppermute | solution.py:785
  572.3 22.8 %collective-permute-done.7 = bf16[256,2048]{1,0:T(8,128)(2,1)} collective-permute-done((bf16[256,2048]{1,0:T(8,128)(2,1)S(1)}, bf16[256,2048]{1,0:T(8,128)(2,1)}, u32[]{:S(2)}, u32[]{:S(2)}) %collective-permute-start.7) | collective-permute-done | bytes 1048608 | tf_op jit(solution)/shard_map/ppermute | solution.py:785
  596.5 8.8 convolution_convert_fusion.5.dg_ref
  605.4 49.5 %mixer_backward.1 = (bf16[512,4736]{1,0:T(8,128)(2,1)}, f32[4,768]{1,0:T(4,128)S(1)}, f32[4,768]{1,0:T(4,128)S(1)}, f32[4,1536]{1,0:T(4,128)S(1)}, f32[8,512]{1,0:T(8,128)S(1)}, /*index=5*/f32[8,128]{1,0:T(8,128)S(1)}) custom-call(s32[1]{0:T(128)S(6)} %copy.119.len_ref, f32[512,4736]{1,0:T(8,128)} %fusion.31.q_ref.k_ref.v_ref.g_ref.bd_ref, ...), custom_call_target="tpu_custom_call" | custom-call | tf_op jit(solution)/shard_map/mixer_backward/pallas_call | solution.py:473
  655.0 17.6 %fusion.4 = (bf16[2048]{0:T(1024)(128)(2,1)S(1)}, f32[512,2048]{1,0:T(8,128)}) fusion(f32[512]{0:T(512)S(1)} %copy-done.37, bf16[256,2048]{1,0:T(8,128)(2,1)} %copy-done.17, bf16[256,2048]{1,0:T(8,128)(2,1)S(1)} %copy-done.16, bf16[512,4736]{1,0:T(8,128)(2,1)} %get-tuple-element.40, bf16[2048,4736]{1,0:T(8,128)(2,1)} %get-tuple-element.33), kind=kOutput, calls=%fused_computation.15 | convolution fusion | flops 9939449856 | bytes 30545920 | tf_op jit(solution)/shard_map/dot_general | solution.py:805
  676.4 16.1 %convolution_convert_fusion = bf16[2048,4736]{1,0:T(8,128)(2,1)} fusion(bf16[512,4736]{1,0:T(8,128)(2,1)} %get-tuple-element.40, f32[2048]{0:T(1024)S(1)} %copy-done.30, f32[512]{0:T(512)S(1)} %copy-done.37, bf16[256,2048]{1,0:T(8,128)(2,1)S(1)} %copy-done.18, bf16[256,2048]{1,0:T(8,128)(2,1)S(1)} %copy-done.16), kind=kOutput, calls=%fused_computation | convolution fusion | flops 9949151232 | bytes 26355712 | tf_op jit(solution)/shard_map/dot_general | solution.py:805
  696.0 6.8 convolution_convert_fusion.4
  702.8 238.1 %scatter_sum.1 = f32[128,6272]{1,0:T(8,128)} custom-call(bf16[8,2,128,4736]{3,2,1,0:T(8,128)(2,1)} %bitcast.84, bf16[8,2,128,1536]{3,2,1,0:T(8,128)(2,1)} %bitcast.85, bf16[8,2,128,128]{3,2,1,0:T(8,128)(2,1)S(1)} %bitcast.83), custom_call_target="tpu_custom_call" | custom-call | tf_op jit(solution)/shard_map/scatter_sum/pallas_call | solution.py:747
  (247 shorter events, 100.3 us)
Async XLA Ops:
  7.2 413.0 %all-gather.4.cloned.1.call-start = ((), (), s32[]{:S(2)}) async-start(), calls=%async_computation.3 | async-start | bytes 12255232 | tf_op jit(solution)/shard_map/all_gather | solution.py:814
  9.8 422.3 %all-gather.6.cloned.1.call-start = ((), (), s32[]{:S(2)}) async-start(), calls=%async_computation.4 | async-start | bytes 12255232 | tf_op jit(solution)/shard_map/all_gather | solution.py:814
  10.8 433.2 %all-gather.8.cloned.1.call-start = ((), (), s32[]{:S(2)}) async-start(), calls=%async_computation.5 | async-start | bytes 12255232 | tf_op jit(solution)/shard_map/all_gather | solution.py:814
  13.3 951.6 %reduce-scatter.8.cloned.1.call-start = ((), (), s32[]{:S(2)}) async-start(), calls=%async_computation.8 | async-start | bytes 12255232 | tf_op jit(solution)/shard_map/reduce_scatter | solution.py:818
  13.4 8.6 collective-permute-start.1
  16.4 268.5 %collective-permute-start = (bf16[256,2048]{1,0:T(8,128)(2,1)S(1)}, bf16[256,2048]{1,0:T(8,128)(2,1)}, u32[]{:S(2)}, u32[]{:S(2)}) collective-permute-start(bf16[256,2048]{1,0:T(8,128)(2,1)S(1)} %copy-done.11), channel_id=1, source_target_pairs={{0,1},{1,0},{2,3},{3,2},{4,5},{5,4},{6,7},{7,6},{8,9},{9,8},{10,11... | collective-permute-start | bytes 3145736 | tf_op jit(solution)/shard_map/ppermute | solution.py:785
  17.4 286.8 %copy-start.3 = (f32[1,128]{1,0:T(1,128)}, f32[1,128]{1,0:T(1,128)S(1)}, u32[]{:S(2)}) copy-start(f32[1,128]{1,0:T(1,128)S(1)} %get-tuple-element.160.bias_ref) | copy-start | bytes 1540
  17.4 286.8 %copy-start.5 = (f32[1,128]{1,0:T(1,128)}, f32[1,128]{1,0:T(1,128)S(1)}, u32[]{:S(2)}) copy-start(f32[1,128]{1,0:T(1,128)S(1)} %get-tuple-element.161.log_ref) | copy-start | bytes 1540
  347.5 26.3 %collective-permute-start.2 = (bf16[256,2048]{1,0:T(8,128)(2,1)}, bf16[256,2048]{1,0:T(8,128)(2,1)}, u32[]{:S(2)}, u32[]{:S(2)}) collective-permute-start(bf16[256,2048]{1,0:T(8,128)(2,1)} %dynamic-slice_convert_fusion.3), channel_id=1, source_target_pairs={{0,1},{1,0},{2,3},{3,2},{4,5},{5,4},{6,7},{7,6},{8,9},{9,8},{10,11... | collective-permute-start | bytes 3145736 | tf_op jit(solution)/shard_map/ppermute | solution.py:785
  349.0 47.3 %collective-permute-start.5 = (bf16[256,2048]{1,0:T(8,128)(2,1)}, bf16[256,2048]{1,0:T(8,128)(2,1)}, u32[]{:S(2)}, u32[]{:S(2)}) collective-permute-start(bf16[256,2048]{1,0:T(8,128)(2,1)} %param.23), channel_id=1, source_target_pairs={{0,1},{1,0},{2,3},{3,2},{4,5},{5,4},{6,7},{7,6},{8,9},{9,8},{10,11... | collective-permute-start | bytes 3145736 | tf_op jit(solution)/shard_map/ppermute | solution.py:785
  376.4 41.9 %copy-start.9 = (f32[256,2048]{1,0:T(8,128)}, f32[256,2048]{1,0:T(8,128)S(1)}, u32[]{:S(2)}) copy-start(f32[256,2048]{1,0:T(8,128)S(1)} %get-tuple-element.116) | copy-start | bytes 6291460
  376.6 41.7 %collective-permute-start.3 = (bf16[256,2048]{1,0:T(8,128)(2,1)S(1)}, bf16[256,2048]{1,0:T(8,128)(2,1)S(1)}, u32[]{:S(2)}, u32[]{:S(2)}) collective-permute-start(bf16[256,2048]{1,0:T(8,128)(2,1)S(1)} %multiply_convert_fusion.3), channel_id=1, source_target_pairs={{0,1},{1,0},{2,3},{3,2},{4,5},{5,4},{6,7},{7,6},{8,9},{9,8},{10,11... | collective-permute-start | bytes 3145736 | tf_op jit(solution)/shard_map/ppermute | solution.py:785
  470.3 497.3 %reduce-scatter.4.cloned.1.call-start = ((), (), s32[]{:S(2)}) async-start(), calls=%async_computation.6 | async-start | bytes 12255232 | tf_op jit(solution)/shard_map/reduce_scatter | solution.py:818
  482.9 486.9 %reduce-scatter.6.cloned.1.call-start = ((), (), s32[]{:S(2)}) async-start(), calls=%async_computation.7 | async-start | bytes 12255232 | tf_op jit(solution)/shard_map/reduce_scatter | solution.py:818
  494.8 26.1 %slice-start = ((s8[11534336]{0:T(1024)(128)(4,1)}), s8[4194304]{0:T(1024)(128)(4,1)S(1)}, s32[]{:S(2)}) async-start(s8[11534336]{0:T(1024)(128)(4,1)} %bitcast.98), calls=%async_computation.9 | async-start | bytes 8388608
  494.8 26.0 %slice-start.1 = ((s8[11534336]{0:T(1024)(128)(4,1)}), s8[4194304]{0:T(1024)(128)(4,1)S(1)}, s32[]{:S(2)}) async-start(s8[11534336]{0:T(1024)(128)(4,1)} %bitcast.98), calls=%async_computation.10 | async-start | bytes 8388608
  519.5 26.1 %collective-permute-start.6 = (bf16[256,2048]{1,0:T(8,128)(2,1)S(1)}, bf16[256,2048]{1,0:T(8,128)(2,1)S(1)}, u32[]{:S(2)}, u32[]{:S(2)}) collective-permute-start(bf16[256,2048]{1,0:T(8,128)(2,1)S(1)} %dynamic-slice_convert_fusion.1), channel_id=1, source_target_pairs={{0,1},{1,0},{2,3},{3,2},{4,5},{5,4},{6,7},{7,6},{8,9},{9,8},{10,11... | collective-permute-start | bytes 3145736 | tf_op jit(solution)/shard_map/ppermute | solution.py:785
  529.1 37.6 %collective-permute-start.4 = (bf16[256,2048]{1,0:T(8,128)(2,1)S(1)}, bf16[256,2048]{1,0:T(8,128)(2,1)S(1)}, u32[]{:S(2)}, u32[]{:S(2)}) collective-permute-start(bf16[256,2048]{1,0:T(8,128)(2,1)S(1)} %dynamic-slice_convert_fusion.2), channel_id=1, source_target_pairs={{0,1},{1,0},{2,3},{3,2},{4,5},{5,4},{6,7},{7,6},{8,9},{9,8},{10,11... | collective-permute-start | bytes 3145736 | tf_op jit(solution)/shard_map/ppermute | solution.py:785
  571.0 24.0 %collective-permute-start.7 = (bf16[256,2048]{1,0:T(8,128)(2,1)S(1)}, bf16[256,2048]{1,0:T(8,128)(2,1)}, u32[]{:S(2)}, u32[]{:S(2)}) collective-permute-start(bf16[256,2048]{1,0:T(8,128)(2,1)S(1)} %get-tuple-element.113), channel_id=1, source_target_pairs={{0,1},{1,0},{2,3},{3,2},{4,5},{5,4},{6,7},{7,6},{8,9},{9,8},{10,11... | collective-permute-start | bytes 3145736 | tf_op jit(solution)/shard_map/ppermute | solution.py:785
  605.4 49.6 %copy-start.16 = (bf16[256,2048]{1,0:T(8,128)(2,1)S(1)}, bf16[256,2048]{1,0:T(8,128)(2,1)}, u32[]{:S(2)}) copy-start(bf16[256,2048]{1,0:T(8,128)(2,1)} %copy-done.15) | copy-start | bytes 3145732
  605.4 49.5 %copy-start.37 = (f32[512]{0:T(512)S(1)}, f32[512]{0:T(512)}, u32[]{:S(2)}) copy-start(f32[512]{0:T(512)} %copy-done.36) | copy-start | bytes 6148
  654.9 21.5 %copy-start.18 = (bf16[256,2048]{1,0:T(8,128)(2,1)S(1)}, bf16[256,2048]{1,0:T(8,128)(2,1)}, u32[]{:S(2)}) copy-start(bf16[256,2048]{1,0:T(8,128)(2,1)} %copy-done.17) | copy-start | bytes 3145732
  675.2 283.9 %collective-permute-start.8 = (bf16[256,2048]{1,0:T(8,128)(2,1)}, bf16[256,2048]{1,0:T(8,128)(2,1)}, u32[]{:S(2)}, u32[]{:S(2)}) collective-permute-start(bf16[256,2048]{1,0:T(8,128)(2,1)} %dynamic-slice_convert_fusion), channel_id=1, source_target_pairs={{0,1},{1,0},{2,3},{3,2},{4,5},{5,4},{6,7},{7,6},{8,9},{9,8},{10,11... | collective-permute-start | bytes 3145736 | tf_op jit(solution)/shard_map/ppermute | solution.py:785
  941.8 13.5 %collective-permute-start.9 = (f32[4,128]{0,1:T(8,128)S(1)}, f32[4,128]{0,1:T(8,128)S(1)}, u32[]{:S(2)}, u32[]{:S(2)}) collective-permute-start(f32[4,128]{0,1:T(8,128)S(1)} %slice_bitcast_fusion.2), channel_id=1, source_target_pairs={{0,1},{1,0},{2,3},{3,2},{4,5},{5,4},{6,7},{7,6},{8,9},{9,8},{10,11... | collective-permute-start | bytes 6152 | tf_op jit(solution)/shard_map/ppermute | solution.py:785
  (38 other events, 327.0 us)
Sparse Core Ops, SparseCore 0:
  10.9 190.3 all-gather.3
  204.2 110.0 all-gather.5
  317.0 97.8 all-gather.7
  470.4 131.6 reduce-scatter.7
  606.6 142.9 reduce-scatter.3
  753.6 187.3 reduce-scatter.5

commit v3 on v2

--- a/solution.py
+++ b/solution.py
@@ -515,7 +515,8 @@
 MESH = pl.DeviceIdType.MESH
 
 
-def column_chunks(widths, size):
+def column_chunks(widths, size, layers):
+    size = size * max(1, layers // 4)
     out = []
     for a, width in enumerate(widths):
         units = width // 128
@@ -547,95 +548,204 @@
     )
 
 
-def gather_kernel(layers, chunks, count, *refs):
-    srcs, outs = refs[:count], refs[count : 2 * count]
-    own_sem, zs, zr, ys, yr, cs, cr = refs[2 * count :]
+def gather_kernel(layers, chunks, count, pairs, *refs):
+    srcs, outs = refs[: count + pairs], refs[count + pairs : 2 * (count + pairs)]
+    own_sem, us, ur, ds, dr, ys, yr, cs, cr, ps, pr, pair_sem = refs[2 * (count + pairs) :]
     rows = srcs[0].shape[0]
     spot, core, side, layer = placement()
-    at = lambda z, y, c: 4 * lax.rem(z + layers, layers) + 2 * y + c
-    z_to = [at(layer + k, side, core) for k in range(1, layers)]
+    turn = lax.axis_index("tensor")
+    at = lambda z, y, c: 4 * z + 2 * y + c
     y_to, c_to = at(layer, 1 - side, core), at(layer, side, 1 - core)
-    greet(z_to + [y_to, c_to])
+    has_up, has_down = layer < layers - 1, layer > 0
+    barrier = pltpu.get_barrier_semaphore()
+    around = [4 * lax.rem(layer + s, layers) + 2 * side + core for s in (1, layers - 1)]
+    for partner in [y_to, c_to] + around:
+        pl.semaphore_signal(barrier, inc=1, device_id={"dp": partner}, device_id_type=MESH)
+    pl.semaphore_signal(barrier, inc=1, device_id={"tensor": 1 - turn}, device_id_type=MESH)
+    pl.semaphore_wait(barrier, 5)
 
     def place(j, origin):
-        a, lo, width = chunks[j]
+        a, lo, width, _ = chunks[j]
         start = pl.multiple_of(origin * rows, rows)
         return outs[a].at[pl.ds(start, rows), lo : lo + width]
 
     def own(j):
-        a, lo, width = chunks[j]
+        a, lo, width, _ = chunks[j]
         return srcs[a].at[:, lo : lo + width]
 
-    def z_copy(j, k, origin, src):
-        return remote(src, place(j, origin), zs.at[j, k - 1], zr.at[j, k - 1], z_to[k - 1])
-
-    def y_copy(j, m, origin, src):
-        return remote(src, place(j, origin), ys.at[j, m], yr.at[j, m], y_to)
-
-    def c_copy(j, m, half, origin, src):
-        i = 2 * m + half
-        return remote(src, place(j, origin), cs.at[j, i], cr.at[j, i], c_to)
-
+    def up_copy(j, k, half, origin, src):
+        i = 2 * k + half
+        return remote(src, place(j, origin), us.at[j, i], ur.at[j, i], spot + 4)
+
+    def down_copy(j, k, half, origin, src):
+        i = 2 * k + half
+        return remote(src, place(j, origin), ds.at[j, i], dr.at[j, i], spot - 4)
+
+    def y_copy(j, slot, origin, src):
+        return remote(src, place(j, origin), ys.at[j, slot], yr.at[j, slot], y_to)
+
+    def c_copy(j, slot, origin, src):
+        return remote(src, place(j, origin), cs.at[j, slot], cr.at[j, slot], c_to)
+
+    number = len(chunks)
+    narrow = [j for j in range(number) if not chunks[j][3]]
+    early = [j for j in range(number) if chunks[j][3]]
     keep = []
-    number = len(chunks)
-    for j in range(number):
-        for k in range(1, layers):
-            z_copy(j, k, spot, own(j)).start()
+    for p in range(pairs):
+        half_rows = srcs[count + p].shape[0]
+        spot_rows = pl.ds(pl.multiple_of(turn * half_rows, half_rows), half_rows)
+        copy = pltpu.make_async_remote_copy(
+            src_ref=srcs[count + p], dst_ref=outs[count + p].at[spot_rows, :],
+            send_sem=ps.at[p], recv_sem=pr.at[p],
+            device_id={"tensor": 1 - turn}, device_id_type=MESH,
+        )
+        copy.start()
+        local_copy = pltpu.make_async_copy(
+            srcs[count + p], outs[count + p].at[spot_rows, :], pair_sem.at[p]
+        )
+        local_copy.start()
+        keep.append((copy, local_copy))
+
+    def send_z(j, half, origin, src):
+        @pl.when(has_up)
+        def _():
+            up_copy(j, 0, half, origin, src).start()
+
+        @pl.when(has_down)
+        def _():
+            down_copy(j, 0, half, origin, src).start()
+
+    locals_ = []
+    for j in early + narrow:
         y_copy(j, 0, spot, own(j)).start()
-        c_copy(j, 0, 0, spot, own(j)).start()
+        send_z(j, 0, spot, own(j))
+        c_copy(j, 0, spot, own(j)).start()
         copy = pltpu.make_async_copy(own(j), place(j, spot), own_sem.at[j])
         copy.start()
-        keep.append(copy)
-
-    def second(j):
+        locals_.append(copy)
+    across = at(layer, 1 - side, core)
+
+    def take_z(j, k, half):
+        there = lax.rem(side + half, 2)
+        for sign, fits, more, copy in (
+            (-1, layer >= k + 1, has_up, up_copy),
+            (1, layer + k + 1 < layers, has_down, down_copy),
+        ):
+
+            @pl.when(fits)
+            def _(sign=sign, more=more, copy=copy):
+                origin = at(layer + sign * (k + 1), there, core)
+                here = place(j, origin)
+                copy(j, k, half, origin, here).wait_recv()
+
+                @pl.when(more)
+                def _():
+                    copy(j, k + 1, half, origin, here).start()
+
+                slot = 2 * k + (1 if sign < 0 else 2)
+                if not chunks[j][3]:
+                    y_copy(j, slot, origin, here).start()
+                c_copy(j, slot if half == 0 else slot + 2 * layers - 1, origin, here).start()
+
+    def take_y(j, k):
+        slots = [(0, None, None)] if k == 0 else [
+            (2 * k - 1, layer >= k, -1), (2 * k, layer + k < layers, 1)
+        ]
+        for slot, fits, sign in slots:
+            shift = 0 if sign is None else sign * k
+
+            def body(slot=slot, shift=shift):
+                origin = at(layer + shift, 1 - side, core)
+                here = place(j, origin)
+                y_copy(j, slot, origin, here).wait_recv()
+                c_copy(j, 2 * layers - 1 + slot, origin, here).start()
+
+            if fits is None:
+                body()
+            else:
+                pl.when(fits)(body)
+
+    for j in early:
+        y_copy(j, 0, across, own(j)).wait_recv()
+        send_z(j, 1, across, place(j, across))
+        c_copy(j, 2 * layers - 1, across, place(j, across)).start()
+    for k in range(layers):
+        if k < layers - 1:
+            for j in early:
+                for half in range(2):
+                    take_z(j, k, half)
+            for j in narrow:
+                take_z(j, k, 0)
+        if k > 0:
+            for j in narrow:
+                take_y(j, k - 1)
+    for j in narrow:
+        take_y(j, layers - 1)
+
+    for copy, local_copy in keep:
+        local_copy.wait()
+        copy.wait()
+    for copy in locals_:
+        copy.wait()
+    for j in range(number):
+        wide = chunks[j][3]
+        me = own(j)
+        for half in range(2 if wide else 1):
+            for k in range(layers - 1):
+
+                @pl.when(has_up & (layer >= k))
+                def _(k=k, half=half):
+                    up_copy(j, k, half, spot, me).wait_send()
+
+                @pl.when(has_down & (layer + k < layers))
+                def _(k=k, half=half):
+                    down_copy(j, k, half, spot, me).wait_send()
+
+        def settle(slot, shift):
+            if slot == 0 or not wide:
+                y_copy(j, slot, spot, me).wait_send()
+            for half in range(2):
+                origin = at(layer + shift, lax.rem(side + half, 2), 1 - core)
+                c_copy(j, slot + half * (2 * layers - 1), origin, place(j, origin)).wait()
+
+        settle(0, 0)
         for k in range(1, layers):
-            origin = at(layer - k, side, core)
-            here = place(j, origin)
-            z_copy(j, k, origin, here).wait_recv()
-            y_copy(j, k, origin, here).start()
-            c_copy(j, k, 0, origin, here).start()
-
-    def third(j):
-        for m in range(layers):
-            origin = at(layer - m, 1 - side, core)
-            here = place(j, origin)
-            y_copy(j, m, origin, here).wait_recv()
-            c_copy(j, m, 1, origin, here).start()
-
-    for j in range(number + 1):
-        if j < number:
-            second(j)
-        if j >= 1:
-            third(j - 1)
-    for j in range(number):
-        keep[j].wait()
-        for k in range(1, layers):
-            z_copy(j, k, spot, own(j)).wait_send()
-        for m in range(layers):
-            y_copy(j, m, spot, own(j)).wait_send()
-            for half in range(2):
-                origin = at(layer - m, lax.rem(side + half, 2), 1 - core)
-                c_copy(j, m, half, origin, place(j, origin)).wait()
-
-
-def gather_all(shards, devices, ident, size=512):
+            pl.when(layer >= k)(functools.partial(settle, 2 * k - 1, -k))
+            pl.when(layer + k < layers)(functools.partial(settle, 2 * k, k))
+
+
+def mark_early(chunks, share):
+    total = sum(c[2] for c in chunks)
+    marked, done = [], 0
+    for c in chunks:
+        early = done + c[2] <= share * total + 64
+        done += c[2] if early else 0
+        marked.append(c + (early,))
+    return marked
+
+
+def gather_all(shards, pairs, devices, ident, size=512, share=1 / 6):
     rows = shards[0].shape[0]
     layers = devices // 4
-    chunks = column_chunks([s.shape[1] for s in shards], size)
+    chunks = mark_early(column_chunks([s.shape[1] for s in shards], size, layers), share)
     n = len(chunks)
     sem = lambda *shape: pltpu.SemaphoreType.DMA(shape)
+    z_slots, slots = 2 * layers, 2 * layers - 1
+    arrays = tuple(shards) + tuple(pairs)
     return pl.pallas_call(
-        functools.partial(gather_kernel, layers, chunks, len(shards)),
-        in_specs=[pl.BlockSpec(memory_space=pl.ANY)] * len(shards),
-        out_specs=[pl.BlockSpec(memory_space=pl.ANY)] * len(shards),
-        out_shape=[jax.ShapeDtypeStruct((devices * rows, s.shape[1]), s.dtype) for s in shards],
+        functools.partial(gather_kernel, layers, chunks, len(shards), len(pairs)),
+        in_specs=[pl.BlockSpec(memory_space=pl.ANY)] * len(arrays),
+        out_specs=[pl.BlockSpec(memory_space=pl.ANY)] * len(arrays),
+        out_shape=[jax.ShapeDtypeStruct((devices * rows, s.shape[1]), s.dtype) for s in shards]
+        + [jax.ShapeDtypeStruct((2 * p.shape[0], p.shape[1]), p.dtype) for p in pairs],
         scratch_shapes=[
-            sem(n), sem(n, layers - 1), sem(n, layers - 1), sem(n, layers), sem(n, layers),
-            sem(n, 2 * layers), sem(n, 2 * layers),
+            sem(n), sem(n, z_slots), sem(n, z_slots), sem(n, z_slots), sem(n, z_slots),
+            sem(n, slots), sem(n, slots), sem(n, 2 * slots), sem(n, 2 * slots),
+            sem(max(1, len(pairs))), sem(max(1, len(pairs))), sem(max(1, len(pairs))),
         ],
         compiler_params=pltpu.CompilerParams(collective_id=ident, has_side_effects=True),
         name="gather_rows",
-    )(*shards)
+    )(*arrays)
 
 
 def scatter_kernel(layers, chunks, count, *refs):
@@ -739,7 +849,7 @@
     widths = [w or p.shape[1] for w, p in zip(widths, parts)]
     rows = parts[0].shape[0] // devices
     layers = devices // 4
-    chunks = column_chunks(widths, size)
+    chunks = column_chunks(widths, size, layers)
     n = len(chunks)
     width = sum(widths)
     widest = max(c[2] for c in chunks)
@@ -793,11 +903,16 @@
     )
 
 
-def pair_scatter(parts):
+def pair_halves(parts):
     rows = parts.shape[0] // 2
     mine = lax.axis_index("tensor") * rows
     kept = lax.dynamic_slice_in_dim(parts, mine, rows)
     sent = lax.dynamic_slice_in_dim(parts, rows - mine, rows).astype(bf16)
+    return kept, sent
+
+
+def pair_scatter(parts):
+    kept, sent = pair_halves(parts)
     return kept + pair_swap(sent).astype(f32)
 
 
@@ -868,9 +983,9 @@
     proj_shard = jnp.concatenate(
         [low(w_query), low(w_key), low(w_value), low(w_gate), small], axis=1
     )
-    seq_x = pair_gather(tokens)
-    seq_cot = pair_gather(cotangent)
-    proj, out_t = gather_all((proj_shard, low(w_output).T), devices, 0)
+    proj, out_t, seq_x, seq_cot = gather_all(
+        (proj_shard, low(w_output).T), (tokens, cotangent), devices, 0
+    )
     extra_at = 12 * heads * 128
     gain_at = extra_at + 2 * heads + filter_cols
     sides = proj[:, gain_at : gain_at + 6].astype(f32)
@@ -913,33 +1028,45 @@
     sigmoid_gate = jax.nn.sigmoid(gate_act)
     silu_gate = gate_act * sigmoid_gate
     inner = low(silu_gate * up_act)
-    result = low(hidden + pair_scatter(dot(inner, down_t, 1, 1)))
-
     grad_inner = dot(seq_cot, down_t)
-    grad_down = low(dot(seq_cot, inner, 0, 0))
     grad_gate_act = low(
         grad_inner * up_act * sigmoid_gate * (1.0 + gate_act * (1.0 - sigmoid_gate))
     )
     grad_up_act = low(grad_inner * silu_gate)
+    grad_down = low(dot(seq_cot, inner, 0, 0))
+    grad_gate_act, grad_up_act, grad_down = lax.optimization_barrier(
+        (grad_gate_act, grad_up_act, grad_down)
+    )
+    down_piece = scatter_rows(grad_down)
+    grad_seq_ffn = dot(grad_gate_act, gate_weight, 1, 1) + dot(grad_up_act, up_weight, 1, 1)
+    kept_ffn, sent_ffn = pair_halves(grad_seq_ffn)
+    sent_ffn, grad_gate_act, grad_up_act, inner = lax.optimization_barrier(
+        (sent_ffn, grad_gate_act, grad_up_act, inner)
+    )
+    grad_normed_ffn = kept_ffn + pair_swap(sent_ffn).astype(f32)
     grad_gate_w = low(dot(seq_ffn, grad_gate_act, 0, 0))
     grad_up_w = low(dot(seq_ffn, grad_up_act, 0, 0))
-    grad_seq_ffn = dot(grad_gate_act, gate_weight, 1, 1) + dot(grad_up_act, up_weight, 1, 1)
-    grad_normed_ffn = pair_scatter(grad_seq_ffn)
+    gate_piece = scatter_rows(grad_gate_w)
+    kept_out, sent_out = pair_halves(dot(inner, down_t, 1, 1))
     grad_hidden_norm, grad_gain_ffn = norm_back(hidden, full_ffn, grad_normed_ffn)
     grad_hidden = cotangent.astype(f32) + grad_hidden_norm
     seq_grad_branch = pair_gather(low(grad_hidden))
-
-    down_piece = scatter_rows(grad_down)
-    gate_piece = scatter_rows(grad_gate_w)
-    up_piece = scatter_rows(grad_up_w)
+    seq_grad_branch, sent_out = lax.optimization_barrier((seq_grad_branch, sent_out))
+    come_out = pair_swap(sent_out)
 
     grad_gated = dot(seq_grad_branch, out_t)
-    grad_out_t = low(dot(seq_grad_branch, gated, 0, 0))
     grad_pre, grad_fq, grad_fk, grad_fv, grad_gain_out, grad_small = mixer_backward(
         *mixer_args, saved, low(grad_gated)
     )
+    grad_pre, come_out = lax.optimization_barrier((grad_pre, come_out))
+    result = low(hidden + kept_out + come_out.astype(f32))
     grad_seq_in = dot(grad_pre, proj, 1, 1)
+    kept_in, sent_in = pair_halves(grad_seq_in)
+    sent_in, grad_pre, gated = lax.optimization_barrier((sent_in, grad_pre, gated))
+    come_in = pair_swap(sent_in)
     grad_proj = low(dot(seq_in, grad_pre, 0, 0))
+    grad_out_t = low(dot(seq_grad_branch, gated, 0, 0))
+    come_in, grad_proj, grad_out_t = lax.optimization_barrier((come_in, grad_proj, grad_out_t))
     by_device = lambda g, piece: g.reshape(tap_count, heads, devices, piece)
     grad_flat = jnp.concatenate(
         [by_device(grad_fq, piece_q), by_device(grad_fk, piece_q), by_device(grad_fv, piece_v)],
@@ -963,8 +1090,12 @@
         [grad_proj[:, extra_at : extra_at + 2 * heads], grad_flat, low(columns)], axis=1
     )
     grad_tiny = jnp.pad(grad_tiny, ((0, 0), (0, EXTRA - grad_tiny.shape[1])))
-    pieces = scatter_sum((grad_proj, grad_out_t, grad_tiny), (extra_at, None, None), devices, 1)
-    grad_normed_in = pair_scatter(grad_seq_in)
+    pieces = scatter_sum(
+        (grad_up_w, grad_proj, grad_out_t, grad_tiny), (None, extra_at, None, None), devices, 1
+    )
+    ffn_width = grad_up_w.shape[1]
+    up_piece, pieces = pieces[:, :ffn_width], pieces[:, ffn_width:]
+    grad_normed_in = kept_in + come_in.astype(f32)
     out_width = w_output.shape[0]
     out_piece = pieces[:, extra_at : extra_at + out_width]
     tiny_piece = pieces[:, extra_at + out_width :]
@@ -1001,7 +1132,7 @@
         sums[3, n_heads : 2 * n_heads],
         out_piece.T,
         gate_piece.astype(f32),
-        up_piece.astype(f32),
+        up_piece,
         down_piece.astype(f32).T,
     )
 

time: 989 us -> 962 us (0.973)
  waiting for transfers between devices: 121 us -> 61.2 us
  Pallas kernels: 570 us -> 620 us
    ppermute x10 -> x8, waiting for transfers between devices: 121 us -> 61.1 us  [pair_swap(): return lax.ppermute(values, 'tensor', [(0, 1), (1, 0)])]
    pallas_call x1, Pallas kernels: 248 us -> 277 us  [gather_all(): pl.pallas_call(functools.partial(gather_kernel, layers, chunks, len(shard...]
    pallas_call x1, Pallas kernels: 238 us -> 259 us  [scatter_sum(): pl.pallas_call(functools.partial(scatter_kernel, layers, chunks, len(part...]
  transfers between devices with their start and end apart: 16 -> 13, of which waited for: 6 -> 4; matrix products, arithmetic and copies ran while one was open for 23% -> 22% of each run, Pallas kernels for 58% -> 65%
where the time goes in v3:
time: 962 us; the launch traced here: 957 us
  Pallas kernels  620 us (64%)
  matrix products  170 us (18%)
  waiting for transfers between devices  61.2 us (6%)
  local copies, waits for them, and re-layouts  43.8 us (5%)
  other arithmetic  35.4 us (4%)
  between operations  15.6 us (2%)
  starting transfers between devices  11 us (1%)
    pallas_call x1, Pallas kernels, gather_all(): pl.pallas_call(functools.partial(gather_kernel, layers, chunks, len(shard...  277 us
    pallas_call x1, Pallas kernels, scatter_sum(): pl.pallas_call(functools.partial(scatter_kernel, layers, chunks, len(part...  259 us
    dot_general x15, matrix products, dot(): lax.dot_general(a, b, (((ca,), (cb,)), ((), ())), preferred_element_type=...  170 us
    ppermute x8, waiting for transfers between devices, pair_swap(): return lax.ppermute(values, 'tensor', [(0, 1), (1, 0)])  61.1 us
    pallas_call x1, Pallas kernels, mixer_backward(): pl.pallas_call(functools.partial(bwd_kernel, heads), grid=(heads,), in_sp...  49.3 us
    pallas_call x1, Pallas kernels, mixer_forward(): pl.pallas_call(functools.partial(fwd_kernel, heads), grid=(heads,), in_sp...  35.3 us
  transfers between devices with their start and end apart: 13, of which 4 were waited for; matrix products, arithmetic and copies ran while one was open for 22% of the time, Pallas kernels for 65%

profile of v3, /device:TPU:0, one launch (start us, length us, event | category | flops | bytes accessed | tf_op | source)
XLA Modules:
  0.0 956.8 jit_solution(1999942595053867008)
XLA Ops:
  23.3 276.9 %gather_rows.1 = (bf16[2048,4736]{1,0:T(8,128)(2,1)}, bf16[2048,1536]{1,0:T(8,128)(2,1)}, bf16[512,2048]{1,0:T(8,128)(2,1)}, bf16[512,2048]{1,0:T(8,128)(2,1)}) custom-call(bf16[128,4736]{1,0:T(8,128)(2,1)} %copy-done.22, bf16[128,1536]{1,0:T(8,128)(2,1)} %bitcast.95, bf16[256,2048]{1,0:T(8,128)(2,1)} %refs_2_.1, bf16[256,2048]{1,0:T(8,128)(2,1)} %refs_3_.1), custom_call_target="tpu_custom_call" | custom-call | tf_op jit(solution)/shard_map/gather_rows/pallas_call | solution.py:735
  312.6 18.0 %fusion.14.q_ref.k_ref.v_ref.g_ref.bd_ref = f32[512,4736]{1,0:T(8,128)} fusion(bf16[2048,4736]{1,0:T(8,128)(2,1)} %get-tuple-element.53, bf16[512,2048]{1,0:T(8,128)(2,1)} %get-tuple-element.52, f32[2048]{0:T(1024)S(1)} %get-tuple-element.148, f32[512]{0:T(512)S(1)} %add_rsqrt_fusion), kind=kOutput, calls=%fused_computation.53 | convolution fusion | flops 9936306176 | bytes 31205376 | tf_op jit(solution)/shard_map/dot_general | solution.py:920
  330.6 35.3 %mixer_forward.1 = (bf16[512,1536]{1,0:T(8,128)(2,1)S(1)}, bf16[3,512,256]{2,1,0:T(8,128)(2,1)S(1)}, bf16[512,1536]{1,0:T(8,128)(2,1)S(1)}, f32[512,1536]{1,0:T(8,128)}, f32[3,1,256,512]{3,2,1,0:T(8,128)}) custom-call(s32[1]{0:T(128)S(6)} %copy.119.len_ref, f32[512,4736]{1,0:T(8,128)} %fusion.14.q_ref.k_ref.v_ref.g_ref.bd_ref, ...), custom_call_target="tpu_custom_call" | custom-call | tf_op jit(solution)/shard_map/mixer_forward/pallas_call | solution.py:437
  365.9 6.3 fusion.35
  375.9 24.3 %collective-permute-done.1 = bf16[256,2048]{1,0:T(8,128)(2,1)} collective-permute-done((bf16[256,2048]{1,0:T(8,128)(2,1)}, bf16[256,2048]{1,0:T(8,128)(2,1)}, u32[]{:S(2)}, u32[]{:S(2)}) %collective-permute-start.1) | collective-permute-done | bytes 1048608 | tf_op jit(solution)/shard_map/ppermute | solution.py:895
  404.4 23.3 %collective-permute-done.2 = bf16[256,2048]{1,0:T(8,128)(2,1)S(1)} collective-permute-done((bf16[256,2048]{1,0:T(8,128)(2,1)S(1)}, bf16[256,2048]{1,0:T(8,128)(2,1)S(1)}, u32[]{:S(2)}, u32[]{:S(2)}) %collective-permute-start.2) | collective-permute-done | bytes 1048608 | tf_op jit(solution)/shard_map/ppermute | solution.py:895
  429.3 13.0 %fusion.26 = f32[512,2816]{1,0:T(8,128)} fusion(bf16[2048,2816]{1,0:T(8,128)(2,1)} %all-gather.8.cloned.1.call-done, bf16[256,2048]{1,0:T(8,128)(2,1)} %get-tuple-element.170, bf16[256,2048]{1,0:T(8,128)(2,1)S(1)} %get-tuple-element.169), kind=kOutput, calls=%fused_computation.109 | convolution fusion | flops 5909774336 | bytes 19398656 | tf_op jit(solution)/shard_map/dot_general | solution.py:920
  442.3 12.6 %fusion.36 = f32[512,2816]{1,0:T(8,128)} fusion(bf16[512,2048]{1,0:T(8,128)(2,1)} %get-tuple-element.56, bf16[2048,2816]{0,1:T(8,128)(2,1)} %all-gather.4.cloned.1.call-done), kind=kOutput, calls=%fused_computation.119 | convolution fusion | flops 5905580032 | bytes 19398656 | tf_op jit(solution)/shard_map/dot_general | solution.py:920
  454.9 15.0 %multiply_convert_fusion = (bf16[512,2816]{1,0:T(8,128)(2,1)S(1)}, bf16[512,2816]{1,0:T(8,128)(2,1)}, bf16[512,2816]{1,0:T(8,128)(2,1)}) fusion(f32[512,2816]{1,0:T(8,128)} %fusion.26, f32[512,2816]{1,0:T(8,128)} %fusion.36, bf16[2048,2816]{1,0:T(8,128)(2,1)} %all-gather.6.cloned.1.call-done, bf16[256,2048]{1,0:T(8,128)(2,1)} %get-tuple-element.170, ...), kind=kOutput, calls=%fused_computation.5 | convolution fusion | flops 5931401216 | bytes 33816576 | tf_op jit(solution)/shard_map/dot_general | solution.py:920
  471.5 9.0 convolution_convert_fusion.3
  481.1 10.2 %fusion.37 = f32[512,2048]{1,0:T(8,128)S(1)} fusion(bf16[512,2816]{1,0:T(8,128)(2,1)} %get-tuple-element.82, bf16[2048,2816]{1,0:T(8,128)(2,1)} %all-gather.8.cloned.1.call-done), kind=kOutput, calls=%fused_computation.120 | convolution fusion | flops 5905580032 | bytes 18612224 | tf_op jit(solution)/shard_map/dot_general | solution.py:920
  491.4 10.0 %convolution_add_fusion = f32[512,2048]{1,0:T(8,128)S(1)} fusion(f32[512,2048]{1,0:T(8,128)S(1)} %fusion.37, bf16[512,2816]{1,0:T(8,128)(2,1)S(1)} %copy-done.51, bf16[2048,2816]{1,0:T(8,128)(2,1)} %all-gather.6.cloned.1.call-done), kind=kOutput, calls=%fused_computation.20 | convolution fusion | flops 5906628608 | bytes 22806528 | tf_op jit(solution)/shard_map/dot_general | solution.py:920
  505.6 9.5 convolution_convert_fusion.1
  515.1 10.0 %fusion.38 = f32[512,2048]{1,0:T(8,128)S(1)} fusion(bf16[512,2816]{1,0:T(8,128)(2,1)} %copy-done.50, bf16[2048,2816]{0,1:T(8,128)(2,1)} %all-gather.4.cloned.1.call-done), kind=kOutput, calls=%fused_computation.121 | convolution fusion | flops 5905580032 | bytes 18612224 | tf_op jit(solution)/shard_map/dot_general | solution.py:920
  533.1 9.3 convolution_convert_fusion.2
  542.5 13.3 %collective-permute-done.4 = bf16[256,2048]{1,0:T(8,128)(2,1)S(1)} collective-permute-done((bf16[256,2048]{1,0:T(8,128)(2,1)S(1)}, bf16[256,2048]{1,0:T(8,128)(2,1)S(1)}, u32[]{:S(2)}, u32[]{:S(2)}) %collective-permute-start.4) | collective-permute-done | bytes 1048608 | tf_op jit(solution)/shard_map/ppermute | solution.py:895
  557.4 4.6 convolution_convert_fusion.5.dg_ref
  562.0 49.3 %mixer_backward.1 = (bf16[512,4736]{1,0:T(8,128)(2,1)}, f32[4,768]{1,0:T(4,128)S(1)}, f32[4,768]{1,0:T(4,128)S(1)}, f32[4,1536]{1,0:T(4,128)S(1)}, f32[8,512]{1,0:T(8,128)S(1)}, /*index=5*/f32[8,128]{1,0:T(8,128)S(1)}) custom-call(s32[1]{0:T(128)S(6)} %copy.119.len_ref, f32[512,4736]{1,0:T(8,128)} %fusion.14.q_ref.k_ref.v_ref.g_ref.bd_ref, ...), custom_call_target="tpu_custom_call" | custom-call | tf_op jit(solution)/shard_map/mixer_backward/pallas_call | solution.py:473
  614.0 19.1 %fusion.4 = (bf16[2048]{0:T(1024)(128)(2,1)S(1)}, f32[512,2048]{1,0:T(8,128)S(1)}) fusion(bf16[512,2048]{1,0:T(8,128)(2,1)} %get-tuple-element.52, f32[512]{0:T(512)} %copy-done.42, bf16[512,4736]{1,0:T(8,128)(2,1)} %get-tuple-element.71, bf16[2048,4736]{1,0:T(8,128)(2,1)} %get-tuple-element.53), kind=kOutput, calls=%fused_computation.15 | convolution fusion | flops 9936304128 | bytes 30545920 | tf_op jit(solution)/shard_map/dot_general | solution.py:920
  635.4 17.5 %convolution_convert_fusion = bf16[2048,4736]{1,0:T(8,128)(2,1)} fusion(bf16[512,4736]{1,0:T(8,128)(2,1)} %get-tuple-element.71, bf16[512,2048]{1,0:T(8,128)(2,1)} %get-tuple-element.52, f32[2048]{0:T(1024)S(1)} %copy-done.34, f32[512]{0:T(512)S(1)} %copy-done.43), kind=kOutput, calls=%fused_computation | convolution fusion | flops 9946005504 | bytes 26355712 | tf_op jit(solution)/shard_map/dot_general | solution.py:920
  653.0 3.2 add_convert_fusion
  656.3 5.4 convolution_convert_fusion.4
  662.5 258.8 %scatter_sum.1 = f32[128,9088]{1,0:T(8,128)} custom-call(bf16[8,2,128,2816]{3,2,1,0:T(8,128)(2,1)} %bitcast.90, bf16[8,2,128,4736]{3,2,1,0:T(8,128)(2,1)} %bitcast.89, bf16[8,2,128,1536]{3,2,1,0:T(8,128)(2,1)} %bitcast.91, bf16[8,2,128,128]{3,2,1,0:T(8,128)(2,1)S(1)} %bitcast.88), custom_call_target="tpu_custom_call" | custom-call | tf_op jit(solution)/shard_map/scatter_sum/pallas_call | solution.py:857
  931.9 3.9 fusion.11
  (261 shorter events, 83.3 us)
Async XLA Ops:
  7.2 422.1 %all-gather.8.cloned.1.call-start = ((), (), s32[]{:S(2)}) async-start(), calls=%async_computation.4 | async-start | bytes 12255232 | tf_op jit(solution)/shard_map/all_gather | solution.py:929
  9.9 432.4 %all-gather.4.cloned.1.call-start = ((), (), s32[]{:S(2)}) async-start(), calls=%async_computation.2 | async-start | bytes 12255232 | tf_op jit(solution)/shard_map/all_gather | solution.py:929
  10.9 444.0 %all-gather.6.cloned.1.call-start = ((), (), s32[]{:S(2)}) async-start(), calls=%async_computation.3 | async-start | bytes 12255232 | tf_op jit(solution)/shard_map/all_gather | solution.py:929
  11.9 933.1 %reduce-scatter.5.cloned.1.call-start = ((), (), s32[]{:S(2)}) async-start(), calls=%async_computation.6 | async-start | bytes 12255232 | tf_op jit(solution)/shard_map/reduce_scatter | solution.py:933
  12.0 9.6 collective-permute-start
  15.9 314.6 %copy-start.1 = (f32[1,128]{1,0:T(1,128)}, f32[1,128]{1,0:T(1,128)S(1)}, u32[]{:S(2)}) copy-start(f32[1,128]{1,0:T(1,128)S(1)} %get-tuple-element.193.bias_ref) | copy-start | bytes 1540
  15.9 314.6 %copy-start.3 = (f32[1,128]{1,0:T(1,128)}, f32[1,128]{1,0:T(1,128)S(1)}, u32[]{:S(2)}) copy-start(f32[1,128]{1,0:T(1,128)S(1)} %get-tuple-element.194.log_ref) | copy-start | bytes 1540
  365.9 34.4 %copy-start.11 = (bf16[256,2048]{1,0:T(8,128)(2,1)S(1)}, bf16[256,2048]{1,0:T(8,128)(2,1)}, u32[]{:S(2)}) copy-start(bf16[256,2048]{1,0:T(8,128)(2,1)} %refs_2_.1) | copy-start | bytes 3145732
  374.5 25.7 %collective-permute-start.1 = (bf16[256,2048]{1,0:T(8,128)(2,1)}, bf16[256,2048]{1,0:T(8,128)(2,1)}, u32[]{:S(2)}, u32[]{:S(2)}) collective-permute-start(bf16[256,2048]{1,0:T(8,128)(2,1)} %dynamic-slice_convert_fusion.3), channel_id=1, source_target_pairs={{0,1},{1,0},{2,3},{3,2},{4,5},{5,4},{6,7},{7,6},{8,9},{9,8},{10,11... | collective-permute-start | bytes 3145736 | tf_op jit(solution)/shard_map/ppermute | solution.py:895
  402.8 24.9 %copy-start.7 = (f32[256,2048]{1,0:T(8,128)}, f32[256,2048]{1,0:T(8,128)S(1)}, u32[]{:S(2)}) copy-start(f32[256,2048]{1,0:T(8,128)S(1)} %get-tuple-element.154) | copy-start | bytes 6291460
  403.1 24.6 %collective-permute-start.2 = (bf16[256,2048]{1,0:T(8,128)(2,1)S(1)}, bf16[256,2048]{1,0:T(8,128)(2,1)S(1)}, u32[]{:S(2)}, u32[]{:S(2)}) collective-permute-start(bf16[256,2048]{1,0:T(8,128)(2,1)S(1)} %multiply_convert_fusion.3), channel_id=1, source_target_pairs={{0,1},{1,0},{2,3},{3,2},{4,5},{5,4},{6,7},{7,6},{8,9},{9,8},{10,11... | collective-permute-start | bytes 3145736 | tf_op jit(solution)/shard_map/ppermute | solution.py:895
  429.3 25.6 %copy-start.27 = (bf16[256,2048]{1,0:T(8,128)(2,1)}, bf16[256,2048]{1,0:T(8,128)(2,1)S(1)}, u32[]{:S(2)}) copy-start(bf16[256,2048]{1,0:T(8,128)(2,1)S(1)} %get-tuple-element.169) | copy-start | bytes 3145732
  480.5 467.3 %reduce-scatter.3.cloned.1.call-start = ((), (), s32[]{:S(2)}) async-start(), calls=%async_computation.5 | async-start | bytes 12255232 | tf_op jit(solution)/shard_map/reduce_scatter | solution.py:933
  504.5 23.8 %collective-permute-start.3 = (bf16[256,2048]{1,0:T(8,128)(2,1)}, bf16[256,2048]{1,0:T(8,128)(2,1)S(1)}, u32[]{:S(2)}, u32[]{:S(2)}) collective-permute-start(bf16[256,2048]{1,0:T(8,128)(2,1)} %dynamic-slice_convert_fusion.2), channel_id=1, source_target_pairs={{0,1},{1,0},{2,3},{3,2},{4,5},{5,4},{6,7},{7,6},{8,9},{9,8},{10,11... | collective-permute-start | bytes 3145736 | tf_op jit(solution)/shard_map/ppermute | solution.py:895
  529.9 27.5 %slice-start.1 = ((s8[6291456]{0:T(1024)(128)(4,1)}), s8[4194304]{0:T(1024)(128)(4,1)S(1)}, s32[]{:S(2)}) async-start(s8[6291456]{0:T(1024)(128)(4,1)} %bitcast.104), calls=%async_computation.8 | async-start | bytes 8388608
  532.1 25.4 %slice-start.2 = ((s8[6291456]{0:T(1024)(128)(4,1)}), s8[2097152]{0:T(1024)(128)(4,1)S(1)}, s32[]{:S(2)}) async-start(s8[6291456]{0:T(1024)(128)(4,1)} %bitcast.104), calls=%async_computation.9 | async-start | bytes 4194304
  532.1 23.8 %collective-permute-start.4 = (bf16[256,2048]{1,0:T(8,128)(2,1)S(1)}, bf16[256,2048]{1,0:T(8,128)(2,1)S(1)}, u32[]{:S(2)}, u32[]{:S(2)}) collective-permute-start(bf16[256,2048]{1,0:T(8,128)(2,1)S(1)} %get-tuple-element.151), channel_id=1, source_target_pairs={{0,1},{1,0},{2,3},{3,2},{4,5},{5,4},{6,7},{7,6},{8,9},{9,8},{10,11... | collective-permute-start | bytes 3145736 | tf_op jit(solution)/shard_map/ppermute | solution.py:895
  556.3 56.8 %collective-permute-start.5 = (bf16[256,2048]{1,0:T(8,128)(2,1)}, bf16[256,2048]{1,0:T(8,128)(2,1)S(1)}, u32[]{:S(2)}, u32[]{:S(2)}) collective-permute-start(bf16[256,2048]{1,0:T(8,128)(2,1)} %dynamic-slice_convert_fusion.1), channel_id=1, source_target_pairs={{0,1},{1,0},{2,3},{3,2},{4,5},{5,4},{6,7},{7,6},{8,9},{9,8},{10,11... | collective-permute-start | bytes 3145736 | tf_op jit(solution)/shard_map/ppermute | solution.py:895
  614.0 21.4 %copy-start.34 = (f32[2048]{0:T(1024)S(1)}, f32[2048]{0:T(1024)}, u32[]{:S(2)}) copy-start(f32[2048]{0:T(1024)} %copy-done.33) | copy-start | bytes 24580
  614.0 21.4 %copy-start.43 = (f32[512]{0:T(512)S(1)}, f32[512]{0:T(512)}, u32[]{:S(2)}) copy-start(f32[512]{0:T(512)} %copy-done.42) | copy-start | bytes 6148
  634.5 27.2 %collective-permute-start.6 = (bf16[256,2048]{1,0:T(8,128)(2,1)}, bf16[256,2048]{1,0:T(8,128)(2,1)}, u32[]{:S(2)}, u32[]{:S(2)}) collective-permute-start(bf16[256,2048]{1,0:T(8,128)(2,1)} %dynamic-slice_convert_fusion), channel_id=1, source_target_pairs={{0,1},{1,0},{2,3},{3,2},{4,5},{5,4},{6,7},{7,6},{8,9},{9,8},{10,11... | collective-permute-start | bytes 3145736 | tf_op jit(solution)/shard_map/ppermute | solution.py:895
  662.5 262.0 %copy-start.12 = (bf16[256,2048]{1,0:T(8,128)(2,1)S(1)}, bf16[256,2048]{1,0:T(8,128)(2,1)}, u32[]{:S(2)}) copy-start(bf16[256,2048]{1,0:T(8,128)(2,1)} %refs_2_.1) | copy-start | bytes 3145732
  662.5 262.0 %copy-start.36 = (f32[256]{0:T(256)S(1)}, f32[256]{0:T(256)}, u32[]{:S(2)}) copy-start(f32[256]{0:T(256)} %add_rsqrt_fusion.1) | copy-start | bytes 3076
  922.3 19.1 %collective-permute-start.7 = (f32[4,128]{0,1:T(8,128)S(1)}, f32[4,128]{0,1:T(8,128)S(1)}, u32[]{:S(2)}, u32[]{:S(2)}) collective-permute-start(f32[4,128]{0,1:T(8,128)S(1)} %slice_bitcast_fusion.2), channel_id=1, source_target_pairs={{0,1},{1,0},{2,3},{3,2},{4,5},{5,4},{6,7},{7,6},{8,9},{9,8},{10,11... | collective-permute-start | bytes 6152 | tf_op jit(solution)/shard_map/ppermute | solution.py:895
  (46 other events, 316.0 us)
Sparse Core Ops, SparseCore 0:
  10.9 139.7 all-gather.7
  153.4 136.1 all-gather.3
  292.5 94.2 all-gather.5
  480.6 125.8 reduce-scatter.4
  611.0 188.9 reduce-scatter.2

commit v4 on v3

--- a/solution.py
+++ b/solution.py
@@ -748,37 +748,52 @@
     )(*arrays)
 
 
-def scatter_kernel(layers, chunks, count, *refs):
-    srcs, out = refs[:count], refs[count]
-    stage, buf1, buf2, buf3, own_sem, cs, cr, ys, yr, zs, zr = refs[count + 1 :]
+def scatter_kernel(layers, chunks, dots, *refs):
+    n_held = max([c[0] for c in chunks if c[3] is None]) + 1
+    srcs, lefts = refs[:n_held], refs[n_held : n_held + dots]
+    rights = refs[n_held + dots : n_held + 2 * dots]
+    sent_ref, out, come_ref = refs[n_held + 2 * dots : n_held + 2 * dots + 3]
+    (stage, sends, buf1, buf2, buf3, own_sem, cs, cr, ys, yr, zs, zr, pair_send,
+     pair_recv) = refs[n_held + 2 * dots + 3 :]
     rows = out.shape[0]
     spot, core, side, layer = placement()
+    turn = lax.axis_index("tensor")
     at = lambda z, y, c: 4 * lax.rem(z + layers, layers) + 2 * y + c
     z_to = [at(layer + k, side, core) for k in range(1, layers)]
     y_to, c_to = at(layer, 1 - side, core), at(layer, side, 1 - core)
-    greet(z_to + [y_to, c_to])
+    barrier = pltpu.get_barrier_semaphore()
+    for partner in z_to + [y_to, c_to]:
+        pl.semaphore_signal(barrier, inc=1, device_id={"dp": partner}, device_id_type=MESH)
+    pl.semaphore_signal(barrier, inc=1, device_id={"tensor": 1 - turn}, device_id_type=MESH)
+    pl.semaphore_wait(barrier, layers + 2)
     number = len(chunks)
     firsts = []
     total = 0
-    for a, lo, width in chunks:
+    for chunk in chunks:
         firsts.append(total)
-        total += width
+        total += chunk[2]
+    pair = pltpu.make_async_remote_copy(
+        src_ref=sent_ref, dst_ref=come_ref, send_sem=pair_send, recv_sem=pair_recv,
+        device_id={"tensor": 1 - turn}, device_id_type=MESH,
+    )
+    pair.start()
 
     def cols(j):
         return slice(firsts[j], firsts[j] + chunks[j][2])
 
     def c_copy(j):
-        a, lo, width = chunks[j]
-        return remote(
-            srcs[a].at[:, 1 - core, :, lo : lo + width], buf1.at[:, :, cols(j)],
-            cs.at[j], cr.at[j], c_to,
-        )
+        a, lo, width, which = chunks[j]
+        if which is None:
+            src = srcs[a].at[:, 1 - core, :, lo : lo + width]
+        else:
+            src = sends.at[j % 3, :, :, 0:width]
+        return remote(src, buf1.at[:, :, cols(j)], cs.at[j], cr.at[j], c_to)
 
     def own_copy(j):
-        a, lo, width = chunks[j]
+        a, lo, width, _ = chunks[j]
         return pltpu.make_async_copy(
             srcs[a].at[:, core, :, lo : lo + width],
-            stage.at[j % 2, :, :, 0:width], own_sem.at[j],
+            stage.at[j % 3, :, :, 0:width], own_sem.at[j],
         )
 
     def y_copy(j, m):
@@ -793,18 +808,44 @@
             z_to[k - 1],
         )
 
-    for j in range(number):
+    def produce(j):
+        a, lo, width, which = chunks[j]
+        if which is None:
+            own_copy(j).start()
+        else:
+            if j >= 3:
+                c_copy(j - 3).wait_send()
+            right = rights[which][:, lo : lo + width]
+
+            wide = 256
+            per = wide // (2 * rows)
+
+            def body(g, _):
+                left = lefts[which][:, pl.ds(pl.multiple_of(g * wide, wide), wide)]
+                both = mm(left, right, 0, 0)
+                for i in range(per):
+                    low_half = both[2 * i * rows : (2 * i + 1) * rows]
+                    high_half = both[(2 * i + 1) * rows : (2 * i + 2) * rows]
+                    mine = jnp.where(core == 0, low_half, high_half)
+                    other = jnp.where(core == 0, high_half, low_half)
+                    stage[j % 3, g * per + i, :, 0:width] = mine.astype(bf16)
+                    sends[j % 3, g * per + i, :, 0:width] = other.astype(bf16)
+                return 0
+
+            lax.fori_loop(0, 2 * layers // per, body, 0)
         c_copy(j).start()
+
     for j in range(min(2, number)):
-        own_copy(j).start()
+        produce(j)
 
     def first(j):
         width = chunks[j][2]
-        own_copy(j).wait()
+        if chunks[j][3] is None:
+            own_copy(j).wait()
         c_copy(j).wait_recv()
 
         def body(b, _):
-            mine = stage[j % 2, b, :, 0:width].astype(f32)
+            mine = stage[j % 3, b, :, 0:width].astype(f32)
             buf1[b, :, cols(j)] = (buf1[b, :, cols(j)].astype(f32) + mine).astype(bf16)
             return 0
 
@@ -812,7 +853,7 @@
         for m in list(range(1, layers)) + [0]:
             y_copy(j, m).start()
         if j + 2 < number:
-            own_copy(j + 2).start()
+            produce(j + 2)
 
     def second(j):
         for m in list(range(1, layers)) + [0]:
@@ -838,40 +879,62 @@
         if 0 <= j - 4 < number:
             third(j - 4)
     for j in range(number):
-        c_copy(j).wait_send()
+        later = j + 3 < number and chunks[j + 3][3] is not None
+        if not later:
+            c_copy(j).wait_send()
         for m in range(layers):
             y_copy(j, m).wait_send()
         for k in range(1, layers):
             z_copy(j, k).wait_send()
-
-
-def scatter_sum(parts, widths, devices, ident, size=512):
-    widths = [w or p.shape[1] for w, p in zip(widths, parts)]
-    rows = parts[0].shape[0] // devices
+    pair.wait()
+
+
+def scatter_sum(held, products, tail, sent, devices, ident, size=512):
+    parts = [held, tail]
+    rows = held.shape[0] // devices
     layers = devices // 4
-    chunks = column_chunks(widths, size, layers)
+    widths = [held.shape[1]] + [w for _, _, w in products] + [tail.shape[1]]
+    chunks = []
+    for a, lo, width in column_chunks(widths, size, 4):
+        if a == 0:
+            chunks.append((0, lo, width, None))
+        elif a <= len(products):
+            chunks.append((a, lo, width, a - 1))
+        else:
+            chunks.append((1, lo, width, None))
     n = len(chunks)
     width = sum(widths)
     widest = max(c[2] for c in chunks)
     sem = lambda *shape: pltpu.SemaphoreType.DMA(shape)
+    hbm, vmem = pl.BlockSpec(memory_space=pl.ANY), pl.BlockSpec(memory_space=pltpu.VMEM)
     return pl.pallas_call(
-        functools.partial(scatter_kernel, layers, chunks, len(parts)),
-        in_specs=[pl.BlockSpec(memory_space=pl.ANY)] * len(parts),
-        out_specs=pl.BlockSpec(memory_space=pltpu.VMEM),
-        out_shape=jax.ShapeDtypeStruct((rows, width), f32),
+        functools.partial(scatter_kernel, layers, chunks, len(products)),
+        in_specs=[hbm] * 2 + [vmem] * (2 * len(products)) + [hbm],
+        out_specs=[vmem, hbm],
+        out_shape=[
+            jax.ShapeDtypeStruct((rows, width), f32),
+            jax.ShapeDtypeStruct(sent.shape, sent.dtype),
+        ],
         scratch_shapes=[
-            pltpu.VMEM((2, 2 * layers, rows, widest), bf16),
+            pltpu.VMEM((3, 2 * layers, rows, widest), bf16),
+            pltpu.VMEM((3, 2 * layers, rows, widest), bf16),
             pltpu.VMEM((2 * layers, rows, width), bf16),
             pltpu.VMEM((layers, rows, width), bf16),
             pltpu.VMEM((layers - 1, rows, width), bf16),
             sem(n), sem(n), sem(n), sem(n, layers), sem(n, layers),
             sem(n, layers - 1), sem(n, layers - 1),
+            pltpu.SemaphoreType.DMA, pltpu.SemaphoreType.DMA,
         ],
         compiler_params=pltpu.CompilerParams(
-            collective_id=ident, has_side_effects=True, vmem_limit_bytes=52 * 1024 * 1024
+            collective_id=ident, has_side_effects=True, vmem_limit_bytes=61 * 1024 * 1024
         ),
         name="scatter_sum",
-    )(*[p.reshape(devices // 2, 2, rows, p.shape[1]) for p in parts])
+    )(
+        *[p.reshape(devices // 2, 2, rows, p.shape[1]) for p in parts],
+        *[p[0] for p in products],
+        *[p[1] for p in products],
+        sent,
+    )
 
 
 EXTRA = 128
@@ -1021,14 +1084,16 @@
     gated, *saved = mixer_forward(*mixer_args)
     hidden = inputs + pair_scatter(dot(gated, out_t, 1, 1))
     normed_ffn = low(hidden * rms_scale(hidden) * full_ffn)
+    normed_ffn, down_t = lax.optimization_barrier((normed_ffn, down_t))
     seq_ffn = pair_gather(normed_ffn)
+    grad_inner = dot(seq_cot, down_t)
+    seq_ffn, grad_inner = lax.optimization_barrier((seq_ffn, grad_inner))
 
     gate_act = dot(seq_ffn, gate_weight)
     up_act = dot(seq_ffn, up_weight)
     sigmoid_gate = jax.nn.sigmoid(gate_act)
     silu_gate = gate_act * sigmoid_gate
     inner = low(silu_gate * up_act)
-    grad_inner = dot(seq_cot, down_t)
     grad_gate_act = low(
         grad_inner * up_act * sigmoid_gate * (1.0 + gate_act * (1.0 - sigmoid_gate))
     )
@@ -1040,18 +1105,22 @@
     down_piece = scatter_rows(grad_down)
     grad_seq_ffn = dot(grad_gate_act, gate_weight, 1, 1) + dot(grad_up_act, up_weight, 1, 1)
     kept_ffn, sent_ffn = pair_halves(grad_seq_ffn)
-    sent_ffn, grad_gate_act, grad_up_act, inner = lax.optimization_barrier(
-        (sent_ffn, grad_gate_act, grad_up_act, inner)
-    )
-    grad_normed_ffn = kept_ffn + pair_swap(sent_ffn).astype(f32)
+    sent_ffn, inner = lax.optimization_barrier((sent_ffn, inner))
+    kept_out, sent_out = pair_halves(dot(inner, down_t, 1, 1))
+    come_ffn, sent_out = lax.optimization_barrier((pair_swap(sent_ffn), sent_out))
+    grad_normed_ffn = kept_ffn + come_ffn.astype(f32)
+    grad_hidden_norm, grad_gain_ffn = norm_back(hidden, full_ffn, grad_normed_ffn)
+    grad_hidden = cotangent.astype(f32) + grad_hidden_norm
+    sent_branch, grad_gate_act, grad_up_act = lax.optimization_barrier(
+        (low(grad_hidden), grad_gate_act, grad_up_act)
+    )
+    seq_grad_branch = pair_gather(sent_branch)
     grad_gate_w = low(dot(seq_ffn, grad_gate_act, 0, 0))
     grad_up_w = low(dot(seq_ffn, grad_up_act, 0, 0))
+    seq_grad_branch, grad_gate_w, grad_up_w, sent_out = lax.optimization_barrier(
+        (seq_grad_branch, grad_gate_w, grad_up_w, sent_out)
+    )
     gate_piece = scatter_rows(grad_gate_w)
-    kept_out, sent_out = pair_halves(dot(inner, down_t, 1, 1))
-    grad_hidden_norm, grad_gain_ffn = norm_back(hidden, full_ffn, grad_normed_ffn)
-    grad_hidden = cotangent.astype(f32) + grad_hidden_norm
-    seq_grad_branch = pair_gather(low(grad_hidden))
-    seq_grad_branch, sent_out = lax.optimization_barrier((seq_grad_branch, sent_out))
     come_out = pair_swap(sent_out)
 
     grad_gated = dot(seq_grad_branch, out_t)
@@ -1062,11 +1131,7 @@
     result = low(hidden + kept_out + come_out.astype(f32))
     grad_seq_in = dot(grad_pre, proj, 1, 1)
     kept_in, sent_in = pair_halves(grad_seq_in)
-    sent_in, grad_pre, gated = lax.optimization_barrier((sent_in, grad_pre, gated))
-    come_in = pair_swap(sent_in)
-    grad_proj = low(dot(seq_in, grad_pre, 0, 0))
-    grad_out_t = low(dot(seq_grad_branch, gated, 0, 0))
-    come_in, grad_proj, grad_out_t = lax.optimization_barrier((come_in, grad_proj, grad_out_t))
+    extra = dot(seq_in, grad_pre[:, extra_at:], 0, 0)
     by_device = lambda g, piece: g.reshape(tap_count, heads, devices, piece)
     grad_flat = jnp.concatenate(
         [by_device(grad_fq, piece_q), by_device(grad_fk, piece_q), by_device(grad_fv, piece_v)],
@@ -1087,12 +1152,14 @@
         axis=1,
     )
     grad_tiny = jnp.concatenate(
-        [grad_proj[:, extra_at : extra_at + 2 * heads], grad_flat, low(columns)], axis=1
+        [low(extra[:, : 2 * heads]), grad_flat, low(columns)], axis=1
     )
     grad_tiny = jnp.pad(grad_tiny, ((0, 0), (0, EXTRA - grad_tiny.shape[1])))
-    pieces = scatter_sum(
-        (grad_up_w, grad_proj, grad_out_t, grad_tiny), (None, extra_at, None, None), devices, 1
-    )
+    products = (
+        (seq_in, grad_pre, extra_at),
+        (seq_grad_branch, gated, gated.shape[1]),
+    )
+    pieces, come_in = scatter_sum(grad_up_w, products, grad_tiny, sent_in, devices, 1)
     ffn_width = grad_up_w.shape[1]
     up_piece, pieces = pieces[:, :ffn_width], pieces[:, ffn_width:]
     grad_normed_in = kept_in + come_in.astype(f32)

time: 962 us -> 954 us (level)
  Pallas kernels: 620 us -> 639 us
  matrix products: 170 us -> 155 us
  waiting for transfers between devices: 61.2 us -> 48.8 us
    pallas_call x1, Pallas kernels: 259 us -> 280 us  [scatter_sum(): pl.pallas_call(functools.partial(scatter_kernel, layers, chunks, len(prod...]
    dot_general x15 -> x14, matrix products: 170 us -> 155 us  [dot(): lax.dot_general(a, b, (((ca,), (cb,)), ((), ())), preferred_element_type=...]
    ppermute x8 -> x7, waiting for transfers between devices: 61.1 us -> 48.7 us  [pair_swap(): return lax.ppermute(values, 'tensor', [(0, 1), (1, 0)])]
  transfers between devices with their start and end apart: 13 -> 12, of which waited for: 4 -> 4; matrix products, arithmetic and copies ran while one was open for 22% -> 21% of each run, Pallas kernels for 65% -> 67%
where the time goes in v4:
time: 954 us; the launch traced here: 949 us
  Pallas kernels  639 us (67%)
  matrix products  155 us (16%)
  waiting for transfers between devices  48.8 us (5%)
  local copies, waits for them, and re-layouts  41.2 us (4%)
  other arithmetic  38.5 us (4%)
  between operations  15.5 us (2%)
  starting transfers between devices  11.7 us (1%)
    pallas_call x1, Pallas kernels, scatter_sum(): pl.pallas_call(functools.partial(scatter_kernel, layers, chunks, len(prod...  280 us
    pallas_call x1, Pallas kernels, gather_all(): pl.pallas_call(functools.partial(gather_kernel, layers, chunks, len(shard...  275 us
    dot_general x14, matrix products, dot(): lax.dot_general(a, b, (((ca,), (cb,)), ((), ())), preferred_element_type=...  155 us
    pallas_call x1, Pallas kernels, mixer_backward(): pl.pallas_call(functools.partial(bwd_kernel, heads), grid=(heads,), in_sp...  49.4 us
    ppermute x7, waiting for transfers between devices, pair_swap(): return lax.ppermute(values, 'tensor', [(0, 1), (1, 0)])  48.7 us
    pallas_call x1, Pallas kernels, mixer_forward(): pl.pallas_call(functools.partial(fwd_kernel, heads), grid=(heads,), in_sp...  34.8 us
  transfers between devices with their start and end apart: 12, of which 4 were waited for; matrix products, arithmetic and copies ran while one was open for 21% of the time, Pallas kernels for 67%

profile of v4, /device:TPU:0, one launch (start us, length us, event | category | flops | bytes accessed | tf_op | source)
XLA Modules:
  0.0 949.4 jit_solution(12292858110900789816)
XLA Ops:
  12.0 2.9 collective-permute-start
  23.4 274.6 %gather_rows.1 = (bf16[2048,4736]{1,0:T(8,128)(2,1)}, bf16[2048,1536]{1,0:T(8,128)(2,1)}, bf16[512,2048]{1,0:T(8,128)(2,1)}, bf16[512,2048]{1,0:T(8,128)(2,1)}) custom-call(bf16[128,4736]{1,0:T(8,128)(2,1)} %copy-done.21, bf16[128,1536]{1,0:T(8,128)(2,1)} %bitcast.94, bf16[256,2048]{1,0:T(8,128)(2,1)} %refs_2_.1, bf16[256,2048]{1,0:T(8,128)(2,1)} %refs_3_.1), custom_call_target="tpu_custom_call" | custom-call | tf_op jit(solution)/shard_map/gather_rows/pallas_call | solution.py:735
  312.6 18.0 %fusion.32.q_ref.k_ref.v_ref.g_ref.bd_ref = f32[512,4736]{1,0:T(8,128)} fusion(bf16[512,2048]{1,0:T(8,128)(2,1)S(1)} %fusion.3.refs_2_, bf16[2048,4736]{1,0:T(8,128)(2,1)} %get-tuple-element.58), kind=kOutput, calls=%fused_computation.116 | convolution fusion | flops 9932111872 | bytes 31195136 | tf_op jit(solution)/shard_map/dot_general | solution.py:983
  330.6 34.8 %mixer_forward.1 = (bf16[512,1536]{1,0:T(8,128)(2,1)S(1)}, bf16[3,512,256]{2,1,0:T(8,128)(2,1)S(1)}, bf16[512,1536]{1,0:T(8,128)(2,1)S(1)}, f32[512,1536]{1,0:T(8,128)}, f32[3,1,256,512]{3,2,1,0:T(8,128)}) custom-call(s32[1]{0:T(128)S(6)} %copy.115.len_ref, f32[512,4736]{1,0:T(8,128)} %fusion.32.q_ref.k_ref.v_ref.g_ref.bd_ref, ...), custom_call_target="tpu_custom_call" | custom-call | tf_op jit(solution)/shard_map/mixer_forward/pallas_call | solution.py:437
  365.4 6.2 fusion.33
  375.4 24.4 %collective-permute-done.1 = bf16[256,2048]{1,0:T(8,128)(2,1)} collective-permute-done((bf16[256,2048]{1,0:T(8,128)(2,1)}, bf16[256,2048]{1,0:T(8,128)(2,1)}, u32[]{:S(2)}, u32[]{:S(2)}) %collective-permute-start.1) | collective-permute-done | bytes 1048608 | tf_op jit(solution)/shard_map/ppermute | solution.py:958
  399.9 3.1 multiply_reduce_fusion.2
  406.1 12.6 %fusion.34 = f32[512,2816]{1,0:T(8,128)} fusion(bf16[512,2048]{1,0:T(8,128)(2,1)} %get-tuple-element.62, bf16[2048,2816]{0,1:T(8,128)(2,1)} %all-gather.4.cloned.1.call-done), kind=kOutput, calls=%fused_computation.118 | convolution fusion | flops 5905580032 | bytes 19398656 | tf_op jit(solution)/shard_map/dot_general | solution.py:983
  418.7 10.7 %collective-permute-done.2 = bf16[256,2048]{1,0:T(8,128)(2,1)S(1)} collective-permute-done((bf16[256,2048]{1,0:T(8,128)(2,1)S(1)}, bf16[256,2048]{1,0:T(8,128)(2,1)S(1)}, u32[]{:S(2)}, u32[]{:S(2)}) %collective-permute-start.2) | collective-permute-done | bytes 1048608 | tf_op jit(solution)/shard_map/ppermute | solution.py:958
  431.2 12.9 %fusion.35 = f32[512,2816]{1,0:T(8,128)} fusion(bf16[512,2048]{1,0:T(8,128)(2,1)} %pad_maximum_fusion, bf16[2048,2816]{1,0:T(8,128)(2,1)} %all-gather.8.cloned.1.call-done), kind=kOutput, calls=%fused_computation.119 | convolution fusion | flops 5905580032 | bytes 19398656 | tf_op jit(solution)/shard_map/dot_general | solution.py:983
  444.1 16.4 %multiply_convert_fusion = (bf16[512,2816]{1,0:T(8,128)(2,1)S(1)}, bf16[512,2816]{1,0:T(8,128)(2,1)}, bf16[512,2816]{1,0:T(8,128)(2,1)}) fusion(f32[512,2816]{1,0:T(8,128)} %fusion.35, f32[512,2816]{1,0:T(8,128)} %fusion.34, bf16[512,2048]{1,0:T(8,128)(2,1)} %pad_maximum_fusion, bf16[2048,2816]{1,0:T(8,128)(2,1)} %all-gather.6.cloned.1.call-done), kind=kOutput, calls=%fused_computation.3 | convolution fusion | flops 5927206912 | bytes 33816576 | tf_op jit(solution)/shard_map/dot_general | solution.py:983
  462.1 9.0 convolution_convert_fusion.2
  471.3 10.2 %fusion.36 = f32[512,2048]{1,0:T(8,128)S(1)} fusion(bf16[512,2816]{1,0:T(8,128)(2,1)} %get-tuple-element.76, bf16[2048,2816]{1,0:T(8,128)(2,1)} %all-gather.8.cloned.1.call-done), kind=kOutput, calls=%fused_computation.120 | convolution fusion | flops 5905580032 | bytes 18612224 | tf_op jit(solution)/shard_map/dot_general | solution.py:983
  481.5 10.0 %convolution_add_fusion = f32[512,2048]{1,0:T(8,128)S(1)} fusion(f32[512,2048]{1,0:T(8,128)S(1)} %fusion.36, bf16[512,2816]{1,0:T(8,128)(2,1)S(1)} %copy-done.41, bf16[2048,2816]{1,0:T(8,128)(2,1)} %all-gather.6.cloned.1.call-done), kind=kOutput, calls=%fused_computation.18 | convolution fusion | flops 5906628608 | bytes 22806528 | tf_op jit(solution)/shard_map/dot_general | solution.py:983
  493.1 9.5 %fusion.37 = f32[512,2048]{1,0:T(8,128)S(1)} fusion(bf16[512,2816]{1,0:T(8,128)(2,1)S(1)} %copy-done.44, bf16[2048,2816]{0,1:T(8,128)(2,1)} %all-gather.4.cloned.1.call-done), kind=kOutput, calls=%fused_computation.121 | convolution fusion | flops 5905580032 | bytes 18612224 | tf_op jit(solution)/shard_map/dot_general | solution.py:983
  503.7 11.9 %collective-permute-done.3 = bf16[256,2048]{1,0:T(8,128)(2,1)S(1)} collective-permute-done((bf16[256,2048]{1,0:T(8,128)(2,1)S(1)}, bf16[256,2048]{1,0:T(8,128)(2,1)S(1)}, u32[]{:S(2)}, u32[]{:S(2)}) %collective-permute-start.3) | collective-permute-done | bytes 1048608 | tf_op jit(solution)/shard_map/ppermute | solution.py:958
  520.0 8.9 convolution_convert_fusion.1
  528.9 11.3 %convolution_convert_fusion = bf16[2048,2816]{1,0:T(8,128)(2,1)} fusion(bf16[512,2048]{1,0:T(8,128)(2,1)} %pad_maximum_fusion, bf16[512,2816]{1,0:T(8,128)(2,1)} %get-tuple-element.77), kind=kOutput, calls=%fused_computation | convolution fusion | flops 5911347200 | bytes 16515072 | tf_op jit(solution)/shard_map/dot_general | solution.py:983
  546.9 8.2 convolution_convert_fusion.3.dg_ref
  555.1 49.4 %mixer_backward.1 = (bf16[512,4736]{1,0:T(8,128)(2,1)}, f32[4,768]{1,0:T(4,128)S(1)}, f32[4,768]{1,0:T(4,128)S(1)}, f32[4,1536]{1,0:T(4,128)S(1)}, f32[8,512]{1,0:T(8,128)S(1)}, /*index=5*/f32[8,128]{1,0:T(8,128)S(1)}) custom-call(s32[1]{0:T(128)S(6)} %copy.115.len_ref, f32[512,4736]{1,0:T(8,128)} %fusion.32.q_ref.k_ref.v_ref.g_ref.bd_ref, ...), custom_call_target="tpu_custom_call" | custom-call | tf_op jit(solution)/shard_map/mixer_backward/pallas_call | solution.py:473
  608.6 19.2 %fusion.4 = (bf16[2048]{0:T(1024)(128)(2,1)S(1)}, f32[512,2048]{1,0:T(8,128)}) fusion(bf16[512,2048]{1,0:T(8,128)(2,1)S(1)} %copy-done.12, f32[512]{0:T(512)S(1)} %copy-done.28, bf16[512,4736]{1,0:T(8,128)(2,1)} %get-tuple-element.83.refs_4_, bf16[2048,4736]{1,0:T(8,128)(2,1)} %get-tuple-element.58), kind=kOutput, calls=%fused_computation.13 | convolution fusion | flops 9936304128 | bytes 30545920 | tf_op jit(solution)/shard_map/dot_general | solution.py:983
  629.2 2.7 dynamic-slice_convert_fusion.refs_6_
  631.9 280.0 %scatter_sum.1 = (f32[128,9088]{1,0:T(8,128)}, bf16[256,2048]{1,0:T(8,128)(2,1)}) custom-call(bf16[8,2,128,2816]{3,2,1,0:T(8,128)(2,1)} %bitcast.89, bf16[8,2,128,128]{3,2,1,0:T(8,128)(2,1)} %bitcast.91, bf16[512,2048]{1,0:T(8,128)(2,1)} %copy-done.9, bf16[512,2048]{1,0:T(8,128)(2,1)} %pad_maximum_fusion.1.refs_3_, ...), custom_call_target="tpu_custom_call" | custom-call | tf_op jit(solution)/shard_map/scatter_sum/pallas_call | solution.py:910
  922.5 3.2 add_convert_fusion
  (235 shorter events, 83.6 us)
Async XLA Ops:
  7.2 397.4 %all-gather.4.cloned.1.call-start = ((), (), s32[]{:S(2)}) async-start(), calls=%async_computation.2 | async-start | bytes 12255232 | tf_op jit(solution)/shard_map/all_gather | solution.py:992
  9.9 421.3 %all-gather.8.cloned.1.call-start = ((), (), s32[]{:S(2)}) async-start(), calls=%async_computation.4 | async-start | bytes 12255232 | tf_op jit(solution)/shard_map/all_gather | solution.py:992
  10.9 433.3 %all-gather.6.cloned.1.call-start = ((), (), s32[]{:S(2)}) async-start(), calls=%async_computation.3 | async-start | bytes 12255232 | tf_op jit(solution)/shard_map/all_gather | solution.py:992
  11.9 925.7 %reduce-scatter.5.cloned.1.call-start = ((), (), s32[]{:S(2)}) async-start(), calls=%async_computation.6 | async-start | bytes 12255232 | tf_op jit(solution)/shard_map/reduce_scatter | solution.py:996
  12.0 9.6 %collective-permute-start = (f32[1,144]{1,0:T(1,128)S(1)}, f32[1,144]{1,0:T(1,128)S(1)}, u32[]{:S(2)}, u32[]{:S(2)}) collective-permute-start(f32[1,144]{1,0:T(1,128)S(1)} %bitcast.101), channel_id=1, source_target_pairs={{0,1},{1,0},{2,3},{3,2},{4,5},{5,4},{6,7},{7,6},{8,9},{9,8},{10,11... | collective-permute-start | bytes 1736 | tf_op jit(solution)/shard_map/ppermute | solution.py:958
  15.9 314.6 %copy-start.2 = (f32[1,128]{1,0:T(1,128)}, f32[1,128]{1,0:T(1,128)S(1)}, u32[]{:S(2)}) copy-start(f32[1,128]{1,0:T(1,128)S(1)} %get-tuple-element.203.bias_ref) | copy-start | bytes 1540
  15.9 314.6 %copy-start.4 = (f32[1,128]{1,0:T(1,128)}, f32[1,128]{1,0:T(1,128)S(1)}, u32[]{:S(2)}) copy-start(f32[1,128]{1,0:T(1,128)S(1)} %get-tuple-element.204.log_ref) | copy-start | bytes 1540
  310.4 20.1 %copy-start.27 = (f32[512]{0:T(512)}, f32[512]{0:T(512)S(1)}, u32[]{:S(2)}) copy-start(f32[512]{0:T(512)S(1)} %add_rsqrt_fusion) | copy-start | bytes 6148
  312.6 18.0 %copy-start.9 = (bf16[512,2048]{1,0:T(8,128)(2,1)}, bf16[512,2048]{1,0:T(8,128)(2,1)S(1)}, u32[]{:S(2)}) copy-start(bf16[512,2048]{1,0:T(8,128)(2,1)S(1)} %fusion.3.refs_2_) | copy-start | bytes 6291460
  365.4 34.4 %copy-start.10 = (bf16[256,2048]{1,0:T(8,128)(2,1)S(1)}, bf16[256,2048]{1,0:T(8,128)(2,1)}, u32[]{:S(2)}) copy-start(bf16[256,2048]{1,0:T(8,128)(2,1)} %refs_2_.1) | copy-start | bytes 3145732
  373.9 25.9 %collective-permute-start.1 = (bf16[256,2048]{1,0:T(8,128)(2,1)}, bf16[256,2048]{1,0:T(8,128)(2,1)}, u32[]{:S(2)}, u32[]{:S(2)}) collective-permute-start(bf16[256,2048]{1,0:T(8,128)(2,1)} %dynamic-slice_convert_fusion.3), channel_id=1, source_target_pairs={{0,1},{1,0},{2,3},{3,2},{4,5},{5,4},{6,7},{7,6},{8,9},{9,8},{10,11... | collective-permute-start | bytes 3145736 | tf_op jit(solution)/shard_map/ppermute | solution.py:958
  404.6 24.9 %collective-permute-start.2 = (bf16[256,2048]{1,0:T(8,128)(2,1)S(1)}, bf16[256,2048]{1,0:T(8,128)(2,1)S(1)}, u32[]{:S(2)}, u32[]{:S(2)}) collective-permute-start(bf16[256,2048]{1,0:T(8,128)(2,1)S(1)} %multiply_convert_fusion.3), channel_id=1, source_target_pairs={{0,1},{1,0},{2,3},{3,2},{4,5},{5,4},{6,7},{7,6},{8,9},{9,8},{10,11... | collective-permute-start | bytes 3145736 | tf_op jit(solution)/shard_map/ppermute | solution.py:958
  444.1 18.0 %copy-start.38 = (bf16[512,2048]{1,0:T(8,128)(2,1)S(1)}, bf16[512,2048]{1,0:T(8,128)(2,1)}, u32[]{:S(2)}) copy-start(bf16[512,2048]{1,0:T(8,128)(2,1)} %get-tuple-element.62) | copy-start | bytes 6291460
  471.2 469.2 %reduce-scatter.3.cloned.1.call-start = ((), (), s32[]{:S(2)}) async-start(), calls=%async_computation.5 | async-start | bytes 12255232 | tf_op jit(solution)/shard_map/reduce_scatter | solution.py:996
  481.5 11.6 %copy-start.44 = (bf16[512,2816]{1,0:T(8,128)(2,1)S(1)}, bf16[512,2816]{1,0:T(8,128)(2,1)}, u32[]{:S(2)}) copy-start(bf16[512,2816]{1,0:T(8,128)(2,1)} %copy-done.43) | copy-start | bytes 8650756
  491.6 24.0 %collective-permute-start.3 = (bf16[256,2048]{1,0:T(8,128)(2,1)S(1)}, bf16[256,2048]{1,0:T(8,128)(2,1)S(1)}, u32[]{:S(2)}, u32[]{:S(2)}) collective-permute-start(bf16[256,2048]{1,0:T(8,128)(2,1)S(1)} %dynamic-slice_convert_fusion.2), channel_id=1, source_target_pairs={{0,1},{1,0},{2,3},{3,2},{4,5},{5,4},{6,7},{7,6},{8,9},{9,8},{10,11... | collective-permute-start | bytes 3145736 | tf_op jit(solution)/shard_map/ppermute | solution.py:958
  502.6 13.8 %copy-start.18 = (f32[512,2048]{1,0:T(8,128)}, f32[512,2048]{1,0:T(8,128)S(1)}, u32[]{:S(2)}) copy-start(f32[512,2048]{1,0:T(8,128)S(1)} %fusion.37) | copy-start | bytes 12582916
  502.6 13.0 %copy-start.7 = (f32[256,2048]{1,0:T(8,128)S(1)}, f32[256,2048]{1,0:T(8,128)}, u32[]{:S(2)}) copy-start(f32[256,2048]{1,0:T(8,128)} %copy-done.6) | copy-start | bytes 6291460
  503.7 12.7 %copy-start.16 = (bf16[256,2048]{1,0:T(8,128)(2,1)S(1)}, bf16[256,2048]{1,0:T(8,128)(2,1)}, u32[]{:S(2)}) copy-start(bf16[256,2048]{1,0:T(8,128)(2,1)} %refs_3_.1) | copy-start | bytes 3145732
  518.6 23.2 %collective-permute-start.4 = (bf16[256,2048]{1,0:T(8,128)(2,1)S(1)}, bf16[256,2048]{1,0:T(8,128)(2,1)}, u32[]{:S(2)}, u32[]{:S(2)}) collective-permute-start(bf16[256,2048]{1,0:T(8,128)(2,1)S(1)} %get-tuple-element.75), channel_id=1, source_target_pairs={{0,1},{1,0},{2,3},{3,2},{4,5},{5,4},{6,7},{7,6},{8,9},{9,8},{10,11... | collective-permute-start | bytes 3145736 | tf_op jit(solution)/shard_map/ppermute | solution.py:958
  545.5 60.6 %collective-permute-start.5 = (bf16[256,2048]{1,0:T(8,128)(2,1)}, bf16[256,2048]{1,0:T(8,128)(2,1)S(1)}, u32[]{:S(2)}, u32[]{:S(2)}) collective-permute-start(bf16[256,2048]{1,0:T(8,128)(2,1)} %dynamic-slice_convert_fusion.1), channel_id=1, source_target_pairs={{0,1},{1,0},{2,3},{3,2},{4,5},{5,4},{6,7},{7,6},{8,9},{9,8},{10,11... | collective-permute-start | bytes 3145736 | tf_op jit(solution)/shard_map/ppermute | solution.py:958
  631.9 283.3 %copy-start.11 = (bf16[256,2048]{1,0:T(8,128)(2,1)S(1)}, bf16[256,2048]{1,0:T(8,128)(2,1)}, u32[]{:S(2)}) copy-start(bf16[256,2048]{1,0:T(8,128)(2,1)} %refs_2_.1) | copy-start | bytes 3145732
  631.9 283.3 %copy-start.26 = (f32[2048]{0:T(1024)S(1)}, f32[2048]{0:T(1024)}, u32[]{:S(2)}) copy-start(f32[2048]{0:T(1024)} %copy-done.25) | copy-start | bytes 24580
  912.8 21.2 %collective-permute-start.6 = (f32[4,128]{0,1:T(8,128)S(1)}, f32[4,128]{0,1:T(8,128)S(1)}, u32[]{:S(2)}, u32[]{:S(2)}) collective-permute-start(f32[4,128]{0,1:T(8,128)S(1)} %slice_bitcast_fusion.2), channel_id=1, source_target_pairs={{0,1},{1,0},{2,3},{3,2},{4,5},{5,4},{6,7},{7,6},{8,9},{9,8},{10,11... | collective-permute-start | bytes 6152 | tf_op jit(solution)/shard_map/ppermute | solution.py:958
  (33 other events, 153.3 us)
Sparse Core Ops, SparseCore 0:
  10.8 145.4 all-gather.3
  159.1 124.2 all-gather.7
  286.3 94.4 all-gather.5
  471.3 125.8 reduce-scatter.4
  601.7 203.7 reduce-scatter.2

commit v5 on v4

--- a/solution.py
+++ b/solution.py
@@ -724,7 +724,7 @@
     return marked
 
 
-def gather_all(shards, pairs, devices, ident, size=512, share=1 / 6):
+def gather_all(shards, pairs, devices, ident, size=1600, share=0):
     rows = shards[0].shape[0]
     layers = devices // 4
     chunks = mark_early(column_chunks([s.shape[1] for s in shards], size, layers), share)

time: 954 us -> 900 us (0.943)
  Pallas kernels: 639 us -> 581 us
    pallas_call x1, Pallas kernels: 275 us -> 218 us  [gather_all(): pl.pallas_call(functools.partial(gather_kernel, layers, chunks, len(shard...]
  transfers between devices with their start and end apart: 12 -> 12, of which waited for: 4 -> 4; matrix products, arithmetic and copies ran while one was open for 21% -> 22% of each run, Pallas kernels for 67% -> 65%
where the time goes in v5:
time: 900 us; the launch traced here: 891 us
  Pallas kernels  581 us (65%)
  matrix products  155 us (17%)
  waiting for transfers between devices  47.1 us (5%)
  local copies, waits for them, and re-layouts  41.1 us (5%)
  other arithmetic  38.5 us (4%)
  between operations  15.7 us (2%)
  starting transfers between devices  12.8 us (1%)
    pallas_call x1, Pallas kernels, scatter_sum(): pl.pallas_call(functools.partial(scatter_kernel, layers, chunks, len(prod...  279 us
    pallas_call x1, Pallas kernels, gather_all(): pl.pallas_call(functools.partial(gather_kernel, layers, chunks, len(shard...  218 us
    dot_general x14, matrix products, dot(): lax.dot_general(a, b, (((ca,), (cb,)), ((), ())), preferred_element_type=...  155 us
    pallas_call x1, Pallas kernels, mixer_backward(): pl.pallas_call(functools.partial(bwd_kernel, heads), grid=(heads,), in_sp...  49.3 us
    ppermute x7, waiting for transfers between devices, pair_swap(): return lax.ppermute(values, 'tensor', [(0, 1), (1, 0)])  47 us
    pallas_call x1, Pallas kernels, mixer_forward(): pl.pallas_call(functools.partial(fwd_kernel, heads), grid=(heads,), in_sp...  34.8 us
  transfers between devices with their start and end apart: 12, of which 4 were waited for; matrix products, arithmetic and copies ran while one was open for 22% of the time, Pallas kernels for 65%

profile of v5, /device:TPU:0, one launch (start us, length us, event | category | flops | bytes accessed | tf_op | source)
XLA Modules:
  0.0 891.1 jit_solution(18140711622511265916)
XLA Ops:
  12.0 2.9 collective-permute-start
  23.4 217.8 %gather_rows.1 = (bf16[2048,4736]{1,0:T(8,128)(2,1)}, bf16[2048,1536]{1,0:T(8,128)(2,1)}, bf16[512,2048]{1,0:T(8,128)(2,1)}, bf16[512,2048]{1,0:T(8,128)(2,1)}) custom-call(bf16[128,4736]{1,0:T(8,128)(2,1)} %copy-done.21, bf16[128,1536]{1,0:T(8,128)(2,1)} %bitcast.94, bf16[256,2048]{1,0:T(8,128)(2,1)} %refs_2_.1, bf16[256,2048]{1,0:T(8,128)(2,1)} %refs_3_.1), custom_call_target="tpu_custom_call" | custom-call | tf_op jit(solution)/shard_map/gather_rows/pallas_call | solution.py:735
  255.8 17.9 %fusion.32.q_ref.k_ref.v_ref.g_ref.bd_ref = f32[512,4736]{1,0:T(8,128)} fusion(bf16[512,2048]{1,0:T(8,128)(2,1)S(1)} %fusion.3.refs_2_, bf16[2048,4736]{1,0:T(8,128)(2,1)} %get-tuple-element.58), kind=kOutput, calls=%fused_computation.116 | convolution fusion | flops 9932111872 | bytes 31195136 | tf_op jit(solution)/shard_map/dot_general | solution.py:983
  273.8 34.8 %mixer_forward.1 = (bf16[512,1536]{1,0:T(8,128)(2,1)S(1)}, bf16[3,512,256]{2,1,0:T(8,128)(2,1)S(1)}, bf16[512,1536]{1,0:T(8,128)(2,1)S(1)}, f32[512,1536]{1,0:T(8,128)}, f32[3,1,256,512]{3,2,1,0:T(8,128)}) custom-call(s32[1]{0:T(128)S(6)} %copy.115.len_ref, f32[512,4736]{1,0:T(8,128)} %fusion.32.q_ref.k_ref.v_ref.g_ref.bd_ref, ...), custom_call_target="tpu_custom_call" | custom-call | tf_op jit(solution)/shard_map/mixer_forward/pallas_call | solution.py:437
  308.6 6.2 fusion.33
  318.7 24.1 %collective-permute-done.1 = bf16[256,2048]{1,0:T(8,128)(2,1)} collective-permute-done((bf16[256,2048]{1,0:T(8,128)(2,1)}, bf16[256,2048]{1,0:T(8,128)(2,1)}, u32[]{:S(2)}, u32[]{:S(2)}) %collective-permute-start.1) | collective-permute-done | bytes 1048608 | tf_op jit(solution)/shard_map/ppermute | solution.py:958
  342.8 3.2 multiply_reduce_fusion.2
  349.2 12.8 %fusion.34 = f32[512,2816]{1,0:T(8,128)} fusion(bf16[512,2048]{1,0:T(8,128)(2,1)} %get-tuple-element.62, bf16[2048,2816]{0,1:T(8,128)(2,1)} %all-gather.4.cloned.1.call-done), kind=kOutput, calls=%fused_computation.118 | convolution fusion | flops 5905580032 | bytes 19398656 | tf_op jit(solution)/shard_map/dot_general | solution.py:983
  362.0 10.2 %collective-permute-done.2 = bf16[256,2048]{1,0:T(8,128)(2,1)S(1)} collective-permute-done((bf16[256,2048]{1,0:T(8,128)(2,1)S(1)}, bf16[256,2048]{1,0:T(8,128)(2,1)S(1)}, u32[]{:S(2)}, u32[]{:S(2)}) %collective-permute-start.2) | collective-permute-done | bytes 1048608 | tf_op jit(solution)/shard_map/ppermute | solution.py:958
  374.0 12.9 %fusion.35 = f32[512,2816]{1,0:T(8,128)} fusion(bf16[512,2048]{1,0:T(8,128)(2,1)} %pad_maximum_fusion, bf16[2048,2816]{1,0:T(8,128)(2,1)} %all-gather.8.cloned.1.call-done), kind=kOutput, calls=%fused_computation.119 | convolution fusion | flops 5905580032 | bytes 19398656 | tf_op jit(solution)/shard_map/dot_general | solution.py:983
  386.9 16.4 %multiply_convert_fusion = (bf16[512,2816]{1,0:T(8,128)(2,1)S(1)}, bf16[512,2816]{1,0:T(8,128)(2,1)}, bf16[512,2816]{1,0:T(8,128)(2,1)}) fusion(f32[512,2816]{1,0:T(8,128)} %fusion.35, f32[512,2816]{1,0:T(8,128)} %fusion.34, bf16[512,2048]{1,0:T(8,128)(2,1)} %pad_maximum_fusion, bf16[2048,2816]{1,0:T(8,128)(2,1)} %all-gather.6.cloned.1.call-done), kind=kOutput, calls=%fused_computation.3 | convolution fusion | flops 5927206912 | bytes 33816576 | tf_op jit(solution)/shard_map/dot_general | solution.py:983
  404.9 9.0 %convolution_convert_fusion.2 = bf16[2048,2816]{1,0:T(8,128)(2,1)} fusion(bf16[512,2048]{1,0:T(8,128)(2,1)S(1)} %copy-done.38, bf16[512,2816]{1,0:T(8,128)(2,1)S(1)} %get-tuple-element.68), kind=kOutput, calls=%fused_computation.2 | convolution fusion | flops 5911347200 | bytes 16515072 | tf_op jit(solution)/shard_map/dot_general | solution.py:983
  414.0 10.9 %fusion.36 = f32[512,2048]{1,0:T(8,128)S(1)} fusion(bf16[512,2816]{1,0:T(8,128)(2,1)} %get-tuple-element.76, bf16[2048,2816]{1,0:T(8,128)(2,1)} %all-gather.8.cloned.1.call-done), kind=kOutput, calls=%fused_computation.120 | convolution fusion | flops 5905580032 | bytes 18612224 | tf_op jit(solution)/shard_map/dot_general | solution.py:983
  425.0 9.9 %convolution_add_fusion = f32[512,2048]{1,0:T(8,128)S(1)} fusion(f32[512,2048]{1,0:T(8,128)S(1)} %fusion.36, bf16[512,2816]{1,0:T(8,128)(2,1)S(1)} %copy-done.41, bf16[2048,2816]{1,0:T(8,128)(2,1)} %all-gather.6.cloned.1.call-done), kind=kOutput, calls=%fused_computation.18 | convolution fusion | flops 5906628608 | bytes 22806528 | tf_op jit(solution)/shard_map/dot_general | solution.py:983
  436.5 9.2 %fusion.37 = f32[512,2048]{1,0:T(8,128)S(1)} fusion(bf16[512,2816]{1,0:T(8,128)(2,1)S(1)} %copy-done.44, bf16[2048,2816]{0,1:T(8,128)(2,1)} %all-gather.4.cloned.1.call-done), kind=kOutput, calls=%fused_computation.121 | convolution fusion | flops 5905580032 | bytes 18612224 | tf_op jit(solution)/shard_map/dot_general | solution.py:983
  446.8 11.7 %collective-permute-done.3 = bf16[256,2048]{1,0:T(8,128)(2,1)S(1)} collective-permute-done((bf16[256,2048]{1,0:T(8,128)(2,1)S(1)}, bf16[256,2048]{1,0:T(8,128)(2,1)S(1)}, u32[]{:S(2)}, u32[]{:S(2)}) %collective-permute-start.3) | collective-permute-done | bytes 1048608 | tf_op jit(solution)/shard_map/ppermute | solution.py:958
  463.1 8.9 %convolution_convert_fusion.1 = bf16[2048,2816]{1,0:T(8,128)(2,1)} fusion(bf16[512,2048]{1,0:T(8,128)(2,1)S(1)} %copy-done.20, bf16[512,2816]{1,0:T(8,128)(2,1)S(1)} %copy-done.42), kind=kOutput, calls=%fused_computation.1 | convolution fusion | flops 5911347200 | bytes 16515072 | tf_op jit(solution)/shard_map/dot_general | solution.py:983
  472.0 11.3 %convolution_convert_fusion = bf16[2048,2816]{1,0:T(8,128)(2,1)} fusion(bf16[512,2048]{1,0:T(8,128)(2,1)} %pad_maximum_fusion, bf16[512,2816]{1,0:T(8,128)(2,1)} %get-tuple-element.77), kind=kOutput, calls=%fused_computation | convolution fusion | flops 5911347200 | bytes 16515072 | tf_op jit(solution)/shard_map/dot_general | solution.py:983
  489.7 8.0 convolution_convert_fusion.3.dg_ref
  497.7 49.3 %mixer_backward.1 = (bf16[512,4736]{1,0:T(8,128)(2,1)}, f32[4,768]{1,0:T(4,128)S(1)}, f32[4,768]{1,0:T(4,128)S(1)}, f32[4,1536]{1,0:T(4,128)S(1)}, f32[8,512]{1,0:T(8,128)S(1)}, /*index=5*/f32[8,128]{1,0:T(8,128)S(1)}) custom-call(s32[1]{0:T(128)S(6)} %copy.115.len_ref, f32[512,4736]{1,0:T(8,128)} %fusion.32.q_ref.k_ref.v_ref.g_ref.bd_ref, ...), custom_call_target="tpu_custom_call" | custom-call | tf_op jit(solution)/shard_map/mixer_backward/pallas_call | solution.py:473
  550.5 19.1 %fusion.4 = (bf16[2048]{0:T(1024)(128)(2,1)S(1)}, f32[512,2048]{1,0:T(8,128)}) fusion(bf16[512,2048]{1,0:T(8,128)(2,1)S(1)} %copy-done.12, f32[512]{0:T(512)S(1)} %copy-done.28, bf16[512,4736]{1,0:T(8,128)(2,1)} %get-tuple-element.83.refs_4_, bf16[2048,4736]{1,0:T(8,128)(2,1)} %get-tuple-element.58), kind=kOutput, calls=%fused_computation.13 | convolution fusion | flops 9936304128 | bytes 30545920 | tf_op jit(solution)/shard_map/dot_general | solution.py:983
  571.1 2.7 dynamic-slice_convert_fusion.refs_6_
  573.8 279.2 %scatter_sum.1 = (f32[128,9088]{1,0:T(8,128)}, bf16[256,2048]{1,0:T(8,128)(2,1)}) custom-call(bf16[8,2,128,2816]{3,2,1,0:T(8,128)(2,1)} %bitcast.89, bf16[8,2,128,128]{3,2,1,0:T(8,128)(2,1)} %bitcast.91, bf16[512,2048]{1,0:T(8,128)(2,1)} %copy-done.9, bf16[512,2048]{1,0:T(8,128)(2,1)} %pad_maximum_fusion.1.refs_3_, ...), custom_call_target="tpu_custom_call" | custom-call | tf_op jit(solution)/shard_map/scatter_sum/pallas_call | solution.py:910
  863.9 3.2 add_convert_fusion
  (235 shorter events, 83.4 us)
Async XLA Ops:
  7.2 340.3 %all-gather.4.cloned.1.call-start = ((), (), s32[]{:S(2)}) async-start(), calls=%async_computation.2 | async-start | bytes 12255232 | tf_op jit(solution)/shard_map/all_gather | solution.py:992
  9.9 364.1 %all-gather.8.cloned.1.call-start = ((), (), s32[]{:S(2)}) async-start(), calls=%async_computation.4 | async-start | bytes 12255232 | tf_op jit(solution)/shard_map/all_gather | solution.py:992
  10.9 376.0 %all-gather.6.cloned.1.call-start = ((), (), s32[]{:S(2)}) async-start(), calls=%async_computation.3 | async-start | bytes 12255232 | tf_op jit(solution)/shard_map/all_gather | solution.py:992
  11.9 867.1 %reduce-scatter.5.cloned.1.call-start = ((), (), s32[]{:S(2)}) async-start(), calls=%async_computation.6 | async-start | bytes 12255232 | tf_op jit(solution)/shard_map/reduce_scatter | solution.py:996
  12.0 9.6 %collective-permute-start = (f32[1,144]{1,0:T(1,128)S(1)}, f32[1,144]{1,0:T(1,128)S(1)}, u32[]{:S(2)}, u32[]{:S(2)}) collective-permute-start(f32[1,144]{1,0:T(1,128)S(1)} %bitcast.101), channel_id=1, source_target_pairs={{0,1},{1,0},{2,3},{3,2},{4,5},{5,4},{6,7},{7,6},{8,9},{9,8},{10,11... | collective-permute-start | bytes 1736 | tf_op jit(solution)/shard_map/ppermute | solution.py:958
  15.9 257.8 %copy-start.2 = (f32[1,128]{1,0:T(1,128)}, f32[1,128]{1,0:T(1,128)S(1)}, u32[]{:S(2)}) copy-start(f32[1,128]{1,0:T(1,128)S(1)} %get-tuple-element.203.bias_ref) | copy-start | bytes 1540
  15.9 257.8 %copy-start.4 = (f32[1,128]{1,0:T(1,128)}, f32[1,128]{1,0:T(1,128)S(1)}, u32[]{:S(2)}) copy-start(f32[1,128]{1,0:T(1,128)S(1)} %get-tuple-element.204.log_ref) | copy-start | bytes 1540
  253.6 20.1 %copy-start.27 = (f32[512]{0:T(512)}, f32[512]{0:T(512)S(1)}, u32[]{:S(2)}) copy-start(f32[512]{0:T(512)S(1)} %add_rsqrt_fusion) | copy-start | bytes 6148
  255.8 17.9 %copy-start.9 = (bf16[512,2048]{1,0:T(8,128)(2,1)}, bf16[512,2048]{1,0:T(8,128)(2,1)S(1)}, u32[]{:S(2)}) copy-start(bf16[512,2048]{1,0:T(8,128)(2,1)S(1)} %fusion.3.refs_2_) | copy-start | bytes 6291460
  308.6 34.2 %copy-start.10 = (bf16[256,2048]{1,0:T(8,128)(2,1)S(1)}, bf16[256,2048]{1,0:T(8,128)(2,1)}, u32[]{:S(2)}) copy-start(bf16[256,2048]{1,0:T(8,128)(2,1)} %refs_2_.1) | copy-start | bytes 3145732
  317.1 25.8 %collective-permute-start.1 = (bf16[256,2048]{1,0:T(8,128)(2,1)}, bf16[256,2048]{1,0:T(8,128)(2,1)}, u32[]{:S(2)}, u32[]{:S(2)}) collective-permute-start(bf16[256,2048]{1,0:T(8,128)(2,1)} %dynamic-slice_convert_fusion.3), channel_id=1, source_target_pairs={{0,1},{1,0},{2,3},{3,2},{4,5},{5,4},{6,7},{7,6},{8,9},{9,8},{10,11... | collective-permute-start | bytes 3145736 | tf_op jit(solution)/shard_map/ppermute | solution.py:958
  347.6 24.7 %collective-permute-start.2 = (bf16[256,2048]{1,0:T(8,128)(2,1)S(1)}, bf16[256,2048]{1,0:T(8,128)(2,1)S(1)}, u32[]{:S(2)}, u32[]{:S(2)}) collective-permute-start(bf16[256,2048]{1,0:T(8,128)(2,1)S(1)} %multiply_convert_fusion.3), channel_id=1, source_target_pairs={{0,1},{1,0},{2,3},{3,2},{4,5},{5,4},{6,7},{7,6},{8,9},{9,8},{10,11... | collective-permute-start | bytes 3145736 | tf_op jit(solution)/shard_map/ppermute | solution.py:958
  386.9 18.0 %copy-start.38 = (bf16[512,2048]{1,0:T(8,128)(2,1)S(1)}, bf16[512,2048]{1,0:T(8,128)(2,1)}, u32[]{:S(2)}) copy-start(bf16[512,2048]{1,0:T(8,128)(2,1)} %get-tuple-element.62) | copy-start | bytes 6291460
  414.0 467.8 %reduce-scatter.3.cloned.1.call-start = ((), (), s32[]{:S(2)}) async-start(), calls=%async_computation.5 | async-start | bytes 12255232 | tf_op jit(solution)/shard_map/reduce_scatter | solution.py:996
  425.0 11.5 %copy-start.44 = (bf16[512,2816]{1,0:T(8,128)(2,1)S(1)}, bf16[512,2816]{1,0:T(8,128)(2,1)}, u32[]{:S(2)}) copy-start(bf16[512,2816]{1,0:T(8,128)(2,1)} %copy-done.43) | copy-start | bytes 8650756
  435.1 23.4 %collective-permute-start.3 = (bf16[256,2048]{1,0:T(8,128)(2,1)S(1)}, bf16[256,2048]{1,0:T(8,128)(2,1)S(1)}, u32[]{:S(2)}, u32[]{:S(2)}) collective-permute-start(bf16[256,2048]{1,0:T(8,128)(2,1)S(1)} %dynamic-slice_convert_fusion.2), channel_id=1, source_target_pairs={{0,1},{1,0},{2,3},{3,2},{4,5},{5,4},{6,7},{7,6},{8,9},{9,8},{10,11... | collective-permute-start | bytes 3145736 | tf_op jit(solution)/shard_map/ppermute | solution.py:958
  445.7 13.7 %copy-start.18 = (f32[512,2048]{1,0:T(8,128)}, f32[512,2048]{1,0:T(8,128)S(1)}, u32[]{:S(2)}) copy-start(f32[512,2048]{1,0:T(8,128)S(1)} %fusion.37) | copy-start | bytes 12582916
  445.7 12.9 %copy-start.7 = (f32[256,2048]{1,0:T(8,128)S(1)}, f32[256,2048]{1,0:T(8,128)}, u32[]{:S(2)}) copy-start(f32[256,2048]{1,0:T(8,128)} %copy-done.6) | copy-start | bytes 6291460
  446.8 12.6 %copy-start.16 = (bf16[256,2048]{1,0:T(8,128)(2,1)S(1)}, bf16[256,2048]{1,0:T(8,128)(2,1)}, u32[]{:S(2)}) copy-start(bf16[256,2048]{1,0:T(8,128)(2,1)} %refs_3_.1) | copy-start | bytes 3145732
  461.6 22.7 %collective-permute-start.4 = (bf16[256,2048]{1,0:T(8,128)(2,1)S(1)}, bf16[256,2048]{1,0:T(8,128)(2,1)}, u32[]{:S(2)}, u32[]{:S(2)}) collective-permute-start(bf16[256,2048]{1,0:T(8,128)(2,1)S(1)} %get-tuple-element.75), channel_id=1, source_target_pairs={{0,1},{1,0},{2,3},{3,2},{4,5},{5,4},{6,7},{7,6},{8,9},{9,8},{10,11... | collective-permute-start | bytes 3145736 | tf_op jit(solution)/shard_map/ppermute | solution.py:958
  487.9 60.5 %collective-permute-start.5 = (bf16[256,2048]{1,0:T(8,128)(2,1)}, bf16[256,2048]{1,0:T(8,128)(2,1)S(1)}, u32[]{:S(2)}, u32[]{:S(2)}) collective-permute-start(bf16[256,2048]{1,0:T(8,128)(2,1)} %dynamic-slice_convert_fusion.1), channel_id=1, source_target_pairs={{0,1},{1,0},{2,3},{3,2},{4,5},{5,4},{6,7},{7,6},{8,9},{9,8},{10,11... | collective-permute-start | bytes 3145736 | tf_op jit(solution)/shard_map/ppermute | solution.py:958
  573.8 282.8 %copy-start.11 = (bf16[256,2048]{1,0:T(8,128)(2,1)S(1)}, bf16[256,2048]{1,0:T(8,128)(2,1)}, u32[]{:S(2)}) copy-start(bf16[256,2048]{1,0:T(8,128)(2,1)} %refs_2_.1) | copy-start | bytes 3145732
  573.8 282.8 %copy-start.26 = (f32[2048]{0:T(1024)S(1)}, f32[2048]{0:T(1024)}, u32[]{:S(2)}) copy-start(f32[2048]{0:T(1024)} %copy-done.25) | copy-start | bytes 24580
  853.9 21.5 %collective-permute-start.6 = (f32[4,128]{0,1:T(8,128)S(1)}, f32[4,128]{0,1:T(8,128)S(1)}, u32[]{:S(2)}, u32[]{:S(2)}) collective-permute-start(f32[4,128]{0,1:T(8,128)S(1)} %slice_bitcast_fusion.2), channel_id=1, source_target_pairs={{0,1},{1,0},{2,3},{3,2},{4,5},{5,4},{6,7},{7,6},{8,9},{9,8},{10,11... | collective-permute-start | bytes 6152 | tf_op jit(solution)/shard_map/ppermute | solution.py:958
  (33 other events, 153.8 us)
Sparse Core Ops, SparseCore 0:
  10.8 160.2 all-gather.3
  173.9 104.8 all-gather.7
  281.7 96.3 all-gather.5
  414.1 124.4 reduce-scatter.4
  543.1 203.0 reduce-scatter.2

commit v6 on v5

--- a/solution.py
+++ b/solution.py
@@ -7,7 +7,7 @@
 from jax.experimental.pallas import tpu as pltpu
 
 CH = 256
-TILE = 64
+TILE = 128
 PADR = 8
 f32 = jnp.float32
 bf16 = jnp.bfloat16

time: 900 us -> 897 us (level)
  no operation moved by 1% of the time
where the time goes in v6:
time: 897 us; the launch traced here: 889 us
  Pallas kernels  580 us (65%)
  matrix products  154 us (17%)
  waiting for transfers between devices  46.8 us (5%)
  local copies, waits for them, and re-layouts  41 us (5%)
  other arithmetic  38.5 us (4%)
  between operations  15.7 us (2%)
  starting transfers between devices  12.7 us (1%)
    pallas_call x1, Pallas kernels, scatter_sum(): pl.pallas_call(functools.partial(scatter_kernel, layers, chunks, len(prod...  283 us
    pallas_call x1, Pallas kernels, gather_all(): pl.pallas_call(functools.partial(gather_kernel, layers, chunks, len(shard...  218 us
    dot_general x14, matrix products, dot(): lax.dot_general(a, b, (((ca,), (cb,)), ((), ())), preferred_element_type=...  154 us
    ppermute x7, waiting for transfers between devices, pair_swap(): return lax.ppermute(values, 'tensor', [(0, 1), (1, 0)])  46.6 us
    pallas_call x1, Pallas kernels, mixer_backward(): pl.pallas_call(functools.partial(bwd_kernel, heads), grid=(heads,), in_sp...  45.6 us
    pallas_call x1, Pallas kernels, mixer_forward(): pl.pallas_call(functools.partial(fwd_kernel, heads), grid=(heads,), in_sp...  32.7 us
  transfers between devices with their start and end apart: 12, of which 4 were waited for; matrix products, arithmetic and copies ran while one was open for 22% of the time, Pallas kernels for 65%

profile of v6, /device:TPU:0, one launch (start us, length us, event | category | flops | bytes accessed | tf_op | source)
XLA Modules:
  0.0 888.6 jit_solution(4818738534976882773)
XLA Ops:
  12.0 2.9 collective-permute-start
  23.4 217.8 %gather_rows.1 = (bf16[2048,4736]{1,0:T(8,128)(2,1)}, bf16[2048,1536]{1,0:T(8,128)(2,1)}, bf16[512,2048]{1,0:T(8,128)(2,1)}, bf16[512,2048]{1,0:T(8,128)(2,1)}) custom-call(bf16[128,4736]{1,0:T(8,128)(2,1)} %copy-done.21, bf16[128,1536]{1,0:T(8,128)(2,1)} %bitcast.94, bf16[256,2048]{1,0:T(8,128)(2,1)} %refs_2_.1, bf16[256,2048]{1,0:T(8,128)(2,1)} %refs_3_.1), custom_call_target="tpu_custom_call" | custom-call | tf_op jit(solution)/shard_map/gather_rows/pallas_call | solution.py:735
  255.8 17.9 %fusion.32.q_ref.k_ref.v_ref.g_ref.bd_ref = f32[512,4736]{1,0:T(8,128)} fusion(bf16[512,2048]{1,0:T(8,128)(2,1)S(1)} %fusion.3.refs_2_, bf16[2048,4736]{1,0:T(8,128)(2,1)} %get-tuple-element.58), kind=kOutput, calls=%fused_computation.116 | convolution fusion | flops 9932111872 | bytes 31195136 | tf_op jit(solution)/shard_map/dot_general | solution.py:983
  273.8 32.7 %mixer_forward.1 = (bf16[512,1536]{1,0:T(8,128)(2,1)S(1)}, bf16[3,512,256]{2,1,0:T(8,128)(2,1)S(1)}, bf16[512,1536]{1,0:T(8,128)(2,1)S(1)}, f32[512,1536]{1,0:T(8,128)}, f32[3,1,256,512]{3,2,1,0:T(8,128)}) custom-call(s32[1]{0:T(128)S(6)} %copy.115.len_ref, f32[512,4736]{1,0:T(8,128)} %fusion.32.q_ref.k_ref.v_ref.g_ref.bd_ref, ...), custom_call_target="tpu_custom_call" | custom-call | tf_op jit(solution)/shard_map/mixer_forward/pallas_call | solution.py:437
  306.5 6.2 fusion.33
  316.7 24.1 %collective-permute-done.1 = bf16[256,2048]{1,0:T(8,128)(2,1)} collective-permute-done((bf16[256,2048]{1,0:T(8,128)(2,1)}, bf16[256,2048]{1,0:T(8,128)(2,1)}, u32[]{:S(2)}, u32[]{:S(2)}) %collective-permute-start.1) | collective-permute-done | bytes 1048608 | tf_op jit(solution)/shard_map/ppermute | solution.py:958
  340.7 3.1 multiply_reduce_fusion.2
  347.2 12.9 %fusion.34 = f32[512,2816]{1,0:T(8,128)} fusion(bf16[512,2048]{1,0:T(8,128)(2,1)} %get-tuple-element.62, bf16[2048,2816]{0,1:T(8,128)(2,1)} %all-gather.4.cloned.1.call-done), kind=kOutput, calls=%fused_computation.118 | convolution fusion | flops 5905580032 | bytes 19398656 | tf_op jit(solution)/shard_map/dot_general | solution.py:983
  360.1 10.1 %collective-permute-done.2 = bf16[256,2048]{1,0:T(8,128)(2,1)S(1)} collective-permute-done((bf16[256,2048]{1,0:T(8,128)(2,1)S(1)}, bf16[256,2048]{1,0:T(8,128)(2,1)S(1)}, u32[]{:S(2)}, u32[]{:S(2)}) %collective-permute-start.2) | collective-permute-done | bytes 1048608 | tf_op jit(solution)/shard_map/ppermute | solution.py:958
  371.9 12.7 %fusion.35 = f32[512,2816]{1,0:T(8,128)} fusion(bf16[512,2048]{1,0:T(8,128)(2,1)} %pad_maximum_fusion, bf16[2048,2816]{1,0:T(8,128)(2,1)} %all-gather.8.cloned.1.call-done), kind=kOutput, calls=%fused_computation.119 | convolution fusion | flops 5905580032 | bytes 19398656 | tf_op jit(solution)/shard_map/dot_general | solution.py:983
  384.6 16.4 %multiply_convert_fusion = (bf16[512,2816]{1,0:T(8,128)(2,1)S(1)}, bf16[512,2816]{1,0:T(8,128)(2,1)}, bf16[512,2816]{1,0:T(8,128)(2,1)}) fusion(f32[512,2816]{1,0:T(8,128)} %fusion.35, f32[512,2816]{1,0:T(8,128)} %fusion.34, bf16[512,2048]{1,0:T(8,128)(2,1)} %pad_maximum_fusion, bf16[2048,2816]{1,0:T(8,128)(2,1)} %all-gather.6.cloned.1.call-done), kind=kOutput, calls=%fused_computation.3 | convolution fusion | flops 5927206912 | bytes 33816576 | tf_op jit(solution)/shard_map/dot_general | solution.py:983
  402.6 9.0 %convolution_convert_fusion.2 = bf16[2048,2816]{1,0:T(8,128)(2,1)} fusion(bf16[512,2048]{1,0:T(8,128)(2,1)S(1)} %copy-done.38, bf16[512,2816]{1,0:T(8,128)(2,1)S(1)} %get-tuple-element.68), kind=kOutput, calls=%fused_computation.2 | convolution fusion | flops 5911347200 | bytes 16515072 | tf_op jit(solution)/shard_map/dot_general | solution.py:983
  411.7 10.9 %fusion.36 = f32[512,2048]{1,0:T(8,128)S(1)} fusion(bf16[512,2816]{1,0:T(8,128)(2,1)} %get-tuple-element.76, bf16[2048,2816]{1,0:T(8,128)(2,1)} %all-gather.8.cloned.1.call-done), kind=kOutput, calls=%fused_computation.120 | convolution fusion | flops 5905580032 | bytes 18612224 | tf_op jit(solution)/shard_map/dot_general | solution.py:983
  422.7 9.9 %convolution_add_fusion = f32[512,2048]{1,0:T(8,128)S(1)} fusion(f32[512,2048]{1,0:T(8,128)S(1)} %fusion.36, bf16[512,2816]{1,0:T(8,128)(2,1)S(1)} %copy-done.41, bf16[2048,2816]{1,0:T(8,128)(2,1)} %all-gather.6.cloned.1.call-done), kind=kOutput, calls=%fused_computation.18 | convolution fusion | flops 5906628608 | bytes 22806528 | tf_op jit(solution)/shard_map/dot_general | solution.py:983
  434.3 9.2 %fusion.37 = f32[512,2048]{1,0:T(8,128)S(1)} fusion(bf16[512,2816]{1,0:T(8,128)(2,1)S(1)} %copy-done.44, bf16[2048,2816]{0,1:T(8,128)(2,1)} %all-gather.4.cloned.1.call-done), kind=kOutput, calls=%fused_computation.121 | convolution fusion | flops 5905580032 | bytes 18612224 | tf_op jit(solution)/shard_map/dot_general | solution.py:983
  444.6 11.7 %collective-permute-done.3 = bf16[256,2048]{1,0:T(8,128)(2,1)S(1)} collective-permute-done((bf16[256,2048]{1,0:T(8,128)(2,1)S(1)}, bf16[256,2048]{1,0:T(8,128)(2,1)S(1)}, u32[]{:S(2)}, u32[]{:S(2)}) %collective-permute-start.3) | collective-permute-done | bytes 1048608 | tf_op jit(solution)/shard_map/ppermute | solution.py:958
  460.8 8.9 %convolution_convert_fusion.1 = bf16[2048,2816]{1,0:T(8,128)(2,1)} fusion(bf16[512,2048]{1,0:T(8,128)(2,1)S(1)} %copy-done.20, bf16[512,2816]{1,0:T(8,128)(2,1)S(1)} %copy-done.42), kind=kOutput, calls=%fused_computation.1 | convolution fusion | flops 5911347200 | bytes 16515072 | tf_op jit(solution)/shard_map/dot_general | solution.py:983
  469.8 11.3 %convolution_convert_fusion = bf16[2048,2816]{1,0:T(8,128)(2,1)} fusion(bf16[512,2048]{1,0:T(8,128)(2,1)} %pad_maximum_fusion, bf16[512,2816]{1,0:T(8,128)(2,1)} %get-tuple-element.77), kind=kOutput, calls=%fused_computation | convolution fusion | flops 5911347200 | bytes 16515072 | tf_op jit(solution)/shard_map/dot_general | solution.py:983
  487.4 8.0 convolution_convert_fusion.3.dg_ref
  495.4 45.6 %mixer_backward.1 = (bf16[512,4736]{1,0:T(8,128)(2,1)}, f32[4,768]{1,0:T(4,128)S(1)}, f32[4,768]{1,0:T(4,128)S(1)}, f32[4,1536]{1,0:T(4,128)S(1)}, f32[8,512]{1,0:T(8,128)S(1)}, /*index=5*/f32[8,128]{1,0:T(8,128)S(1)}) custom-call(s32[1]{0:T(128)S(6)} %copy.115.len_ref, f32[512,4736]{1,0:T(8,128)} %fusion.32.q_ref.k_ref.v_ref.g_ref.bd_ref, ...), custom_call_target="tpu_custom_call" | custom-call | tf_op jit(solution)/shard_map/mixer_backward/pallas_call | solution.py:473
  544.3 18.7 %fusion.4 = (bf16[2048]{0:T(1024)(128)(2,1)S(1)}, f32[512,2048]{1,0:T(8,128)}) fusion(bf16[512,2048]{1,0:T(8,128)(2,1)S(1)} %copy-done.12, f32[512]{0:T(512)S(1)} %copy-done.28, bf16[512,4736]{1,0:T(8,128)(2,1)} %get-tuple-element.83.refs_4_, bf16[2048,4736]{1,0:T(8,128)(2,1)} %get-tuple-element.58), kind=kOutput, calls=%fused_computation.13 | convolution fusion | flops 9936304128 | bytes 30545920 | tf_op jit(solution)/shard_map/dot_general | solution.py:983
  564.4 2.8 dynamic-slice_convert_fusion.refs_6_
  567.2 283.4 %scatter_sum.1 = (f32[128,9088]{1,0:T(8,128)}, bf16[256,2048]{1,0:T(8,128)(2,1)}) custom-call(bf16[8,2,128,2816]{3,2,1,0:T(8,128)(2,1)} %bitcast.89, bf16[8,2,128,128]{3,2,1,0:T(8,128)(2,1)} %bitcast.91, bf16[512,2048]{1,0:T(8,128)(2,1)} %copy-done.9, bf16[512,2048]{1,0:T(8,128)(2,1)} %pad_maximum_fusion.1.refs_3_, ...), custom_call_target="tpu_custom_call" | custom-call | tf_op jit(solution)/shard_map/scatter_sum/pallas_call | solution.py:910
  861.5 3.2 add_convert_fusion
  (235 shorter events, 83.1 us)
Async XLA Ops:
  7.2 338.3 %all-gather.4.cloned.1.call-start = ((), (), s32[]{:S(2)}) async-start(), calls=%async_computation.2 | async-start | bytes 12255232 | tf_op jit(solution)/shard_map/all_gather | solution.py:992
  9.9 362.0 %all-gather.8.cloned.1.call-start = ((), (), s32[]{:S(2)}) async-start(), calls=%async_computation.4 | async-start | bytes 12255232 | tf_op jit(solution)/shard_map/all_gather | solution.py:992
  10.9 373.7 %all-gather.6.cloned.1.call-start = ((), (), s32[]{:S(2)}) async-start(), calls=%async_computation.3 | async-start | bytes 12255232 | tf_op jit(solution)/shard_map/all_gather | solution.py:992
  11.9 864.7 %reduce-scatter.5.cloned.1.call-start = ((), (), s32[]{:S(2)}) async-start(), calls=%async_computation.6 | async-start | bytes 12255232 | tf_op jit(solution)/shard_map/reduce_scatter | solution.py:996
  12.0 9.6 %collective-permute-start = (f32[1,144]{1,0:T(1,128)S(1)}, f32[1,144]{1,0:T(1,128)S(1)}, u32[]{:S(2)}, u32[]{:S(2)}) collective-permute-start(f32[1,144]{1,0:T(1,128)S(1)} %bitcast.101), channel_id=1, source_target_pairs={{0,1},{1,0},{2,3},{3,2},{4,5},{5,4},{6,7},{7,6},{8,9},{9,8},{10,11... | collective-permute-start | bytes 1736 | tf_op jit(solution)/shard_map/ppermute | solution.py:958
  15.9 257.8 %copy-start.2 = (f32[1,128]{1,0:T(1,128)}, f32[1,128]{1,0:T(1,128)S(1)}, u32[]{:S(2)}) copy-start(f32[1,128]{1,0:T(1,128)S(1)} %get-tuple-element.203.bias_ref) | copy-start | bytes 1540
  15.9 257.8 %copy-start.4 = (f32[1,128]{1,0:T(1,128)}, f32[1,128]{1,0:T(1,128)S(1)}, u32[]{:S(2)}) copy-start(f32[1,128]{1,0:T(1,128)S(1)} %get-tuple-element.204.log_ref) | copy-start | bytes 1540
  253.6 20.1 %copy-start.27 = (f32[512]{0:T(512)}, f32[512]{0:T(512)S(1)}, u32[]{:S(2)}) copy-start(f32[512]{0:T(512)S(1)} %add_rsqrt_fusion) | copy-start | bytes 6148
  255.8 17.9 %copy-start.9 = (bf16[512,2048]{1,0:T(8,128)(2,1)}, bf16[512,2048]{1,0:T(8,128)(2,1)S(1)}, u32[]{:S(2)}) copy-start(bf16[512,2048]{1,0:T(8,128)(2,1)S(1)} %fusion.3.refs_2_) | copy-start | bytes 6291460
  306.5 34.3 %copy-start.10 = (bf16[256,2048]{1,0:T(8,128)(2,1)S(1)}, bf16[256,2048]{1,0:T(8,128)(2,1)}, u32[]{:S(2)}) copy-start(bf16[256,2048]{1,0:T(8,128)(2,1)} %refs_2_.1) | copy-start | bytes 3145732
  315.0 25.8 %collective-permute-start.1 = (bf16[256,2048]{1,0:T(8,128)(2,1)}, bf16[256,2048]{1,0:T(8,128)(2,1)}, u32[]{:S(2)}, u32[]{:S(2)}) collective-permute-start(bf16[256,2048]{1,0:T(8,128)(2,1)} %dynamic-slice_convert_fusion.3), channel_id=1, source_target_pairs={{0,1},{1,0},{2,3},{3,2},{4,5},{5,4},{6,7},{7,6},{8,9},{9,8},{10,11... | collective-permute-start | bytes 3145736 | tf_op jit(solution)/shard_map/ppermute | solution.py:958
  345.5 24.7 %collective-permute-start.2 = (bf16[256,2048]{1,0:T(8,128)(2,1)S(1)}, bf16[256,2048]{1,0:T(8,128)(2,1)S(1)}, u32[]{:S(2)}, u32[]{:S(2)}) collective-permute-start(bf16[256,2048]{1,0:T(8,128)(2,1)S(1)} %multiply_convert_fusion.3), channel_id=1, source_target_pairs={{0,1},{1,0},{2,3},{3,2},{4,5},{5,4},{6,7},{7,6},{8,9},{9,8},{10,11... | collective-permute-start | bytes 3145736 | tf_op jit(solution)/shard_map/ppermute | solution.py:958
  384.6 18.0 %copy-start.38 = (bf16[512,2048]{1,0:T(8,128)(2,1)S(1)}, bf16[512,2048]{1,0:T(8,128)(2,1)}, u32[]{:S(2)}) copy-start(bf16[512,2048]{1,0:T(8,128)(2,1)} %get-tuple-element.62) | copy-start | bytes 6291460
  411.7 467.6 %reduce-scatter.3.cloned.1.call-start = ((), (), s32[]{:S(2)}) async-start(), calls=%async_computation.5 | async-start | bytes 12255232 | tf_op jit(solution)/shard_map/reduce_scatter | solution.py:996
  422.7 11.6 %copy-start.44 = (bf16[512,2816]{1,0:T(8,128)(2,1)S(1)}, bf16[512,2816]{1,0:T(8,128)(2,1)}, u32[]{:S(2)}) copy-start(bf16[512,2816]{1,0:T(8,128)(2,1)} %copy-done.43) | copy-start | bytes 8650756
  432.8 23.4 %collective-permute-start.3 = (bf16[256,2048]{1,0:T(8,128)(2,1)S(1)}, bf16[256,2048]{1,0:T(8,128)(2,1)S(1)}, u32[]{:S(2)}, u32[]{:S(2)}) collective-permute-start(bf16[256,2048]{1,0:T(8,128)(2,1)S(1)} %dynamic-slice_convert_fusion.2), channel_id=1, source_target_pairs={{0,1},{1,0},{2,3},{3,2},{4,5},{5,4},{6,7},{7,6},{8,9},{9,8},{10,11... | collective-permute-start | bytes 3145736 | tf_op jit(solution)/shard_map/ppermute | solution.py:958
  443.5 13.6 %copy-start.18 = (f32[512,2048]{1,0:T(8,128)}, f32[512,2048]{1,0:T(8,128)S(1)}, u32[]{:S(2)}) copy-start(f32[512,2048]{1,0:T(8,128)S(1)} %fusion.37) | copy-start | bytes 12582916
  443.5 12.8 %copy-start.7 = (f32[256,2048]{1,0:T(8,128)S(1)}, f32[256,2048]{1,0:T(8,128)}, u32[]{:S(2)}) copy-start(f32[256,2048]{1,0:T(8,128)} %copy-done.6) | copy-start | bytes 6291460
  444.6 12.5 %copy-start.16 = (bf16[256,2048]{1,0:T(8,128)(2,1)S(1)}, bf16[256,2048]{1,0:T(8,128)(2,1)}, u32[]{:S(2)}) copy-start(bf16[256,2048]{1,0:T(8,128)(2,1)} %refs_3_.1) | copy-start | bytes 3145732
  459.3 22.7 %collective-permute-start.4 = (bf16[256,2048]{1,0:T(8,128)(2,1)S(1)}, bf16[256,2048]{1,0:T(8,128)(2,1)}, u32[]{:S(2)}, u32[]{:S(2)}) collective-permute-start(bf16[256,2048]{1,0:T(8,128)(2,1)S(1)} %get-tuple-element.75), channel_id=1, source_target_pairs={{0,1},{1,0},{2,3},{3,2},{4,5},{5,4},{6,7},{7,6},{8,9},{9,8},{10,11... | collective-permute-start | bytes 3145736 | tf_op jit(solution)/shard_map/ppermute | solution.py:958
  485.6 56.5 %collective-permute-start.5 = (bf16[256,2048]{1,0:T(8,128)(2,1)}, bf16[256,2048]{1,0:T(8,128)(2,1)S(1)}, u32[]{:S(2)}, u32[]{:S(2)}) collective-permute-start(bf16[256,2048]{1,0:T(8,128)(2,1)} %dynamic-slice_convert_fusion.1), channel_id=1, source_target_pairs={{0,1},{1,0},{2,3},{3,2},{4,5},{5,4},{6,7},{7,6},{8,9},{9,8},{10,11... | collective-permute-start | bytes 3145736 | tf_op jit(solution)/shard_map/ppermute | solution.py:958
  567.2 286.9 %copy-start.11 = (bf16[256,2048]{1,0:T(8,128)(2,1)S(1)}, bf16[256,2048]{1,0:T(8,128)(2,1)}, u32[]{:S(2)}) copy-start(bf16[256,2048]{1,0:T(8,128)(2,1)} %refs_2_.1) | copy-start | bytes 3145732
  567.2 286.9 %copy-start.26 = (f32[2048]{0:T(1024)S(1)}, f32[2048]{0:T(1024)}, u32[]{:S(2)}) copy-start(f32[2048]{0:T(1024)} %copy-done.25) | copy-start | bytes 24580
  851.6 21.3 %collective-permute-start.6 = (f32[4,128]{0,1:T(8,128)S(1)}, f32[4,128]{0,1:T(8,128)S(1)}, u32[]{:S(2)}, u32[]{:S(2)}) collective-permute-start(f32[4,128]{0,1:T(8,128)S(1)} %slice_bitcast_fusion.2), channel_id=1, source_target_pairs={{0,1},{1,0},{2,3},{3,2},{4,5},{5,4},{6,7},{7,6},{8,9},{9,8},{10,11... | collective-permute-start | bytes 6152 | tf_op jit(solution)/shard_map/ppermute | solution.py:958
  (33 other events, 153.2 us)
Sparse Core Ops, SparseCore 0:
  10.8 160.2 all-gather.3
  173.9 104.8 all-gather.7
  281.7 96.3 all-gather.5
  411.8 124.3 reduce-scatter.4
  540.7 213.9 reduce-scatter.2
